TPU v7x, 32 devices: a whole 2x2x4 slice. The times are simulated.
32 devices in a mesh: dp: 8 (over y, x, core), mp: 4 (over z).
Axes of the slice: x: 2, y: 2, z: 4, core: 2. Of those that a mesh axis runs over, the one named last changes fastest.
Arguments:
- inputs: bfloat16 [96, 128, 768], P(('dp', 'mp')), may hold values from -6 to 6
- slot_valid: int32 [96, 128], P('dp'), may hold values from 0 to 1, as said below
- ln1_gain: float32 [2, 768], replicated, may hold values from 0.5 to 1.5
- ln1_bias: float32 [2, 768], replicated, may hold values from -2 to 2
- w_query: bfloat16 [2, 768, 768], replicated, may hold values from -0.21875 to 0.21875
- w_key: bfloat16 [2, 768, 768], replicated, may hold values from -0.21875 to 0.21875
- w_value: bfloat16 [2, 768, 768], replicated, may hold values from -0.21875 to 0.21875
- w_out: bfloat16 [2, 768, 768], replicated, may hold values from -0.875 to 0.875
- gate_logit: float32 [768], replicated, may hold values from -4 to 4
- ln2_gain: float32 [2, 768], replicated, may hold values from 0.5 to 1.5
- ln2_bias: float32 [2, 768], replicated, may hold values from -2 to 2
- w_up: bfloat16 [2, 768, 3072], P(None, None, 'mp'), may hold values from -0.21875 to 0.21875
- b_up: float32 [2, 3072], P(None, 'mp'), may hold values from -3 to 3
- w_down: bfloat16 [2, 3072, 768], P(None, 'mp'), may hold values from -0.109375 to 0.109375
- b_down: float32 [2, 768], replicated, may hold values from -2 to 2
- cotangent: bfloat16 [96, 128, 768], P(('dp', 'mp')), may hold values from -6 to 6
Outputs:
- outputs: bfloat16 [96, 128, 768], P(('dp', 'mp'))
- grad_inputs: float32 [96, 128, 768], P(('dp', 'mp'))
- grad_ln1_gain: float32 [2, 768], P(None, 'dp')
- grad_ln1_bias: float32 [2, 768], P(None, 'dp')
- grad_w_query: float32 [2, 768, 768], P(None, 'dp', 'mp')
- grad_w_key: float32 [2, 768, 768], P(None, 'dp', 'mp')
- grad_w_value: float32 [2, 768, 768], P(None, 'dp', 'mp')
- grad_w_out: float32 [2, 768, 768], P(None, 'dp', 'mp')
- grad_gate: float32 [768], P('dp')
- grad_ln2_gain: float32 [2, 768], P(None, 'dp')
- grad_ln2_bias: float32 [2, 768], P(None, 'dp')
- grad_w_up: float32 [2, 768, 3072], P(None, 'dp', 'mp')
- grad_b_up: float32 [2, 3072], P(None, 'mp')
- grad_w_down: float32 [2, 3072, 768], P(None, 'mp', 'dp')
- grad_b_down: float32 [2, 768], P(None, 'dp')
Inputs may be any that keep to these rules, and one draw needn't show every extreme that they name: `slot_valid`: on every page slots 0 to 112 (the text blocks and the first visual slot) are 1.
All inputs are finite; a program needn't handle non-finite values.
Results may differ from a plain program's by a relative error of at most 0.02.
Values may be sent and summed in bfloat16 or wider, within the bound.
No kernel may reach another device: no remote copies, remote signals or barrier semaphores. Data moves between devices by JAX's collectives and lax.ppermute only.
A program may use at most 192 MiB of HBM per device.

v0:
```python
import math

import jax
import jax.numpy as jnp
from jax import lax
from jax.sharding import PartitionSpec as P

HEADS = 12
TEXT = 112


def normalize(resid, gain, shift):
    center = jnp.mean(resid, axis=-1, keepdims=True)
    centered = resid - center
    spread = jnp.mean(centered * centered, axis=-1, keepdims=True)
    return centered * lax.rsqrt(spread + 1e-05) * gain + shift


def exact_gelu(values):
    return jax.nn.gelu(values, approximate=False)


def gated(logit, values):
    return jax.nn.sigmoid(logit) * values


def allowed_keys(slot_valid, crossed):
    slot_count = slot_valid.shape[1]
    key_live = (slot_valid == 1)[:, None, None, :]
    if crossed:
        query_text = lax.broadcasted_iota(jnp.int32, (slot_count, slot_count), 0) < TEXT
        key_text = lax.broadcasted_iota(jnp.int32, (slot_count, slot_count), 1) < TEXT
        return jnp.logical_and(key_live, (query_text != key_text)[None, None])
    return key_live


def masked_scores(queries, key_rows, allowed):
    scale = 1.0 / math.sqrt(queries.shape[-1])
    raw = (
        jnp.einsum("pshe,pthe->phst", queries, key_rows, preferred_element_type=jnp.float32) * scale
    )
    return jnp.where(allowed, raw, -1e30)


def forward_layer(resid, slot_valid, weights, layer_index, crossed):
    (
        ln1_gain,
        ln1_bias,
        w_query,
        w_key,
        w_value,
        w_out,
        gate_logit,
        ln2_gain,
        ln2_bias,
        w_up,
        b_up,
        w_down,
        b_down,
    ) = weights
    local_pages, slot_count, model_width = resid.shape
    head_count = HEADS
    head_width = model_width // head_count
    normed = normalize(resid, ln1_gain[layer_index], ln1_bias[layer_index]).astype(jnp.bfloat16)
    gathered = lax.all_gather(normed, "mp", axis=0, tiled=True)
    page_start = lax.axis_index("mp") * local_pages
    page_count = gathered.shape[0]
    row_matrix = gathered.reshape(page_count * slot_count, model_width)

    def project(weight):
        made = jnp.dot(row_matrix, weight, preferred_element_type=jnp.float32).astype(jnp.bfloat16)
        return made.reshape(page_count, slot_count, head_count, head_width)

    queries = project(w_query[layer_index])
    key_rows = project(w_key[layer_index])
    value_rows = project(w_value[layer_index])
    allowed = allowed_keys(slot_valid, crossed)
    masked = masked_scores(queries, key_rows, allowed)
    top_score = jnp.max(masked, axis=-1, keepdims=True)
    log_total = top_score + jnp.log(jnp.sum(jnp.exp(masked - top_score), axis=-1, keepdims=True))
    probs_low = jnp.exp(masked - log_total).astype(jnp.bfloat16)
    context = jnp.einsum(
        "phst,pthe->pshe", probs_low, value_rows, preferred_element_type=jnp.float32
    )
    context = context.astype(jnp.bfloat16).reshape(page_count, slot_count, model_width)
    own_context = lax.dynamic_slice_in_dim(context, page_start, local_pages, 0)
    branch = jnp.dot(
        own_context.reshape(-1, model_width), w_out[layer_index], preferred_element_type=jnp.float32
    ).reshape(local_pages, slot_count, model_width)
    if crossed:
        mixed = resid + gated(gate_logit, branch)
    else:
        mixed = resid + branch
    normed_two = normalize(mixed, ln2_gain[layer_index], ln2_bias[layer_index]).astype(jnp.bfloat16)
    gathered_two = lax.all_gather(normed_two, "mp", axis=0, tiled=True)
    upper = (
        jnp.einsum(
            "psd,df->psf", gathered_two, w_up[layer_index], preferred_element_type=jnp.float32
        )
        + b_up[layer_index]
    )
    active = exact_gelu(upper).astype(jnp.bfloat16)
    down_terms = jnp.einsum(
        "psf,fd->psd", active, w_down[layer_index], preferred_element_type=jnp.float32
    )
    result = (
        mixed
        + lax.psum_scatter(
            down_terms.astype(jnp.bfloat16), "mp", scatter_dimension=0, tiled=True
        ).astype(jnp.float32)
        + b_down[layer_index]
    )
    kept = (
        resid,
        normed,
        gathered,
        queries,
        key_rows,
        value_rows,
        log_total,
        probs_low,
        own_context,
        branch,
        mixed,
        gathered_two,
        upper,
        active,
    )
    return (result, kept)


def backward_layer(grad_out, kept, slot_valid, weights, layer_index, crossed):
    (
        ln1_gain,
        ln1_bias,
        w_query,
        w_key,
        w_value,
        w_out,
        gate_logit,
        ln2_gain,
        ln2_bias,
        w_up,
        b_up,
        w_down,
        b_down,
    ) = weights
    (
        resid,
        normed,
        gathered,
        queries,
        key_rows,
        value_rows,
        log_total,
        probs_low,
        own_context,
        branch,
        mixed,
        gathered_two,
        upper,
        active,
    ) = kept
    local_pages, slot_count, model_width = resid.shape
    page_count = gathered.shape[0]
    scale = 1.0 / math.sqrt(queries.shape[-1])
    grad_b_down = jnp.sum(grad_out, axis=(0, 1))
    grad_low = grad_out.astype(jnp.bfloat16)
    grad_all = lax.all_gather(grad_low, "mp", axis=0, tiled=True)
    grad_active = jnp.einsum(
        "psd,fd->psf", grad_all, w_down[layer_index], preferred_element_type=jnp.float32
    )
    unused_gelu, gelu_back = jax.vjp(exact_gelu, upper)
    grad_upper = gelu_back(grad_active)[0]
    grad_b_up = jnp.sum(grad_upper, axis=(0, 1))
    upper_low = grad_upper.astype(jnp.bfloat16)
    grad_w_down = jnp.einsum("psf,psd->fd", active, grad_all, preferred_element_type=jnp.float32)
    grad_w_up = jnp.einsum(
        "psd,psf->df", gathered_two, upper_low, preferred_element_type=jnp.float32
    )
    normed_terms = jnp.einsum(
        "psf,df->psd", upper_low, w_up[layer_index], preferred_element_type=jnp.float32
    )
    grad_normed_two = lax.psum_scatter(
        normed_terms.astype(jnp.bfloat16), "mp", scatter_dimension=0, tiled=True
    ).astype(jnp.float32)
    unused_norm, norm_back = jax.vjp(normalize, mixed, ln2_gain[layer_index], ln2_bias[layer_index])
    grad_from_norm, grad_ln2_gain, grad_ln2_bias = norm_back(grad_normed_two)
    grad_mixed = grad_out + grad_from_norm
    if crossed:
        unused_gate, gate_back = jax.vjp(gated, gate_logit, branch)
        grad_gate, grad_branch = gate_back(grad_mixed)
    else:
        grad_gate = jnp.zeros((model_width,), jnp.float32)
        grad_branch = grad_mixed
    branch_low = grad_branch.astype(jnp.bfloat16)
    grad_w_out = jnp.einsum(
        "psd,pse->de", own_context, branch_low, preferred_element_type=jnp.float32
    )
    branch_all = lax.all_gather(branch_low, "mp", axis=0, tiled=True)
    page_start = lax.axis_index("mp") * local_pages
    grad_context = jnp.einsum(
        "pse,de->psd", branch_all, w_out[layer_index], preferred_element_type=jnp.float32
    )
    grad_context = grad_context.astype(jnp.bfloat16).reshape(queries.shape)
    allowed = allowed_keys(slot_valid, crossed)
    probs = jnp.exp(masked_scores(queries, key_rows, allowed) - log_total)
    grad_probs = jnp.einsum(
        "pshe,pthe->phst", grad_context, value_rows, preferred_element_type=jnp.float32
    )
    row_delta = jnp.sum(probs * grad_probs, axis=-1, keepdims=True)
    grad_scores = (probs * (grad_probs - row_delta)).astype(jnp.bfloat16)
    full_shape = (page_count, slot_count, model_width)
    grad_queries = (
        (
            jnp.einsum("phst,pthe->pshe", grad_scores, key_rows, preferred_element_type=jnp.float32)
            * scale
        )
        .astype(jnp.bfloat16)
        .reshape(full_shape)
    )
    grad_keys = (
        (
            jnp.einsum("phst,pshe->pthe", grad_scores, queries, preferred_element_type=jnp.float32)
            * scale
        )
        .astype(jnp.bfloat16)
        .reshape(full_shape)
    )
    grad_values = (
        jnp.einsum("phst,pshe->pthe", probs_low, grad_context, preferred_element_type=jnp.float32)
        .astype(jnp.bfloat16)
        .reshape(full_shape)
    )
    own_queries = lax.dynamic_slice_in_dim(grad_queries, page_start, local_pages, 0)
    own_keys = lax.dynamic_slice_in_dim(grad_keys, page_start, local_pages, 0)
    own_values = lax.dynamic_slice_in_dim(grad_values, page_start, local_pages, 0)
    grad_w_query = jnp.einsum(
        "psd,pse->de", gathered, grad_queries, preferred_element_type=jnp.float32
    )
    grad_w_key = jnp.einsum("psd,pse->de", gathered, grad_keys, preferred_element_type=jnp.float32)
    grad_w_value = jnp.einsum(
        "psd,pse->de", gathered, grad_values, preferred_element_type=jnp.float32
    )
    grad_normed = jnp.einsum(
        "pse,de->psd", own_queries, w_query[layer_index], preferred_element_type=jnp.float32
    )
    grad_normed = grad_normed + jnp.einsum(
        "pse,de->psd", own_keys, w_key[layer_index], preferred_element_type=jnp.float32
    )
    grad_normed = grad_normed + jnp.einsum(
        "pse,de->psd", own_values, w_value[layer_index], preferred_element_type=jnp.float32
    )
    unused_first, first_back = jax.vjp(
        normalize, resid, ln1_gain[layer_index], ln1_bias[layer_index]
    )
    grad_from_first, grad_ln1_gain, grad_ln1_bias = first_back(grad_normed)
    grad_resid = grad_mixed + grad_from_first
    grads = (
        grad_ln1_gain,
        grad_ln1_bias,
        grad_w_query,
        grad_w_key,
        grad_w_value,
        grad_w_out,
        grad_gate,
        grad_ln2_gain,
        grad_ln2_bias,
        grad_w_up,
        grad_b_up,
        grad_w_down,
        grad_b_down,
    )
    return (grad_resid, grads)


def shards(
    inputs,
    slot_valid,
    ln1_gain,
    ln1_bias,
    w_query,
    w_key,
    w_value,
    w_out,
    gate_logit,
    ln2_gain,
    ln2_bias,
    w_up,
    b_up,
    w_down,
    b_down,
    cotangent,
):
    weights = (
        ln1_gain,
        ln1_bias,
        w_query,
        w_key,
        w_value,
        w_out,
        gate_logit,
        ln2_gain,
        ln2_bias,
        w_up,
        b_up,
        w_down,
        b_down,
    )
    first_out, first_kept = forward_layer(inputs.astype(jnp.float32), slot_valid, weights, 0, True)
    second_out, second_kept = forward_layer(first_out, slot_valid, weights, 1, False)
    grad_middle, second_grads = backward_layer(
        cotangent.astype(jnp.float32), second_kept, slot_valid, weights, 1, False
    )
    grad_inputs, first_grads = backward_layer(grad_middle, first_kept, slot_valid, weights, 0, True)
    stacked = [
        jnp.stack([first_part, second_part])
        for first_part, second_part in zip(first_grads, second_grads)
    ]
    model_width = inputs.shape[2]
    col_share = model_width // lax.axis_size("mp")
    col_offset = lax.axis_index("mp") * col_share
    wide_query, wide_key, wide_value = (
        lax.psum_scatter(stacked[2], "dp", scatter_dimension=1, tiled=True),
        lax.psum_scatter(stacked[3], "dp", scatter_dimension=1, tiled=True),
        lax.psum_scatter(stacked[4], "dp", scatter_dimension=1, tiled=True),
    )
    grad_wq = lax.dynamic_slice_in_dim(wide_query, col_offset, col_share, 2)
    grad_wk = lax.dynamic_slice_in_dim(wide_key, col_offset, col_share, 2)
    grad_wv = lax.dynamic_slice_in_dim(wide_value, col_offset, col_share, 2)
    rows_out, part_g1, part_b1, part_g2, part_b2, part_bdown, part_gate = (
        lax.psum_scatter(stacked[5], "dp", scatter_dimension=1, tiled=True),
        lax.psum_scatter(stacked[0], "dp", scatter_dimension=1, tiled=True),
        lax.psum_scatter(stacked[1], "dp", scatter_dimension=1, tiled=True),
        lax.psum_scatter(stacked[7], "dp", scatter_dimension=1, tiled=True),
        lax.psum_scatter(stacked[8], "dp", scatter_dimension=1, tiled=True),
        lax.psum_scatter(stacked[12], "dp", scatter_dimension=1, tiled=True),
        lax.psum_scatter(first_grads[6], "dp", scatter_dimension=0, tiled=True),
    )
    grad_wo = lax.psum_scatter(
        rows_out.astype(jnp.bfloat16), "mp", scatter_dimension=2, tiled=True
    ).astype(jnp.float32)
    grad_g1, grad_b1, grad_g2, grad_b2, grad_bdown, grad_gate = lax.psum(
        (part_g1, part_b1, part_g2, part_b2, part_bdown, part_gate), "mp"
    )
    grad_wup, grad_wdown = (
        lax.psum_scatter(stacked[9], "dp", scatter_dimension=1, tiled=True),
        lax.psum_scatter(stacked[11], "dp", scatter_dimension=2, tiled=True),
    )
    grad_bup = lax.psum(stacked[10], "dp")
    return (
        second_out.astype(jnp.bfloat16),
        grad_inputs,
        grad_g1,
        grad_b1,
        grad_wq,
        grad_wk,
        grad_wv,
        grad_wo,
        grad_gate,
        grad_g2,
        grad_b2,
        grad_wup,
        grad_bup,
        grad_wdown,
        grad_bdown,
    )


def solution(mesh):
    placed = (
        P(("dp", "mp"), None, None),
        P("dp", None),
        P(),
        P(),
        P(),
        P(),
        P(),
        P(),
        P(),
        P(),
        P(),
        P(None, None, "mp"),
        P(None, "mp"),
        P(None, "mp", None),
        P(),
        P(("dp", "mp"), None, None),
    )
    return jax.shard_map(
        shards,
        mesh=mesh,
        in_specs=placed,
        out_specs=(
            P(("dp", "mp"), None, None),
            P(("dp", "mp"), None, None),
            P(None, "dp"),
            P(None, "dp"),
            P(None, "dp", "mp"),
            P(None, "dp", "mp"),
            P(None, "dp", "mp"),
            P(None, "dp", "mp"),
            P("dp"),
            P(None, "dp"),
            P(None, "dp"),
            P(None, "dp", "mp"),
            P(None, "mp"),
            P(None, "mp", "dp"),
            P(None, "dp"),
        ),
        check_vma=False,
    )
```

profile of v0, /device:TPU:0, one launch (start us, length us, event | category | flops | bytes accessed | tf_op | source)
XLA Modules:
  0.0 1413.8 jit_solution(11953052416355874428)
XLA Ops:
  14.8 52.2 %all-gather.9.cloned.1.call-done = bf16[12,128,768]{2,1,0:T(8,128)(2,1)} async-done(((bf16[3,128,768]{2,1,0:T(8,128)(2,1)}), bf16[12,128,768]{2,1,0:T(8,128)(2,1)}) %all-gather.9.cloned.1.call-update) | async-done | bytes 2359312 | tf_op jit(solution)/shard_map/all_gather | solution.py:65
  136.3 48.6 %all-gather.11.cloned.1.call-done = bf16[12,128,768]{2,1,0:T(8,128)(2,1)} async-done(((bf16[3,128,768]{2,1,0:T(8,128)(2,1)}), bf16[12,128,768]{2,1,0:T(8,128)(2,1)}) %all-gather.11.cloned.1.call-update) | async-done | bytes 2359312 | tf_op jit(solution)/shard_map/all_gather | solution.py:95
  208.0 45.7 %reduce-scatter.28.cloned.1.call-done = bf16[3,128,768]{2,1,0:T(8,128)(2,1)} async-done(((bf16[12,128,768]{2,1,0:T(8,128)(2,1)}), bf16[3,128,768]{2,1,0:T(8,128)(2,1)}) %reduce-scatter.28.cloned.1.call-update) | async-done | bytes 589840 | tf_op jit(solution)/shard_map/reduce_scatter | solution.py:108
  256.5 50.1 %all-gather.13.cloned.1.call-done = bf16[12,128,768]{2,1,0:T(8,128)(2,1)} async-done(((bf16[3,128,768]{2,1,0:T(8,128)(2,1)}), bf16[12,128,768]{2,1,0:T(8,128)(2,1)}) %all-gather.13.cloned.1.call-update) | async-done | bytes 2359312 | tf_op jit(solution)/shard_map/all_gather | solution.py:65
  382.3 48.6 %all-gather.15.cloned.1.call-done = bf16[12,128,768]{2,1,0:T(8,128)(2,1)} async-done(((bf16[3,128,768]{2,1,0:T(8,128)(2,1)}), bf16[12,128,768]{2,1,0:T(8,128)(2,1)}) %all-gather.15.cloned.1.call-update) | async-done | bytes 2359312 | tf_op jit(solution)/shard_map/all_gather | solution.py:95
  438.4 11.8 multiply_convert_fusion.6
  450.2 31.5 %all-gather.17.cloned.1.call-done = bf16[12,128,768]{2,1,0:T(8,128)(2,1)} async-done(((bf16[3,128,768]{2,1,0:T(8,128)(2,1)}), bf16[12,128,768]{2,1,0:T(8,128)(2,1)}) %all-gather.17.cloned.1.call-update) | async-done | bytes 2359312 | tf_op jit(solution)/shard_map/all_gather | solution.py:169
  495.5 47.0 %reduce-scatter.32.cloned.1.call-done = bf16[3,128,768]{2,1,0:T(8,128)(2,1)} async-done(((bf16[12,128,768]{2,1,0:T(8,128)(2,1)}), bf16[3,128,768]{2,1,0:T(8,128)(2,1)}) %reduce-scatter.32.cloned.1.call-update) | async-done | bytes 589840 | tf_op jit(solution)/shard_map/reduce_scatter | solution.py:184
  555.6 44.6 %all-gather.19.cloned.1.call-done = bf16[12,128,768]{2,1,0:T(8,128)(2,1)} async-done(((bf16[3,128,768]{2,1,0:T(8,128)(2,1)}), bf16[12,128,768]{2,1,0:T(8,128)(2,1)}) %all-gather.19.cloned.1.call-update) | async-done | bytes 2359312 | tf_op jit(solution)/shard_map/all_gather | solution.py:200
  610.5 12.1 multiply_reduce_fusion.1
  655.3 50.1 %all-gather.21.cloned.1.call-done = bf16[12,128,768]{2,1,0:T(8,128)(2,1)} async-done(((bf16[3,128,768]{2,1,0:T(8,128)(2,1)}), bf16[12,128,768]{2,1,0:T(8,128)(2,1)}) %all-gather.21.cloned.1.call-update) | async-done | bytes 2359312 | tf_op jit(solution)/shard_map/all_gather | solution.py:169
  718.7 47.0 %reduce-scatter.34.cloned.1.call-done = bf16[3,128,768]{2,1,0:T(8,128)(2,1)} async-done(((bf16[12,128,768]{2,1,0:T(8,128)(2,1)}), bf16[3,128,768]{2,1,0:T(8,128)(2,1)}) %reduce-scatter.34.cloned.1.call-update) | async-done | bytes 589840 | tf_op jit(solution)/shard_map/reduce_scatter | solution.py:184
  808.7 14.8 %all-gather.23.cloned.1.call-done = bf16[12,128,768]{2,1,0:T(8,128)(2,1)} async-done(((bf16[3,128,768]{2,1,0:T(8,128)(2,1)}), bf16[12,128,768]{2,1,0:T(8,128)(2,1)}) %all-gather.23.cloned.1.call-update) | async-done | bytes 2359312 | tf_op jit(solution)/shard_map/all_gather | solution.py:200
  850.1 12.1 multiply_convert_fusion
  928.1 79.0 %all-reduce.6.cloned.1.call-done = f32[2,768,768]{1,0,2:T(2,128)} async-done(((f32[2,768,768]{1,0,2:T(2,128)}), f32[2,768,768]{1,0,2:T(2,128)}) %all-reduce.6.cloned.1.call-update) | async-done | bytes 4718608
  1009.8 23.3 %all-reduce.2 = (f32[768]{0:T(1024)S(1)}, f32[2,768]{1,0:T(2,128)}) all-reduce(f32[768]{0:T(1024)S(1)} %fusion.112, f32[2,768]{1,0:T(2,128)} %pad_maximum_fusion.10), channel_id=13, replica_groups=mesh['dp'=8,'mp'=4] {'dp'}, use_global_device_ids=true, to_apply=%region_40.41.clone | all-reduce | flops 2304 | bytes 18432
  1045.4 35.9 %reduce-scatter.54.cloned.1.call-done = f32[96,2]{1,0:T(8,128)} async-done(((f32[768,2]{1,0:T(8,128)}), f32[96,2]{1,0:T(8,128)}) %reduce-scatter.54.cloned.1.call-update) | async-done | bytes 784
  1084.3 33.8 %reduce-scatter.46.cloned.1.call-done = f32[96,2]{1,0:T(8,128)} async-done(((f32[768,2]{1,0:T(8,128)}), f32[96,2]{1,0:T(8,128)}) %reduce-scatter.46.cloned.1.call-update) | async-done | bytes 784
  1118.9 36.1 %reduce-scatter.48.cloned.1.call-done = f32[96,2]{1,0:T(8,128)} async-done(((f32[768,2]{1,0:T(8,128)}), f32[96,2]{1,0:T(8,128)}) %reduce-scatter.48.cloned.1.call-update) | async-done | bytes 784
  1155.8 12.4 all-reduce.3
  1179.7 54.1 %reduce-scatter.40.cloned.1.call-done = f32[2,96,768]{2,1,0:T(8,128)} async-done(((f32[2,768,768]{2,1,0:T(8,128)}), f32[2,96,768]{2,1,0:T(8,128)}) %reduce-scatter.40.cloned.1.call-update) | async-done | bytes 589840 | tf_op jit(solution)/shard_map/reduce_scatter | solution.py:326
  1235.5 55.6 %reduce-scatter.36.cloned.1.call-done = f32[2,96,768]{2,1,0:T(8,128)} async-done(((f32[2,768,768]{2,1,0:T(8,128)}), f32[2,96,768]{2,1,0:T(8,128)}) %reduce-scatter.36.cloned.1.call-update) | async-done | bytes 589840 | tf_op jit(solution)/shard_map/reduce_scatter | solution.py:324
  1292.9 56.0 %reduce-scatter.38.cloned.1.call-done = f32[2,96,768]{2,1,0:T(8,128)} async-done(((f32[2,768,768]{2,1,0:T(8,128)}), f32[2,96,768]{2,1,0:T(8,128)}) %reduce-scatter.38.cloned.1.call-update) | async-done | bytes 589840 | tf_op jit(solution)/shard_map/reduce_scatter | solution.py:325
  1350.7 56.0 %reduce-scatter.44.cloned.1.call-done = f32[2,96,768]{2,1,0:T(8,128)} async-done(((f32[2,768,768]{2,1,0:T(8,128)}), f32[2,96,768]{2,1,0:T(8,128)}) %reduce-scatter.44.cloned.1.call-update) | async-done | bytes 589840 | tf_op jit(solution)/shard_map/reduce_scatter | solution.py:347
  (461 shorter events, 438.7 us)
Async XLA Ops:
  7.2 59.8 %all-gather.9.cloned.1.call-start = ((), (), s32[]{:S(2)}) async-start(), calls=%async_computation.15 | async-start | bytes 2949120 | tf_op jit(solution)/shard_map/all_gather | solution.py:65
  13.7 171.2 %all-gather.11.cloned.1.call-start = ((), (), s32[]{:S(2)}) async-start(), calls=%async_computation.16 | async-start | bytes 2949120 | tf_op jit(solution)/shard_map/all_gather | solution.py:95
  135.4 118.3 %reduce-scatter.28.cloned.1.call-start = ((), (), s32[]{:S(2)}) async-start(), calls=%async_computation.17 | async-start | bytes 2949120 | tf_op jit(solution)/shard_map/reduce_scatter | solution.py:108
  206.8 99.8 %all-gather.13.cloned.1.call-start = ((), (), s32[]{:S(2)}) async-start(), calls=%async_computation.18 | async-start | bytes 2949120 | tf_op jit(solution)/shard_map/all_gather | solution.py:65
  256.4 174.5 %all-gather.15.cloned.1.call-start = ((), (), s32[]{:S(2)}) async-start(), calls=%async_computation.19 | async-start | bytes 2949120 | tf_op jit(solution)/shard_map/all_gather | solution.py:95
  381.5 100.2 %all-gather.17.cloned.1.call-start = ((), (), s32[]{:S(2)}) async-start(), calls=%async_computation.21 | async-start | bytes 2949120 | tf_op jit(solution)/shard_map/all_gather | solution.py:169
  382.1 160.4 %reduce-scatter.32.cloned.1.call-start = ((), (), s32[]{:S(2)}) async-start(), calls=%async_computation.22 | async-start | bytes 2949120 | tf_op jit(solution)/shard_map/reduce_scatter | solution.py:184
  495.4 104.8 %all-gather.19.cloned.1.call-start = ((), (), s32[]{:S(2)}) async-start(), calls=%async_computation.23 | async-start | bytes 2949120 | tf_op jit(solution)/shard_map/all_gather | solution.py:200
  550.1 99.3 %reduce-scatter.30.cloned.1.call-start = ((), (), s32[]{:S(2)}) async-start(), calls=%async_computation.20 | async-start | bytes 2949120 | tf_op jit(solution)/shard_map/reduce_scatter | solution.py:108
  555.6 149.7 %all-gather.21.cloned.1.call-start = ((), (), s32[]{:S(2)}) async-start(), calls=%async_computation.24 | async-start | bytes 2949120 | tf_op jit(solution)/shard_map/all_gather | solution.py:169
  655.2 110.4 %reduce-scatter.34.cloned.1.call-start = ((), (), s32[]{:S(2)}) async-start(), calls=%async_computation.25 | async-start | bytes 2949120 | tf_op jit(solution)/shard_map/reduce_scatter | solution.py:184
  718.6 104.9 %all-gather.23.cloned.1.call-start = ((), (), s32[]{:S(2)}) async-start(), calls=%async_computation.26 | async-start | bytes 2949120 | tf_op jit(solution)/shard_map/all_gather | solution.py:200
  773.4 111.3 %reduce-scatter.42.cloned.1.call-start = ((), (), s32[]{:S(2)}) async-start(), calls=%async_computation.30 | async-start | bytes 5308416 | tf_op jit(solution)/shard_map/reduce_scatter | solution.py:332
  779.9 146.2 %reduce-scatter.56.cloned.1.call-start = ((), (), s32[]{:S(2)}) async-start(), calls=%async_computation.37 | async-start | bytes 442368
  787.3 219.8 %all-reduce.6.cloned.1.call-start = ((), (), s32[]{:S(2)}) async-start(), calls=%async_computation.38 | async-start | bytes 9437184
  802.0 242.5 %reduce-scatter.52.cloned.1.call-start = ((), (), s32[]{:S(2)}) async-start(), calls=%async_computation.35 | async-start | bytes 442368
  806.7 274.5 %reduce-scatter.54.cloned.1.call-start = ((), (), s32[]{:S(2)}) async-start(), calls=%async_computation.36 | async-start | bytes 442368
  808.6 309.4 %reduce-scatter.46.cloned.1.call-start = ((), (), s32[]{:S(2)}) async-start(), calls=%async_computation.32 | async-start | bytes 442368
  877.7 277.2 %reduce-scatter.48.cloned.1.call-start = ((), (), s32[]{:S(2)}) async-start(), calls=%async_computation.33 | async-start | bytes 442368
  878.8 299.1 %reduce-scatter.50.cloned.1.call-start = ((), (), s32[]{:S(2)}) async-start(), calls=%async_computation.34 | async-start | bytes 491520
  888.8 345.0 %reduce-scatter.40.cloned.1.call-start = ((), (), s32[]{:S(2)}) async-start(), calls=%async_computation.29 | async-start | bytes 5308416 | tf_op jit(solution)/shard_map/reduce_scatter | solution.py:326
  896.0 395.2 %reduce-scatter.36.cloned.1.call-start = ((), (), s32[]{:S(2)}) async-start(), calls=%async_computation.27 | async-start | bytes 5308416 | tf_op jit(solution)/shard_map/reduce_scatter | solution.py:324
  905.3 443.6 %reduce-scatter.38.cloned.1.call-start = ((), (), s32[]{:S(2)}) async-start(), calls=%async_computation.28 | async-start | bytes 5308416 | tf_op jit(solution)/shard_map/reduce_scatter | solution.py:325
  914.7 492.1 %reduce-scatter.44.cloned.1.call-start = ((), (), s32[]{:S(2)}) async-start(), calls=%async_computation.31 | async-start | bytes 5308416 | tf_op jit(solution)/shard_map/reduce_scatter | solution.py:347
  (122 other events, 1964.0 us)
Sparse Core Ops, SparseCore 0:
  13.8 53.1 all-gather.8
  135.5 49.2 all-gather.10
  206.9 46.8 reduce-scatter.27
  256.6 49.9 all-gather.12
  381.6 49.2 all-gather.14
  432.3 49.2 all-gather.16
  495.5 46.8 reduce-scatter.31
  550.2 49.9 all-gather.18
  602.6 46.8 reduce-scatter.29
  655.3 49.9 all-gather.20
  718.7 46.8 reduce-scatter.33
  773.5 49.9 all-gather.22
  827.0 52.6 reduce-scatter.41
  882.9 33.7 reduce-scatter.55
  920.2 86.7 all-reduce.5
  1010.6 33.8 reduce-scatter.51
  1047.4 33.8 reduce-scatter.53
  1084.2 33.8 reduce-scatter.45
  1121.1 33.8 reduce-scatter.47
  1157.1 20.7 reduce-scatter.49
  1181.7 52.0 reduce-scatter.39
  1237.2 53.8 reduce-scatter.35
  1295.0 53.8 reduce-scatter.37
  1352.8 53.8 reduce-scatter.43
where the time goes:
time: 1420 us; the launch traced here: 1410 us
  waiting for transfers between devices  910 us (64%)
  matrix products  193 us (14%)
  local copies, waits for them, and re-layouts  155 us (11%)
  other arithmetic  102 us (7%)
  blocking collectives  35.7 us (3%)
  between operations  16.7 us (1%)
    unnamed x31, waiting for transfers between devices  207 us
    all_gather x2, waiting for transfers between devices, forward_layer(): gathered = lax.all_gather(normed, 'mp', axis=0, tiled=True)  102 us
    all_gather x2, waiting for transfers between devices, forward_layer(): gathered_two = lax.all_gather(normed_two, 'mp', axis=0, tiled=True)  97.2 us
    reduce_scatter x2, waiting for transfers between devices, backward_layer(): lax.psum_scatter(normed_terms.astype(jnp.bfloat16), 'mp', scatter_dimensi...  93.9 us
    reshape x12, local copies, waits for them, and re-layouts, project(): return made.reshape(page_count, slot_count, head_count, head_width)  90.5 us
    all_gather x2, waiting for transfers between devices, backward_layer(): grad_all = lax.all_gather(grad_low, 'mp', axis=0, tiled=True)  81.6 us
    all_gather x2, waiting for transfers between devices, backward_layer(): branch_all = lax.all_gather(branch_low, 'mp', axis=0, tiled=True)  59.4 us
    reduce_scatter x1, waiting for transfers between devices, shards(): lax.psum_scatter(stacked[9], 'dp', scatter_dimension=1, tiled=True)  56 us
  transfers between devices with their start and end apart: 24, of which 22 were waited for; matrix products, arithmetic and copies ran while one was open for 15% of the time, Pallas kernels for 0%

commit v1 on v0

v1 whole, which is shorter than its diff:
```python
import functools

import jax
import jax.numpy as jnp
from jax import lax
from jax.experimental import pallas as pl
from jax.experimental.pallas import tpu as pltpu
from jax.sharding import PartitionSpec as P

HEADS = 12
TEXT = 112
F32 = jnp.float32
BF16 = jnp.bfloat16
VMEM_BYTES = 56 * 2**20


def dot(a, b, a_dim, b_dim):
    return lax.dot_general(a, b, (((a_dim,), (b_dim,)), ((), ())), preferred_element_type=F32)


def whiten(rows):
    centered = rows - jnp.mean(rows, axis=-1, keepdims=True)
    spread = jnp.mean(centered * centered, axis=-1, keepdims=True)
    inverse = lax.rsqrt(spread + 1e-05)
    return centered * inverse, inverse


def whiten_back(white, inverse, gain, grad):
    scaled = grad * gain
    first = jnp.mean(scaled, axis=-1, keepdims=True)
    second = jnp.mean(scaled * white, axis=-1, keepdims=True)
    return inverse * (scaled - first - white * second)


def column_sum(rows):
    return jnp.sum(rows, axis=0, keepdims=True)


def gelu_and_slope(values):
    size = jnp.abs(values)
    t = 1.0 / (1.0 + (0.3275911 * 0.7071067811865476) * size)
    bell = jnp.exp(-0.5 * values * values)
    poly = 0.5 * 1.061405429
    poly = poly * t + 0.5 * -1.453152027
    poly = poly * t + 0.5 * 1.421413741
    poly = poly * t + 0.5 * -0.284496736
    poly = poly * t + 0.5 * 0.254829592
    tail = poly * t * bell
    phi = jnp.where(values >= 0.0, 1.0 - tail, tail)
    return values * phi, phi + values * bell * 0.3989422804014327


def split_heads(pair):
    lane = lax.broadcasted_iota(jnp.int32, pair.shape, 1)
    first = lane < pair.shape[1] // 2
    zero = jnp.zeros_like(pair)
    return jnp.concatenate([jnp.where(first, pair, zero), jnp.where(first, zero, pair)], axis=0)


def join_heads(both):
    slots = both.shape[0] // 2
    lane = lax.broadcasted_iota(jnp.int32, (slots, both.shape[1]), 1)
    return jnp.where(lane < both.shape[1] // 2, both[:slots], both[slots:])


def start_copies(sources, targets, sems):
    copies = [
        pltpu.make_async_copy(source, target, sems.at[at])
        for at, (source, target) in enumerate(zip(sources, targets))
    ]
    for copy in copies:
        copy.start()
    return copies


def attend_kernel(layer, crossed, resid, mask, gain, shift, gate, wq, wk, wv, wo,
                  q_out, k_out, v_out, p_out, c_out, mixed, branch_out, held, sems):
    pages, slots = mask.shape[0], mask.shape[1]
    width = resid.shape[1]
    pairs = HEADS // 2
    pair_width = width // pairs
    scale = 1.0 / (width // HEADS) ** 0.5
    copies = start_copies(
        [w.at[layer] for w in (wq, wk, wv, wo)], [held.at[at] for at in range(4)], sems
    )
    white, _ = whiten(resid[...].astype(F32))
    normed = (white * gain[layer:layer + 1] + shift[layer:layer + 1]).astype(BF16)
    copies[0].wait()
    q_out[...] = (dot(normed, held[0], 1, 0).astype(BF16).astype(F32) * scale).astype(BF16)
    copies[1].wait()
    k_out[...] = dot(normed, held[1], 1, 0).astype(BF16)
    copies[2].wait()
    v_out[...] = dot(normed, held[2], 1, 0).astype(BF16)

    for page in range(pages):
        rows = slice(page * slots, (page + 1) * slots)
        bias = mask[page]
        for pair in range(pairs):
            cols = slice(pair * pair_width, (pair + 1) * pair_width)
            scores = dot(split_heads(k_out[rows, cols]), q_out[rows, cols], 1, 1)
            scores = scores.reshape(2, slots, slots) + bias[None]
            top = jnp.max(scores, axis=1, keepdims=True)
            raised = jnp.exp(scores - top)
            probs = raised * (1.0 / jnp.sum(raised, axis=1, keepdims=True))
            probs = probs.reshape(2 * slots, slots).astype(BF16)
            p_out[page, pair] = probs
            c_out[rows, cols] = dot(probs, split_heads(v_out[rows, cols]), 0, 0).astype(BF16)
    copies[3].wait()
    branch = dot(c_out[...], held[3], 1, 0)
    if crossed:
        branch_out[...] = branch.astype(BF16)
        branch = branch * jax.nn.sigmoid(gate[...])
    mixed[...] = resid[...].astype(F32) + branch


def attend(layer, crossed, resid, mask, gain, shift, gate, weights):
    rows, width = resid.shape
    pages, slots = mask.shape[:2]
    low = jax.ShapeDtypeStruct((rows, width), BF16)
    vmem = pl.BlockSpec(memory_space=pltpu.VMEM)
    outs = [low, low, low, jax.ShapeDtypeStruct((pages, HEADS // 2, 2 * slots, slots), BF16), low,
            jax.ShapeDtypeStruct((rows, width), F32)]
    if crossed:
        outs.append(low)

    def body(*refs):
        ins, rest = refs[:9], list(refs[9:])
        if not crossed:
            rest.insert(6, None)
        attend_kernel(layer, crossed, *ins, *rest)

    return pl.pallas_call(
        body,
        out_shape=outs,
        in_specs=[vmem] * 5 + [pl.BlockSpec(memory_space=pl.ANY)] * 4,
        out_specs=[vmem] * len(outs),
        scratch_shapes=[pltpu.VMEM((4, width, width), BF16), pltpu.SemaphoreType.DMA((4,))],
        compiler_params=pltpu.CompilerParams(vmem_limit_bytes=VMEM_BYTES),
        cost_estimate=pl.CostEstimate(flops=8 * rows * width * width, bytes_accessed=14 * 2**20, transcendentals=0),
    )(resid, mask, gain, shift, gate, *weights)


class Pieces:
    def __init__(self, arrays, plan, blocks, piece_rows):
        self.arrays, self.plan, self.blocks, self.piece_rows = arrays, plan, blocks, piece_rows

    def copies(self, refs, held, blocks, sems, shard):
        made = []
        for at, (array, index, kind, owner, place) in enumerate(self.plan):
            if owner != shard:
                continue
            if place is None:
                target = held[kind].at[shard]
            else:
                start = pl.multiple_of(blocks[place] * self.piece_rows, self.piece_rows)
                target = held[kind].at[shard, pl.ds(start, self.piece_rows)]
            made.append(pltpu.make_async_copy(refs[array].at[index], target, sems.at[at]))
        return made

    def start_and_wait(self, refs, held, blocks, sems, shards):
        step = pl.program_id(0)

        @pl.when(step == 0)
        def _():
            for shard in range(shards):
                for copy in self.copies(refs, held, blocks, sems, shard):
                    copy.start()

        def wait():
            for shard in range(shards):
                @pl.when(step == shard)
                def _():
                    for copy in self.copies(refs, held, blocks, sems, shard):
                        copy.wait()
        return wait


def feed_kernel(layer, pieces, blocks, mixed, gain, shift, b_up, b_down, *rest):
    count = len(pieces.arrays)
    refs = rest[:count]
    result, active_out, slope_out, up, down, low, total, sems = rest[count:]
    shards, width = up.shape[0], up.shape[2]
    step = pl.program_id(0)
    wait = pieces.start_and_wait(refs, (up, down), blocks, sems, shards)

    @pl.when(step == 0)
    def _():
        white, _ = whiten(mixed[...])
        low[...] = (white * gain[layer:layer + 1] + shift[layer:layer + 1]).astype(BF16)
        total[...] = mixed[...] + b_down[layer:layer + 1]

    wait()
    parts = 3
    part = width // parts
    for at in range(parts):
        cols = slice(at * part, (at + 1) * part)
        upper = dot(low[...], up[step, :, cols], 1, 0) + b_up[0, :, cols]
        active, slope = gelu_and_slope(upper)
        active = active.astype(BF16)
        active_out[0, :, cols] = active
        slope_out[0, :, cols] = slope.astype(BF16)
        total[...] += dot(active, down[step, cols, :], 1, 0)

    @pl.when(step == shards - 1)
    def _():
        result[...] = total[...].astype(result.dtype)


def feed(layer, mixed, gain, shift, b_up, b_down, pieces, out_type):
    rows, width = mixed.shape
    shards = b_up.shape[0]
    whole = lambda shape: pl.BlockSpec(shape, lambda step: (0,) * len(shape))
    each = lambda shape: pl.BlockSpec((1,) + shape, lambda step: (step,) + (0,) * len(shape))
    return pl.pallas_call(
        functools.partial(feed_kernel, layer, pieces),
        grid=(shards,),
        out_shape=[jax.ShapeDtypeStruct((rows, width), out_type)]
        + [jax.ShapeDtypeStruct((shards, rows, width), BF16)] * 2,
        in_specs=[pl.BlockSpec(memory_space=pltpu.SMEM), whole((rows, width)), whole(gain.shape), whole(shift.shape),
                  each((1, width)), whole(b_down.shape)]
        + [pl.BlockSpec(memory_space=pl.ANY)] * len(pieces.arrays),
        out_specs=[whole((rows, width)), each((rows, width)), each((rows, width))],
        scratch_shapes=[pltpu.VMEM((shards, width, width), BF16), pltpu.VMEM((shards, width, width), BF16),
                        pltpu.VMEM((rows, width), BF16), pltpu.VMEM((rows, width), F32),
                        pltpu.SemaphoreType.DMA((len(pieces.plan),))],
        compiler_params=pltpu.CompilerParams(vmem_limit_bytes=VMEM_BYTES),
        cost_estimate=pl.CostEstimate(flops=16 * rows * width * width, bytes_accessed=20 * 2**20, transcendentals=0),
    )(pieces.blocks, mixed, gain, shift, b_up, b_down, *pieces.arrays)


def turn_rows(rows, held, turned, blocks, order):
    held[...] = rows.T
    size = held.shape[0] // len(order)
    for at, place in enumerate(order):
        start = pl.multiple_of(blocks[place] * size, size)
        turned[at * size:(at + 1) * size] = held[pl.ds(start, size)]


def feed_back_kernel(layer, pieces, orders, blocks, grad_out, mixed, gain, shift, active, slope, *rest):
    count = len(pieces.arrays)
    refs = rest[:count]
    (grad_mixed, up_keep, up_send, down_keep, down_send, sums, up_sums,
     up, down, low, low_turned, normed_turned, held, total, sems) = rest[count:]
    shards = up.shape[0]
    half = up_keep.shape[1]
    step = pl.program_id(0)
    wait = pieces.start_and_wait(refs, (up, down), blocks, sems, shards)

    @pl.when(step == 0)
    def _():
        rows = grad_out[...].astype(F32)
        low[...] = rows.astype(BF16)
        sums[0:1] = column_sum(rows)
        turn_rows(low[...], held, low_turned, blocks, orders[1])
        white, _ = whiten(mixed[...])
        normed = (white * gain[layer:layer + 1] + shift[layer:layer + 1]).astype(BF16)
        turn_rows(normed, held, normed_turned, blocks, orders[0])
        total[...] = jnp.zeros_like(total)

    wait()
    made = dot(low_turned[...], active[0], 1, 0).astype(BF16)
    down_keep[0] = made[:half]
    down_send[0] = made[half:]
    upper = dot(low[...], down[step], 1, 1) * slope[0].astype(F32)
    up_sums[0] = column_sum(upper)
    upper_low = upper.astype(BF16)
    made = dot(normed_turned[...], upper_low, 1, 0).astype(BF16)
    up_keep[0] = made[:half]
    up_send[0] = made[half:]
    total[...] += dot(upper_low, up[step], 1, 1)

    @pl.when(step == shards - 1)
    def _():
        white, inverse = whiten(mixed[...])
        grad = total[...]
        sums[1:2] = column_sum(grad * white)
        sums[2:3] = column_sum(grad)
        grad_mixed[...] = grad_out[...].astype(F32) + whiten_back(white, inverse, gain[layer:layer + 1], grad)


def feed_back(layer, grad_out, mixed, gain, shift, active, slope, pieces, orders):
    rows, width = mixed.shape
    shards = active.shape[0]
    half = width // 2
    whole = lambda shape: pl.BlockSpec(shape, lambda step: (0,) * len(shape))
    each = lambda shape: pl.BlockSpec((1,) + shape, lambda step: (step,) + (0,) * len(shape))
    return pl.pallas_call(
        functools.partial(feed_back_kernel, layer, pieces, orders),
        grid=(shards,),
        out_shape=[jax.ShapeDtypeStruct((rows, width), F32)]
        + [jax.ShapeDtypeStruct((shards, half, width), BF16)] * 4
        + [jax.ShapeDtypeStruct((3, width), F32), jax.ShapeDtypeStruct((shards, 1, width), F32)],
        in_specs=[pl.BlockSpec(memory_space=pltpu.SMEM), whole((rows, width)), whole((rows, width)), whole(gain.shape),
                  whole(shift.shape), each((rows, width)), each((rows, width))]
        + [pl.BlockSpec(memory_space=pl.ANY)] * len(pieces.arrays),
        out_specs=[whole((rows, width))] + [each((half, width))] * 4 + [whole((3, width)), each((1, width))],
        scratch_shapes=[pltpu.VMEM((shards, width, width), BF16), pltpu.VMEM((shards, width, width), BF16),
                        pltpu.VMEM((rows, width), BF16), pltpu.VMEM((width, rows), BF16),
                        pltpu.VMEM((width, rows), BF16), pltpu.VMEM((width, rows), BF16),
                        pltpu.VMEM((rows, width), F32), pltpu.SemaphoreType.DMA((len(pieces.plan),))],
        compiler_params=pltpu.CompilerParams(vmem_limit_bytes=VMEM_BYTES),
        cost_estimate=pl.CostEstimate(flops=32 * rows * width * width, bytes_accessed=30 * 2**20, transcendentals=0),
    )(pieces.blocks, grad_out, mixed, gain, shift, active, slope, *pieces.arrays)


def attend_back_kernel(layer, crossed, orders, blocks, grad_mixed, resid, gain, shift, gate, q, k, v, p, context, branch,
                       wq, wk, wv, wo, grad_resid, first_keep, first_send, second_keep, second_send, sums,
                       held, turning, turned, gc, gq, gk, gv, sems):
    pages, slots = p.shape[0], p.shape[3]
    width = resid.shape[1]
    half = width // 2
    pairs = HEADS // 2
    pair_width = width // pairs
    scale = 1.0 / (width // HEADS) ** 0.5
    copies = start_copies(
        [w.at[layer] for w in (wo, wq, wk, wv)], [held.at[at] for at in range(4)], sems
    )
    grad = grad_mixed[...]
    if crossed:
        opened = jax.nn.sigmoid(gate[...])
        sums[2:3] = column_sum(grad * branch[...].astype(F32)) * (opened * (1.0 - opened))
        low = (grad * opened).astype(BF16)
    else:
        low = grad.astype(BF16)
    turn_rows(context[...], turning, turned, blocks, orders[1])
    made = dot(turned[...], low, 1, 0).astype(BF16)
    second_keep[1] = made[:half]
    second_send[1] = made[half:]
    copies[0].wait()
    gc[...] = dot(low, held[0], 1, 1).astype(BF16)

    for page in range(pages):
        rows = slice(page * slots, (page + 1) * slots)
        for pair in range(pairs):
            cols = slice(pair * pair_width, (pair + 1) * pair_width)
            probs_low = p[page, pair]
            probs = probs_low.astype(F32).reshape(2, slots, slots)
            grad_probs = dot(split_heads(v[rows, cols]), gc[rows, cols], 1, 1).reshape(2, slots, slots)
            delta = jnp.sum(probs * grad_probs, axis=1, keepdims=True)
            grad_scores = (probs * (grad_probs - delta)).astype(BF16).reshape(2 * slots, slots)
            gq[rows, cols] = (dot(grad_scores, split_heads(k[rows, cols]), 0, 0) * scale).astype(BF16)
            gk[rows, cols] = join_heads(dot(grad_scores, q[rows, cols], 1, 0)).astype(BF16)
            gv[rows, cols] = join_heads(dot(probs_low, gc[rows, cols], 1, 0)).astype(BF16)

    white, inverse = whiten(resid[...].astype(F32))
    normed = (white * gain[layer:layer + 1] + shift[layer:layer + 1]).astype(BF16)
    turn_rows(normed, turning, turned, blocks, orders[1])
    made = dot(turned[...], gv[...], 1, 0).astype(BF16)
    second_keep[0] = made[:half]
    second_send[0] = made[half:]
    turn_rows(normed, turning, turned, blocks, orders[0])
    for at, rows in enumerate((gq, gk)):
        made = dot(turned[...], rows[...], 1, 0).astype(BF16)
        first_keep[at] = made[:half]
        first_send[at] = made[half:]
    for copy in copies[1:]:
        copy.wait()
    total = dot(gq[...], held[1], 1, 1) + dot(gk[...], held[2], 1, 1) + dot(gv[...], held[3], 1, 1)
    sums[0:1] = column_sum(total * white)
    sums[1:2] = column_sum(total)
    grad_resid[...] = grad + whiten_back(white, inverse, gain[layer:layer + 1], total)


def attend_back(layer, crossed, grad_mixed, resid, gain, shift, gate, kept, weights, blocks, orders):
    rows, width = resid.shape
    half = width // 2
    vmem = pl.BlockSpec(memory_space=pltpu.VMEM)
    kept = list(kept)
    given = 6 + len(kept) + 4

    def body(*refs):
        ins, rest = list(refs[:given]), refs[given:]
        if not crossed:
            ins.insert(11, None)
        attend_back_kernel(layer, crossed, orders, *ins, *rest)

    low = pltpu.VMEM((rows, width), BF16)
    return pl.pallas_call(
        body,
        out_shape=[jax.ShapeDtypeStruct((rows, width), F32)]
        + [jax.ShapeDtypeStruct((2, half, width), BF16)] * 4
        + [jax.ShapeDtypeStruct((3 if crossed else 2, width), F32)],
        in_specs=[pl.BlockSpec(memory_space=pltpu.SMEM)] + [vmem] * (5 + len(kept))
        + [pl.BlockSpec(memory_space=pl.ANY)] * 4,
        out_specs=[vmem] * 6,
        scratch_shapes=[pltpu.VMEM((4, width, width), BF16), pltpu.VMEM((width, rows), BF16),
                        pltpu.VMEM((width, rows), BF16), low, low, low, low, pltpu.SemaphoreType.DMA((4,))],
        compiler_params=pltpu.CompilerParams(vmem_limit_bytes=VMEM_BYTES),
        cost_estimate=pl.CostEstimate(flops=16 * rows * width * width, bytes_accessed=24 * 2**20, transcendentals=0),
    )(blocks, grad_mixed, resid, gain, shift, gate, *kept, *(weights[at] for at in (0, 1, 2, 3)))


def swap(value, axis, bit):
    size = lax.axis_size(axis)
    return lax.ppermute(value, axis, [(at, at ^ bit) for at in range(size)])


class Eighths:
    bits = (1, 2, 4)
    orders = ((0, 4, 2, 6, 1, 5, 3, 7), (0, 2, 4, 6, 1, 3, 5, 7))

    def __init__(self):
        self.parts = 8
        self.blocks = lax.axis_index("dp") ^ jnp.arange(8, dtype=jnp.int32)

    def gather(self, w_up, w_down):
        layers, width, shard_width = w_up.shape
        rows = width // 8
        at = lax.axis_index("dp") * rows
        shards = lax.axis_size("mp")
        own = jnp.stack([lax.dynamic_slice_in_dim(w_up, at, rows, 1), lax.dynamic_slice_in_dim(w_down, at, rows, 1)], 1)
        made = []
        for layer in range(layers):
            mine = own[layer]
            far = [swap(mine, "mp", other) for other in range(1, shards)]
            ups = jnp.stack([piece[0] for piece in far])
            downs = jnp.stack([piece[1] for piece in far])
            ups_x = swap(ups, "dp", 2)
            downs_y = swap(downs, "dp", 4)
            ups_two = jnp.stack([ups, ups_x])
            downs_two = jnp.stack([downs, downs_y])
            ups_y = swap(ups_two, "dp", 4)
            downs_x = swap(downs_two, "dp", 2)
            halves = [ups_two, ups_y, downs_two, downs_x]
            arrays = [w_up, w_down] + halves + [swap(half, "dp", 1) for half in halves]
            plan = [(0, layer, 0, 0, None), (1, layer, 1, 0, None)]
            for core in range(2):
                for kind in range(2):
                    inner, outer = ((2, 4), (4, 2))[kind]
                    for second in range(2):
                        for first in range(2):
                            for other in range(1, shards):
                                place = core + inner * first + outer * second
                                plan.append((2 + 4 * core + 2 * kind + second, (first, other - 1), kind, other, place))
            made.append(Pieces(arrays, plan, self.blocks, rows))
        return made

    def order_hidden(self, bias):
        shards = lax.axis_size("mp")
        far = [bias] + [swap(bias, "mp", other) for other in range(1, shards)]
        return jnp.stack(far, 1)[:, :, None, :]

    def hidden_sums(self, sums):
        shards = lax.axis_size("mp")
        me = lax.axis_index("mp")
        return jnp.concatenate([lax.dynamic_slice_in_dim(sums[:, 0], me ^ at, 1, 0) for at in range(shards)])

    def add_rows(self, keep, send, first, second):
        size = keep.shape[1] // 4
        terms = [keep, swap(send, "dp", 1)]
        for bit, start in ((first, 2 * size), (second, size)):
            out = sum(term[:, start:2 * start].astype(F32) for term in terms).astype(BF16)
            terms.append(swap(out, "dp", bit))
        return [term[:, :size] for term in terms]

    def add_hidden(self, terms):
        shards = terms[0].shape[0]
        parts = [sum(term[at].astype(F32) for term in terms) for at in range(shards)]
        return parts[0] + sum(swap(parts[at].astype(BF16), "mp", at).astype(F32) for at in range(1, shards))

    def add_columns(self, terms):
        shards = lax.axis_size("mp")
        me = lax.axis_index("mp")
        share = terms[0].shape[-1] // shards
        whole = sum(term.astype(F32) for term in terms)
        parts = [lax.dynamic_slice_in_dim(whole, (me ^ at) * share, share, 2) for at in range(shards)]
        return parts[0] + sum(swap(parts[at].astype(BF16), "mp", at).astype(F32) for at in range(1, shards))

    def add_feed(self, keep, send, kind):
        return self.add_hidden(self.add_rows(keep, send, *((2, 4), (4, 2))[kind]))

    def add_attend(self, keep, send, kind):
        return self.add_columns(self.add_rows(keep, send, *((2, 4), (4, 2))[kind]))


class Anywhere:
    orders = ((0, 1), (0, 1))

    def __init__(self):
        self.blocks = jnp.arange(2, dtype=jnp.int32)

    def gather(self, w_up, w_down):
        shards = lax.axis_size("mp")
        made = []
        for layer in range(w_up.shape[0]):
            arrays = [lax.all_gather(w_up[layer], "mp"), lax.all_gather(w_down[layer], "mp")]
            plan = [(kind, at, kind, at, None) for kind in range(2) for at in range(shards)]
            made.append(Pieces(arrays, plan, self.blocks, 0))
        return made

    def order_hidden(self, bias):
        return lax.all_gather(bias, "mp", axis=1)[:, :, None, :]

    def hidden_sums(self, sums):
        return sums[:, 0]

    def add_feed(self, keep, send, kind):
        whole = jnp.concatenate([keep, send], 1)
        whole = lax.psum_scatter(whole, "mp", scatter_dimension=0, tiled=True)
        return lax.psum_scatter(whole[0].astype(F32), "dp", scatter_dimension=0, tiled=True)

    def add_attend(self, keep, send, kind):
        whole = jnp.concatenate([keep, send], 1)
        whole = lax.psum_scatter(whole, "mp", scatter_dimension=2, tiled=True)
        return lax.psum_scatter(whole.astype(F32), "dp", scatter_dimension=1, tiled=True)


def shards(inputs, slot_valid, ln1_gain, ln1_bias, w_query, w_key, w_value, w_out, gate_logit,
           ln2_gain, ln2_bias, w_up, b_up, w_down, b_down, cotangent):
    pages, slots, width = inputs.shape
    dp, mp = lax.axis_size("dp"), lax.axis_size("mp")
    way = Eighths() if dp == 8 and mp == 4 and width % (16 * dp) == 0 else Anywhere()
    blocks, orders = way.blocks, way.orders

    own_valid = lax.dynamic_slice_in_dim(slot_valid, lax.axis_index("mp") * pages, pages, 0) == 1
    key_text = lax.broadcasted_iota(jnp.int32, (slots, slots), 0) < TEXT
    query_text = lax.broadcasted_iota(jnp.int32, (slots, slots), 1) < TEXT
    live = jnp.broadcast_to(own_valid[:, :, None], (pages, slots, slots))
    masks = [
        jnp.where(jnp.logical_and(live, (key_text != query_text)[None]), 0.0, -1e30).astype(F32),
        jnp.where(live, 0.0, -1e30).astype(F32),
    ]
    gate = gate_logit[None]
    pieces = way.gather(w_up, w_down)
    hidden_bias = way.order_hidden(b_up)
    forward_weights = (w_query, w_key, w_value, w_out)
    backward_weights = (w_query, w_key, w_value, w_out)

    resid = inputs.reshape(pages * slots, width)
    kept = []
    for layer in range(2):
        crossed = layer == 0
        q, k, v, p, context, mixed, *branch = attend(
            layer, crossed, resid, masks[layer], ln1_gain, ln1_bias, gate, forward_weights)
        result, active, slope = feed(
            layer, mixed, ln2_gain, ln2_bias, hidden_bias[layer], b_down, pieces[layer], F32 if crossed else BF16)
        kept.append((resid, (q, k, v, p, context, *branch), mixed, active, slope))
        resid = result

    grad = cotangent.reshape(pages * slots, width)
    feed_grads, attend_grads, sums = [None] * 2, [None] * 2, [None] * 2
    for layer in (1, 0):
        crossed = layer == 0
        before, saved, mixed, active, slope = kept[layer]
        grad, up_keep, up_send, down_keep, down_send, feed_sums, up_sums = feed_back(
            layer, grad, mixed, ln2_gain, ln2_bias, active, slope, pieces[layer], orders)
        down_grad = way.add_feed(down_keep, down_send, 1)
        up_grad = way.add_feed(up_keep, up_send, 0)
        grad, first_keep, first_send, second_keep, second_send, attend_sums = attend_back(
            layer, crossed, grad, before, ln1_gain, ln1_bias, gate, saved, backward_weights, blocks, orders)
        first = way.add_attend(first_keep, first_send, 0)
        second = way.add_attend(second_keep, second_send, 1)
        feed_grads[layer] = (up_grad, down_grad.T)
        attend_grads[layer] = (first[0], first[1], second[0], second[1])
        sums[layer] = jnp.concatenate([feed_sums, attend_sums, way.hidden_sums(up_sums)])

    both = lax.psum(jnp.concatenate(sums), ("dp", "mp"))
    lines = width // dp
    mine = lax.dynamic_slice_in_dim(both, lax.axis_index("dp") * lines, lines, 1)
    early = sums[0].shape[0]
    pick = lambda first, second: jnp.stack([mine[first], mine[early + second]])
    me = lax.axis_index("mp")
    bup_grad = jnp.concatenate([
        lax.dynamic_slice_in_dim(both, 6 + me, 1, 0), lax.dynamic_slice_in_dim(both, early + 5 + me, 1, 0)])
    pairs = [jnp.stack([attend_grads[0][at], attend_grads[1][at]]) for at in range(4)]
    return (
        resid.reshape(pages, slots, width),
        grad.reshape(pages, slots, width),
        pick(3, 3),
        pick(4, 4),
        pairs[0],
        pairs[1],
        pairs[2],
        pairs[3],
        mine[5],
        pick(1, 1),
        pick(2, 2),
        jnp.stack([feed_grads[0][0], feed_grads[1][0]]),
        bup_grad,
        jnp.stack([feed_grads[0][1], feed_grads[1][1]]),
        pick(0, 0),
    )


def solution(mesh):
    rows = P(("dp", "mp"), None, None)
    return jax.shard_map(
        shards,
        mesh=mesh,
        in_specs=(rows, P("dp", None), P(), P(), P(), P(), P(), P(), P(), P(), P(), P(None, None, "mp"),
                  P(None, "mp"), P(None, "mp", None), P(), rows),
        out_specs=(rows, rows, P(None, "dp"), P(None, "dp"), P(None, "dp", "mp"), P(None, "dp", "mp"),
                   P(None, "dp", "mp"), P(None, "dp", "mp"), P("dp"), P(None, "dp"), P(None, "dp"),
                   P(None, "dp", "mp"), P(None, "mp"), P(None, "mp", "dp"), P(None, "dp")),
        check_vma=False,
    )
```

time: 1420 us -> 502 us (0.35)
  waiting for transfers between devices: 910 us -> 208 us
  matrix products: 193 us -> 0 us
  local copies, waits for them, and re-layouts: 155 us -> 14.2 us
  Pallas kernels: 0 us -> 107 us
  starting transfers between devices: 1.95 us -> 95.9 us
  other arithmetic: 102 us -> 28.5 us
  between operations: 16.7 us -> 1.82 us
    reduce_scatter x9 -> x0, waiting for transfers between devices: 363 us -> none  [the longest x2 93.9 us: backward_layer(): lax.psum_scatter(normed_terms.astype(jnp.bfloat16), 'mp', scatter_dimensi...]
    all_gather x8 -> x0, waiting for transfers between devices: 341 us -> none  [the longest x2 102 us: forward_layer(): gathered = lax.all_gather(normed, 'mp', axis=0, tiled=True)]
    ppermute x0 -> x73, waiting for transfers between devices: none -> 208 us  [swap(): return lax.ppermute(value, axis, [(at, at ^ bit) for at in range(size)])]
    unnamed x31 -> x0, waiting for transfers between devices: 207 us -> none
    dot_general x48 -> x0, matrix products: 193 us -> none  [the longest x6 23.2 us: project(): jnp.dot(row_matrix, weight, preferred_element_type=jnp.float32)]
    pallas_call x0 -> x8, Pallas kernels: none -> 107 us  [the longest x2 34.2 us: feed_back(): pl.pallas_call(functools.partial(feed_back_kernel, layer, pieces, orders)...]
    ppermute x0 -> x73, starting transfers between devices: none -> 95.9 us  [swap(): return lax.ppermute(value, axis, [(at, at ^ bit) for at in range(size)])]
    reshape x12 -> x0, local copies, waits for them, and re-layouts: 90.5 us -> none  [project(): return made.reshape(page_count, slot_count, head_count, head_width)]
  transfers between devices with their start and end apart: 24 -> 73, of which waited for: 22 -> 32; matrix products, arithmetic and copies ran while one was open for 15% -> 8% of each run, Pallas kernels for 0% -> 13%
where the time goes in v1:
time: 502 us; the launch traced here: 495 us
  waiting for transfers between devices  208 us (41%)
  Pallas kernels  107 us (21%)
  starting transfers between devices  95.9 us (19%)
  blocking collectives  39.6 us (8%)
  other arithmetic  28.5 us (6%)
  local copies, waits for them, and re-layouts  14.2 us (3%)
    ppermute x73, waiting for transfers between devices, swap(): return lax.ppermute(value, axis, [(at, at ^ bit) for at in range(size)])  208 us
    ppermute x73, starting transfers between devices, swap(): return lax.ppermute(value, axis, [(at, at ^ bit) for at in range(size)])  95.9 us
    psum x1, blocking collectives, shards(): both = lax.psum(jnp.concatenate(sums), ('dp', 'mp'))  39.6 us
    pallas_call x2, Pallas kernels, feed_back(): pl.pallas_call(functools.partial(feed_back_kernel, layer, pieces, orders)...  34.2 us
    pallas_call x2, Pallas kernels, attend_back(): pl.pallas_call(body, out_shape=[jax.ShapeDtypeStruct((rows, width), F32)]...  27.6 us
    pallas_call x2, Pallas kernels, feed(): pl.pallas_call(functools.partial(feed_kernel, layer, pieces), grid=(shard...  26.7 us
    pallas_call x2, Pallas kernels, attend(): pl.pallas_call(body, out_shape=outs, in_specs=[vmem] * 5 + [pl.BlockSpec(...  18.3 us
    convert_element_type x16, other arithmetic, add_rows(): sum((term[:, start:2 * start].astype(F32) for term in terms)).astype(BF16)  11.3 us
  transfers between devices with their start and end apart: 73, of which 32 were waited for; matrix products, arithmetic and copies ran while one was open for 8% of the time, Pallas kernels for 13%

profile of v1, /device:TPU:0, one launch (start us, length us, event | category | flops | bytes accessed | tf_op | source)
XLA Modules:
  0.0 495.1 jit_solution(2441332982780899202)
XLA Ops:
  1.8 5.1 %collective-permute-start.5 = (bf16[2,96,768]{2,1,0:T(8,128)(2,1)S(1)}, bf16[2,96,768]{2,1,0:T(8,128)(2,1)S(1)}, u32[]{:S(2)}, u32[]{:S(2)}) collective-permute-start(bf16[2,96,768]{2,1,0:T(8,128)(2,1)S(1)} %get-tuple-element.132), channel_id=1, source_target_pairs={{0,3},{1,2},{2,1},{3,0},{4,7},{5,6},{6,5},{7,4},{8,11},{9,10},{10,... | collective-permute-start | bytes 884744 | tf_op jit(solution)/shard_map/ppermute | solution.py:395
  14.9 13.2 %collective-permute-start.14 = (bf16[2,96,768]{2,1,0:T(8,128)(2,1)S(1)}, bf16[2,96,768]{2,1,0:T(8,128)(2,1)S(1)}, u32[]{:S(2)}, u32[]{:S(2)}) collective-permute-start(bf16[2,96,768]{2,1,0:T(8,128)(2,1)S(1)} %get-tuple-element.131), channel_id=1, source_target_pairs={{0,1},{1,0},{2,3},{3,2},{4,5},{5,4},{6,7},{7,6},{8,9},{9,8},{10,11... | collective-permute-start | bytes 884744 | tf_op jit(solution)/shard_map/ppermute | solution.py:395
  28.1 17.5 %collective-permute-done.4 = bf16[2,96,768]{2,1,0:T(8,128)(2,1)S(1)} collective-permute-done((bf16[2,96,768]{2,1,0:T(8,128)(2,1)S(1)}, bf16[2,96,768]{2,1,0:T(8,128)(2,1)S(1)}, u32[]{:S(2)}, u32[]{:S(2)}) %collective-permute-start.4) | collective-permute-done | bytes 294944 | tf_op jit(solution)/shard_map/ppermute | solution.py:395
  49.0 8.3 %collective-permute-done.15 = bf16[2,96,768]{2,1,0:T(8,128)(2,1)S(1)} collective-permute-done((bf16[2,96,768]{2,1,0:T(8,128)(2,1)S(1)}, bf16[2,96,768]{2,1,0:T(8,128)(2,1)S(1)}, u32[]{:S(2)}, u32[]{:S(2)}) %collective-permute-start.15) | collective-permute-done | bytes 294944 | tf_op jit(solution)/shard_map/ppermute | solution.py:395
  62.1 27.0 %collective-permute-done.17 = bf16[3,96,768]{2,1,0:T(8,128)(2,1)S(1)} collective-permute-done((bf16[3,96,768]{2,1,0:T(8,128)(2,1)S(1)}, bf16[3,96,768]{2,1,0:T(8,128)(2,1)S(1)}, u32[]{:S(2)}, u32[]{:S(2)}) %collective-permute-start.17) | collective-permute-done | bytes 442400 | tf_op jit(solution)/shard_map/ppermute | solution.py:395
  105.6 9.1 %shard_map.271 = (bf16[384,768]{1,0:T(8,128)(2,1)}, bf16[384,768]{1,0:T(8,128)(2,1)}, bf16[384,768]{1,0:T(8,128)(2,1)}, bf16[3,6,256,128]{3,2,1,0:T(8,128)(2,1)}...) custom-call(bf16[384,768]{1,0:T(8,128)(2,1)} %bitcast.102, ...), custom_call_target="tpu_custom_call" | custom-call | flops 1811939328 | bytes 14680064 | tf_op jit(solution)/shard_map/pallas_call | solution.py:132
  114.8 6.4 %collective-permute-done.18.rest_3_ = bf16[2,3,96,768]{3,2,1,0:T(8,128)(2,1)} collective-permute-done((bf16[2,3,96,768]{3,2,1,0:T(8,128)(2,1)S(1)}, bf16[2,3,96,768]{3,2,1,0:T(8,128)(2,1)}, u32[]{:S(2)}, u32[]{:S(2)}) %collective-permute-start.18) | collective-permute-done | bytes 884768 | tf_op jit(solution)/shard_map/ppermute | solution.py:395
  123.2 13.7 %shard_map.272 = (f32[384,768]{1,0:T(8,128)}, bf16[4,384,768]{2,1,0:T(8,128)(2,1)}, bf16[4,384,768]{2,1,0:T(8,128)(2,1)}) custom-call(s32[8]{0:T(128)} %iota_xor_fusion.blocks.refs_0_, f32[384,768]{1,0:T(8,128)} %get-tuple-element.60.mixed, f32[2,768]{1,0:T(2,128)} %gain.7, f32[2,768]{1,0:T(2,128)} %shift.7, f32[4,1,768]{2,1,0:T(1,128)} %get-tuple-element.175.b_up, ...), custom_call_target="tpu_custom_call" | custom-call | flops 3623878656 | bytes 20971520 | tf_op jit(solution)/shard_map/pallas_call | solution.py:214
  137.7 9.1 %shard_map.273 = (bf16[384,768]{1,0:T(8,128)(2,1)}, bf16[384,768]{1,0:T(8,128)(2,1)}, bf16[384,768]{1,0:T(8,128)(2,1)}, bf16[3,6,256,128]{3,2,1,0:T(8,128)(2,1)}...) custom-call(f32[384,768]{1,0:T(8,128)} %get-tuple-element.61.refs_0_.refs_2_, f32[3,128,128]{2,1,0:T(8,128)} %broadcast_in_dim.33.refs_1_, ...), custom_call_target="tpu_custom_call" | custom-call | flops 1811939328 | bytes 14680064 | tf_op jit(solution)/shard_map/pallas_call | solution.py:132
  147.8 13.0 %shard_map.274 = (bf16[384,768]{1,0:T(8,128)(2,1)}, bf16[4,384,768]{2,1,0:T(8,128)(2,1)}, bf16[4,384,768]{2,1,0:T(8,128)(2,1)}) custom-call(s32[8]{0:T(128)} %iota_xor_fusion.blocks.refs_0_, f32[384,768]{1,0:T(8,128)} %get-tuple-element.62.mixed, f32[2,768]{1,0:T(2,128)} %gain.7, f32[2,768]{1,0:T(2,128)} %shift.7, f32[4,1,768]{2,1,0:T(1,128)} %get-tuple-element.174.b_up, ...), custom_call_target="tpu_custom_call" | custom-call | flops 3623878656 | bytes 20971520 | tf_op jit(solution)/shard_map/pallas_call | solution.py:214
  160.8 17.0 %shard_map.275 = (f32[384,768]{1,0:T(8,128)}, bf16[4,384,768]{2,1,0:T(8,128)(2,1)}, bf16[4,384,768]{2,1,0:T(8,128)(2,1)}, bf16[4,384,768]{2,1,0:T(8,128)(2,1)}, ...) custom-call(s32[8]{0:T(128)} %iota_xor_fusion.blocks.refs_0_, bf16[384,768]{1,0:T(8,128)(2,1)} %bitcast.113, ...), custom_call_target="tpu_custom_call" | custom-call | flops 7247757312 | bytes 31457280 | tf_op jit(solution)/shard_map/pallas_call | solution.py:287
  177.8 13.8 %shard_map.276 = (f32[384,768]{1,0:T(8,128)}, bf16[2,384,768]{2,1,0:T(8,128)(2,1)}, bf16[2,384,768]{2,1,0:T(8,128)(2,1)}, bf16[2,384,768]{2,1,0:T(8,128)(2,1)}, ...) custom-call(s32[8]{0:T(128)} %iota_xor_fusion.blocks.refs_0_, f32[384,768]{1,0:T(8,128)} %get-tuple-element.66.refs_1_, ...), custom_call_target="tpu_custom_call" | custom-call | flops 3623878656 | bytes 25165824 | tf_op jit(solution)/shard_map/pallas_call | solution.py:378
  191.9 17.2 %shard_map.277 = (f32[384,768]{1,0:T(8,128)}, bf16[4,384,768]{2,1,0:T(8,128)(2,1)}, bf16[4,384,768]{2,1,0:T(8,128)(2,1)}, bf16[4,384,768]{2,1,0:T(8,128)(2,1)}, ...) custom-call(s32[8]{0:T(128)} %iota_xor_fusion.blocks.refs_0_, ...), custom_call_target="tpu_custom_call" | custom-call | flops 7247757312 | bytes 31457280 | tf_op jit(solution)/shard_map/pallas_call | solution.py:287
  209.1 13.8 %shard_map.278 = (f32[384,768]{1,0:T(8,128)}, bf16[2,384,768]{2,1,0:T(8,128)(2,1)}, bf16[2,384,768]{2,1,0:T(8,128)(2,1)}, bf16[2,384,768]{2,1,0:T(8,128)(2,1)}, ...) custom-call(s32[8]{0:T(128)} %iota_xor_fusion.blocks.refs_0_, f32[384,768]{1,0:T(8,128)} %get-tuple-element.75.refs_1_, ...), custom_call_target="tpu_custom_call" | custom-call | flops 3623878656 | bytes 25165824 | tf_op jit(solution)/shard_map/pallas_call | solution.py:378
  229.3 39.6 %psum.7 = f32[19,768]{1,0:T(8,128)} all-reduce(f32[19,768]{1,0:T(8,128)} %concatenate.6), channel_id=1, replica_groups=mesh['dp'=8,'mp'=4] {'dp','mp'}, use_global_device_ids=true, to_apply=%region_0.1 | all-reduce | flops 14592 | bytes 116736 | tf_op jit(solution)/shard_map/psum | solution.py:557
  284.0 8.5 %collective-permute-done.32 = bf16[2,192,768]{2,1,0:T(8,128)(2,1)S(1)} collective-permute-done((bf16[2,192,768]{2,1,0:T(8,128)(2,1)S(1)}, bf16[2,192,768]{2,1,0:T(8,128)(2,1)S(1)}, u32[]{:S(2)}, u32[]{:S(2)}) %collective-permute-start.32) | collective-permute-done | bytes 589856 | tf_op jit(solution)/shard_map/ppermute | solution.py:395
  295.4 9.5 %collective-permute-done.26 = bf16[2,192,768]{2,1,0:T(8,128)(2,1)S(1)} collective-permute-done((bf16[2,192,768]{2,1,0:T(8,128)(2,1)S(1)}, bf16[2,192,768]{2,1,0:T(8,128)(2,1)S(1)}, u32[]{:S(2)}, u32[]{:S(2)}) %collective-permute-start.26) | collective-permute-done | bytes 589856 | tf_op jit(solution)/shard_map/ppermute | solution.py:395
  363.7 5.6 %collective-permute-done.41 = bf16[2,96,192]{2,1,0:T(8,128)(2,1)S(1)} collective-permute-done((bf16[2,96,192]{2,1,0:T(8,128)(2,1)S(1)}, bf16[2,96,192]{2,1,0:T(8,128)(2,1)S(1)}, u32[]{:S(2)}, u32[]{:S(2)}) %collective-permute-start.41) | collective-permute-done | bytes 73760 | tf_op jit(solution)/shard_map/ppermute | solution.py:395
  383.4 19.9 %collective-permute-done.56 = bf16[4,192,768]{2,1,0:T(8,128)(2,1)S(1)} collective-permute-done((bf16[4,192,768]{2,1,0:T(8,128)(2,1)S(1)}, bf16[4,192,768]{2,1,0:T(8,128)(2,1)S(1)}, u32[]{:S(2)}, u32[]{:S(2)}) %collective-permute-start.56) | collective-permute-done | bytes 1179680 | tf_op jit(solution)/shard_map/ppermute | solution.py:395
  405.5 19.6 %collective-permute-done.50 = bf16[4,192,768]{2,1,0:T(8,128)(2,1)S(1)} collective-permute-done((bf16[4,192,768]{2,1,0:T(8,128)(2,1)S(1)}, bf16[4,192,768]{2,1,0:T(8,128)(2,1)S(1)}, u32[]{:S(2)}, u32[]{:S(2)}) %collective-permute-start.50) | collective-permute-done | bytes 1179680 | tf_op jit(solution)/shard_map/ppermute | solution.py:395
  427.6 5.1 %collective-permute-done.62 = bf16[4,192,768]{2,1,0:T(8,128)(2,1)S(1)} collective-permute-done((bf16[4,192,768]{2,1,0:T(8,128)(2,1)S(1)}, bf16[4,192,768]{2,1,0:T(8,128)(2,1)S(1)}, u32[]{:S(2)}, u32[]{:S(2)}) %collective-permute-start.62) | collective-permute-done | bytes 1179680 | tf_op jit(solution)/shard_map/ppermute | solution.py:395
  434.2 11.1 %collective-permute-done.57 = bf16[4,96,768]{2,1,0:T(8,128)(2,1)S(1)} collective-permute-done((bf16[4,96,768]{2,1,0:T(8,128)(2,1)S(1)}, bf16[4,96,768]{2,1,0:T(8,128)(2,1)S(1)}, u32[]{:S(2)}, u32[]{:S(2)}) %collective-permute-start.57) | collective-permute-done | bytes 589856 | tf_op jit(solution)/shard_map/ppermute | solution.py:395
  463.8 7.5 %collective-permute-start.70 = (bf16[96,768]{1,0:T(8,128)(2,1)S(1)}, bf16[96,768]{1,0:T(8,128)(2,1)S(1)}, u32[]{:S(2)}, u32[]{:S(2)}) collective-permute-start(bf16[96,768]{1,0:T(8,128)(2,1)S(1)} %get-tuple-element.110), channel_id=1, source_target_pairs={{0,1},{1,0},{2,3},{3,2},{4,5},{5,4},{6,7},{7,6},{8,9},{9,8},{10,11... | collective-permute-start | bytes 442376 | tf_op jit(solution)/shard_map/ppermute | solution.py:395
  471.3 8.6 %collective-permute-done.53 = bf16[96,768]{1,0:T(8,128)(2,1)S(1)} collective-permute-done((bf16[96,768]{1,0:T(8,128)(2,1)S(1)}, bf16[96,768]{1,0:T(8,128)(2,1)S(1)}, u32[]{:S(2)}, u32[]{:S(2)}) %collective-permute-start.53) | collective-permute-done | bytes 147488 | tf_op jit(solution)/shard_map/ppermute | solution.py:395
  (261 shorter events, 174.0 us)
Async XLA Ops:
  6.9 38.7 %collective-permute-start.4 = (bf16[2,96,768]{2,1,0:T(8,128)(2,1)S(1)}, bf16[2,96,768]{2,1,0:T(8,128)(2,1)S(1)}, u32[]{:S(2)}, u32[]{:S(2)}) collective-permute-start(bf16[2,96,768]{2,1,0:T(8,128)(2,1)S(1)} %get-tuple-element.132), channel_id=1, source_target_pairs={{0,2},{1,3},{2,0},{3,1},{4,6},{5,7},{6,4},{7,5},{8,10},{9,11},{10,... | collective-permute-start | bytes 884744 | tf_op jit(solution)/shard_map/ppermute | solution.py:395
  6.9 38.7 %collective-permute-start.3 = (bf16[2,96,768]{2,1,0:T(8,128)(2,1)S(1)}, bf16[2,96,768]{2,1,0:T(8,128)(2,1)S(1)}, u32[]{:S(2)}, u32[]{:S(2)}) collective-permute-start(bf16[2,96,768]{2,1,0:T(8,128)(2,1)S(1)} %get-tuple-element.132), channel_id=1, source_target_pairs={{0,1},{1,0},{2,3},{3,2},{4,5},{5,4},{6,7},{7,6},{8,9},{9,8},{10,11... | collective-permute-start | bytes 884744 | tf_op jit(solution)/shard_map/ppermute | solution.py:395
  7.6 41.4 %collective-permute-start.16 = (bf16[2,96,768]{2,1,0:T(8,128)(2,1)S(1)}, bf16[2,96,768]{2,1,0:T(8,128)(2,1)S(1)}, u32[]{:S(2)}, u32[]{:S(2)}) collective-permute-start(bf16[2,96,768]{2,1,0:T(8,128)(2,1)S(1)} %get-tuple-element.131), channel_id=1, source_target_pairs={{0,3},{1,2},{2,1},{3,0},{4,7},{5,6},{6,5},{7,4},{8,11},{9,10},{10,... | collective-permute-start | bytes 884744 | tf_op jit(solution)/shard_map/ppermute | solution.py:395
  11.3 46.0 %collective-permute-start.15 = (bf16[2,96,768]{2,1,0:T(8,128)(2,1)S(1)}, bf16[2,96,768]{2,1,0:T(8,128)(2,1)S(1)}, u32[]{:S(2)}, u32[]{:S(2)}) collective-permute-start(bf16[2,96,768]{2,1,0:T(8,128)(2,1)S(1)} %get-tuple-element.131), channel_id=1, source_target_pairs={{0,2},{1,3},{2,0},{3,1},{4,6},{5,7},{6,4},{7,5},{8,10},{9,11},{10,... | collective-permute-start | bytes 884744 | tf_op jit(solution)/shard_map/ppermute | solution.py:395
  14.9 45.8 %collective-permute-start.14 = (bf16[2,96,768]{2,1,0:T(8,128)(2,1)S(1)}, bf16[2,96,768]{2,1,0:T(8,128)(2,1)S(1)}, u32[]{:S(2)}, u32[]{:S(2)}) collective-permute-start(bf16[2,96,768]{2,1,0:T(8,128)(2,1)S(1)} %get-tuple-element.131), channel_id=1, source_target_pairs={{0,1},{1,0},{2,3},{3,2},{4,5},{5,4},{6,7},{7,6},{8,9},{9,8},{10,11... | collective-permute-start | bytes 884744 | tf_op jit(solution)/shard_map/ppermute | solution.py:395
  57.5 42.2 %collective-permute-start.7 = (bf16[2,3,96,768]{3,2,1,0:T(8,128)(2,1)S(1)}, bf16[2,3,96,768]{3,2,1,0:T(8,128)(2,1)}, u32[]{:S(2)}, u32[]{:S(2)}) collective-permute-start(bf16[2,3,96,768]{3,2,1,0:T(8,128)(2,1)S(1)} %pad_maximum_fusion.rest_2_), channel_id=1, source_target_pairs={{0,16},{4,20},{8,24},{12,28},{16,0},{20,4},{24,8},{28,12},{1,17},{... | collective-permute-start | bytes 2654216 | tf_op jit(solution)/shard_map/ppermute | solution.py:395
  59.1 42.0 %collective-permute-start.9 = (bf16[2,3,96,768]{3,2,1,0:T(8,128)(2,1)S(1)}, bf16[2,3,96,768]{3,2,1,0:T(8,128)(2,1)S(1)}, u32[]{:S(2)}, u32[]{:S(2)}) collective-permute-start(bf16[2,3,96,768]{3,2,1,0:T(8,128)(2,1)S(1)} %pad_maximum_fusion.1.rest_4_), channel_id=1, source_target_pairs={{0,8},{4,12},{8,0},{12,4},{16,24},{20,28},{24,16},{28,20},{1,9},{5... | collective-permute-start | bytes 2654216 | tf_op jit(solution)/shard_map/ppermute | solution.py:395
  60.8 28.3 %collective-permute-start.17 = (bf16[3,96,768]{2,1,0:T(8,128)(2,1)S(1)}, bf16[3,96,768]{2,1,0:T(8,128)(2,1)S(1)}, u32[]{:S(2)}, u32[]{:S(2)}) collective-permute-start(bf16[3,96,768]{2,1,0:T(8,128)(2,1)S(1)} %get-tuple-element.136), channel_id=1, source_target_pairs={{0,8},{4,12},{8,0},{12,4},{16,24},{20,28},{24,16},{28,20},{1,9},{5... | collective-permute-start | bytes 1327112 | tf_op jit(solution)/shard_map/ppermute | solution.py:395
  61.5 33.1 %collective-permute-start.19 = (bf16[3,96,768]{2,1,0:T(8,128)(2,1)S(1)}, bf16[3,96,768]{2,1,0:T(8,128)(2,1)S(1)}, u32[]{:S(2)}, u32[]{:S(2)}) collective-permute-start(bf16[3,96,768]{2,1,0:T(8,128)(2,1)S(1)} %get-tuple-element.134), channel_id=1, source_target_pairs={{0,16},{4,20},{8,24},{12,28},{16,0},{20,4},{24,8},{28,12},{1,17},{... | collective-permute-start | bytes 1327112 | tf_op jit(solution)/shard_map/ppermute | solution.py:395
  62.1 40.2 %collective-permute-start.10 = (bf16[2,3,96,768]{3,2,1,0:T(8,128)(2,1)S(1)}, bf16[2,3,96,768]{3,2,1,0:T(8,128)(2,1)}, u32[]{:S(2)}, u32[]{:S(2)}) collective-permute-start(bf16[2,3,96,768]{3,2,1,0:T(8,128)(2,1)S(1)} %pad_maximum_fusion.rest_2_), channel_id=1, source_target_pairs={{0,4},{4,0},{8,12},{12,8},{16,20},{20,16},{24,28},{28,24},{1,5},{5... | collective-permute-start | bytes 2654216 | tf_op jit(solution)/shard_map/ppermute | solution.py:395
  114.8 32.1 %collective-permute-start.21 = (bf16[2,3,96,768]{3,2,1,0:T(8,128)(2,1)S(1)}, bf16[2,3,96,768]{3,2,1,0:T(8,128)(2,1)S(1)}, u32[]{:S(2)}, u32[]{:S(2)}) collective-permute-start(bf16[2,3,96,768]{3,2,1,0:T(8,128)(2,1)S(1)} %pad_maximum_fusion.2.rest_2_), channel_id=1, source_target_pairs={{0,4},{4,0},{8,12},{12,8},{16,20},{20,16},{24,28},{28,24},{1,5},{5... | collective-permute-start | bytes 2654216 | tf_op jit(solution)/shard_map/ppermute | solution.py:395
  191.5 83.1 %collective-permute-start.31 = (bf16[2,384,768]{2,1,0:T(8,128)(2,1)}, bf16[2,384,768]{2,1,0:T(8,128)(2,1)}, u32[]{:S(2)}, u32[]{:S(2)}) collective-permute-start(bf16[2,384,768]{2,1,0:T(8,128)(2,1)} %get-tuple-element.92), channel_id=1, source_target_pairs={{0,4},{4,0},{8,12},{12,8},{16,20},{20,16},{24,28},{28,24},{1,5},{5... | collective-permute-start | bytes 3538952 | tf_op jit(solution)/shard_map/ppermute | solution.py:395
  223.0 52.9 %collective-permute-start.25 = (bf16[2,384,768]{2,1,0:T(8,128)(2,1)}, bf16[2,384,768]{2,1,0:T(8,128)(2,1)}, u32[]{:S(2)}, u32[]{:S(2)}) collective-permute-start(bf16[2,384,768]{2,1,0:T(8,128)(2,1)} %get-tuple-element.90), channel_id=1, source_target_pairs={{0,4},{4,0},{8,12},{12,8},{16,20},{20,16},{24,28},{28,24},{1,5},{5... | collective-permute-start | bytes 3538952 | tf_op jit(solution)/shard_map/ppermute | solution.py:395
  223.3 56.2 %collective-permute-start.43 = (bf16[2,384,768]{2,1,0:T(8,128)(2,1)}, bf16[2,384,768]{2,1,0:T(8,128)(2,1)}, u32[]{:S(2)}, u32[]{:S(2)}) collective-permute-start(bf16[2,384,768]{2,1,0:T(8,128)(2,1)} %get-tuple-element.96), channel_id=1, source_target_pairs={{0,4},{4,0},{8,12},{12,8},{16,20},{20,16},{24,28},{28,24},{1,5},{5... | collective-permute-start | bytes 3538952 | tf_op jit(solution)/shard_map/ppermute | solution.py:395
  223.6 57.4 %collective-permute-start.37 = (bf16[2,384,768]{2,1,0:T(8,128)(2,1)}, bf16[2,384,768]{2,1,0:T(8,128)(2,1)}, u32[]{:S(2)}, u32[]{:S(2)}) collective-permute-start(bf16[2,384,768]{2,1,0:T(8,128)(2,1)} %get-tuple-element.94), channel_id=1, source_target_pairs={{0,4},{4,0},{8,12},{12,8},{16,20},{20,16},{24,28},{28,24},{1,5},{5... | collective-permute-start | bytes 3538952 | tf_op jit(solution)/shard_map/ppermute | solution.py:395
  223.8 150.2 %collective-permute-start.55 = (bf16[4,384,768]{2,1,0:T(8,128)(2,1)}, bf16[4,384,768]{2,1,0:T(8,128)(2,1)S(1)}, u32[]{:S(2)}, u32[]{:S(2)}) collective-permute-start(bf16[4,384,768]{2,1,0:T(8,128)(2,1)} %get-tuple-element.100), channel_id=1, source_target_pairs={{0,4},{4,0},{8,12},{12,8},{16,20},{20,16},{24,28},{28,24},{1,5},{5... | collective-permute-start | bytes 7077896 | tf_op jit(solution)/shard_map/ppermute | solution.py:395
  274.6 101.8 %collective-permute-start.49 = (bf16[4,384,768]{2,1,0:T(8,128)(2,1)}, bf16[4,384,768]{2,1,0:T(8,128)(2,1)S(1)}, u32[]{:S(2)}, u32[]{:S(2)}) collective-permute-start(bf16[4,384,768]{2,1,0:T(8,128)(2,1)} %get-tuple-element.98), channel_id=1, source_target_pairs={{0,4},{4,0},{8,12},{12,8},{16,20},{20,16},{24,28},{28,24},{1,5},{5... | collective-permute-start | bytes 7077896 | tf_op jit(solution)/shard_map/ppermute | solution.py:395
  338.0 40.1 %collective-permute-start.67 = (bf16[4,384,768]{2,1,0:T(8,128)(2,1)S(1)}, bf16[4,384,768]{2,1,0:T(8,128)(2,1)S(1)}, u32[]{:S(2)}, u32[]{:S(2)}) collective-permute-start(bf16[4,384,768]{2,1,0:T(8,128)(2,1)S(1)} %copy-done.20), channel_id=1, source_target_pairs={{0,4},{4,0},{8,12},{12,8},{16,20},{20,16},{24,28},{28,24},{1,5},{5... | collective-permute-start | bytes 7077896 | tf_op jit(solution)/shard_map/ppermute | solution.py:395
  349.2 30.5 %collective-permute-start.61 = (bf16[4,384,768]{2,1,0:T(8,128)(2,1)S(1)}, bf16[4,384,768]{2,1,0:T(8,128)(2,1)S(1)}, u32[]{:S(2)}, u32[]{:S(2)}) collective-permute-start(bf16[4,384,768]{2,1,0:T(8,128)(2,1)S(1)} %copy-done.21), channel_id=1, source_target_pairs={{0,4},{4,0},{8,12},{12,8},{16,20},{20,16},{24,28},{28,24},{1,5},{5... | collective-permute-start | bytes 7077896 | tf_op jit(solution)/shard_map/ppermute | solution.py:395
  374.3 29.0 %collective-permute-start.56 = (bf16[4,192,768]{2,1,0:T(8,128)(2,1)S(1)}, bf16[4,192,768]{2,1,0:T(8,128)(2,1)S(1)}, u32[]{:S(2)}, u32[]{:S(2)}) collective-permute-start(bf16[4,192,768]{2,1,0:T(8,128)(2,1)S(1)} %add_convert_fusion.2), channel_id=1, source_target_pairs={{0,8},{4,12},{8,0},{12,4},{16,24},{20,28},{24,16},{28,20},{1,9},{5... | collective-permute-start | bytes 3538952 | tf_op jit(solution)/shard_map/ppermute | solution.py:395
  376.7 48.4 %collective-permute-start.50 = (bf16[4,192,768]{2,1,0:T(8,128)(2,1)S(1)}, bf16[4,192,768]{2,1,0:T(8,128)(2,1)S(1)}, u32[]{:S(2)}, u32[]{:S(2)}) collective-permute-start(bf16[4,192,768]{2,1,0:T(8,128)(2,1)S(1)} %add_convert_fusion.3), channel_id=1, source_target_pairs={{0,8},{4,12},{8,0},{12,4},{16,24},{20,28},{24,16},{28,20},{1,9},{5... | collective-permute-start | bytes 3538952 | tf_op jit(solution)/shard_map/ppermute | solution.py:395
  378.4 47.8 %collective-permute-start.68 = (bf16[4,192,768]{2,1,0:T(8,128)(2,1)S(1)}, bf16[4,192,768]{2,1,0:T(8,128)(2,1)S(1)}, u32[]{:S(2)}, u32[]{:S(2)}) collective-permute-start(bf16[4,192,768]{2,1,0:T(8,128)(2,1)S(1)} %add_convert_fusion), channel_id=1, source_target_pairs={{0,16},{4,20},{8,24},{12,28},{16,0},{20,4},{24,8},{28,12},{1,17},{... | collective-permute-start | bytes 3538952 | tf_op jit(solution)/shard_map/ppermute | solution.py:395
  380.0 52.6 %collective-permute-start.62 = (bf16[4,192,768]{2,1,0:T(8,128)(2,1)S(1)}, bf16[4,192,768]{2,1,0:T(8,128)(2,1)S(1)}, u32[]{:S(2)}, u32[]{:S(2)}) collective-permute-start(bf16[4,192,768]{2,1,0:T(8,128)(2,1)S(1)} %add_convert_fusion.1), channel_id=1, source_target_pairs={{0,16},{4,20},{8,24},{12,28},{16,0},{20,4},{24,8},{28,12},{1,17},{... | collective-permute-start | bytes 3538952 | tf_op jit(solution)/shard_map/ppermute | solution.py:395
  403.5 41.7 %collective-permute-start.57 = (bf16[4,96,768]{2,1,0:T(8,128)(2,1)S(1)}, bf16[4,96,768]{2,1,0:T(8,128)(2,1)S(1)}, u32[]{:S(2)}, u32[]{:S(2)}) collective-permute-start(bf16[4,96,768]{2,1,0:T(8,128)(2,1)S(1)} %add_convert_fusion.6), channel_id=1, source_target_pairs={{0,16},{4,20},{8,24},{12,28},{16,0},{20,4},{24,8},{28,12},{1,17},{... | collective-permute-start | bytes 1769480 | tf_op jit(solution)/shard_map/ppermute | solution.py:395
  (73 other events, 1072.2 us)

commit v2 on v1

v2 whole, which is shorter than its diff:
```python
import functools

import jax
import jax.numpy as jnp
from jax import lax
from jax.experimental import pallas as pl
from jax.experimental.pallas import tpu as pltpu
from jax.sharding import PartitionSpec as P

HEADS = 12
TEXT = 112
F32 = jnp.float32
BF16 = jnp.bfloat16
VMEM_BYTES = 56 * 2**20


def dot(a, b, a_dim, b_dim):
    return lax.dot_general(a, b, (((a_dim,), (b_dim,)), ((), ())), preferred_element_type=F32)


def whiten(rows):
    centered = rows - jnp.mean(rows, axis=-1, keepdims=True)
    spread = jnp.mean(centered * centered, axis=-1, keepdims=True)
    inverse = lax.rsqrt(spread + 1e-05)
    return centered * inverse, inverse


def whiten_back(white, inverse, gain, grad):
    scaled = grad * gain
    first = jnp.mean(scaled, axis=-1, keepdims=True)
    second = jnp.mean(scaled * white, axis=-1, keepdims=True)
    return inverse * (scaled - first - white * second)


def column_sum(rows):
    return jnp.sum(rows, axis=0, keepdims=True)


def gelu_and_slope(values):
    size = jnp.abs(values)
    t = 1.0 / (1.0 + (0.3275911 * 0.7071067811865476) * size)
    bell = jnp.exp(-0.5 * values * values)
    poly = 0.5 * 1.061405429
    poly = poly * t + 0.5 * -1.453152027
    poly = poly * t + 0.5 * 1.421413741
    poly = poly * t + 0.5 * -0.284496736
    poly = poly * t + 0.5 * 0.254829592
    tail = poly * t * bell
    phi = jnp.where(values >= 0.0, 1.0 - tail, tail)
    return values * phi, phi + values * bell * 0.3989422804014327


def split_heads(pair):
    lane = lax.broadcasted_iota(jnp.int32, pair.shape, 1)
    first = lane < pair.shape[1] // 2
    zero = jnp.zeros_like(pair)
    return jnp.concatenate([jnp.where(first, pair, zero), jnp.where(first, zero, pair)], axis=0)


def join_heads(both):
    slots = both.shape[0] // 2
    lane = lax.broadcasted_iota(jnp.int32, (slots, both.shape[1]), 1)
    return jnp.where(lane < both.shape[1] // 2, both[:slots], both[slots:])


def start_copies(sources, targets, sems):
    copies = [
        pltpu.make_async_copy(source, target, sems.at[at])
        for at, (source, target) in enumerate(zip(sources, targets))
    ]
    for copy in copies:
        copy.start()
    return copies


def attend_kernel(layer, crossed, resid, mask, gain, shift, gate, wq, wk, wv, wo,
                  q_out, k_out, v_out, p_out, c_out, mixed, branch_out, held, sems):
    pages, slots = mask.shape[0], mask.shape[1]
    width = resid.shape[1]
    pairs = HEADS // 2
    pair_width = width // pairs
    scale = 1.0 / (width // HEADS) ** 0.5
    copies = start_copies(
        [w.at[layer] for w in (wq, wk, wv, wo)], [held.at[at] for at in range(4)], sems
    )
    white, _ = whiten(resid[...].astype(F32))
    normed = (white * gain[layer:layer + 1] + shift[layer:layer + 1]).astype(BF16)
    copies[0].wait()
    q_out[...] = (dot(normed, held[0], 1, 0).astype(BF16).astype(F32) * scale).astype(BF16)
    copies[1].wait()
    k_out[...] = dot(normed, held[1], 1, 0).astype(BF16)
    copies[2].wait()
    v_out[...] = dot(normed, held[2], 1, 0).astype(BF16)

    for page in range(pages):
        rows = slice(page * slots, (page + 1) * slots)
        bias = mask[page]
        for pair in range(pairs):
            cols = slice(pair * pair_width, (pair + 1) * pair_width)
            scores = dot(split_heads(k_out[rows, cols]), q_out[rows, cols], 1, 1)
            scores = scores.reshape(2, slots, slots) + bias[None]
            top = jnp.max(scores, axis=1, keepdims=True)
            raised = jnp.exp(scores - top)
            probs = raised * (1.0 / jnp.sum(raised, axis=1, keepdims=True))
            probs = probs.reshape(2 * slots, slots).astype(BF16)
            p_out[page, pair] = probs
            c_out[rows, cols] = dot(probs, split_heads(v_out[rows, cols]), 0, 0).astype(BF16)
    copies[3].wait()
    branch = dot(c_out[...], held[3], 1, 0)
    if crossed:
        branch_out[...] = branch.astype(BF16)
        branch = branch * jax.nn.sigmoid(gate[...])
    mixed[...] = resid[...].astype(F32) + branch


def attend(layer, crossed, resid, mask, gain, shift, gate, weights, ties):
    rows, width = resid.shape
    pages, slots = mask.shape[:2]
    low = jax.ShapeDtypeStruct((rows, width), BF16)
    vmem = pl.BlockSpec(memory_space=pltpu.VMEM)
    outs = [low, low, low, jax.ShapeDtypeStruct((pages, HEADS // 2, 2 * slots, slots), BF16), low,
            jax.ShapeDtypeStruct((rows, width), F32)]
    if crossed:
        outs.append(low)

    def body(*refs):
        ins, rest = refs[:9], list(refs[9 + len(ties):])
        if not crossed:
            rest.insert(6, None)
        attend_kernel(layer, crossed, *ins, *rest)

    return pl.pallas_call(
        body,
        out_shape=outs,
        in_specs=[vmem] * 5 + [pl.BlockSpec(memory_space=pl.ANY)] * (4 + len(ties)),
        out_specs=[vmem] * len(outs),
        scratch_shapes=[pltpu.VMEM((4, width, width), BF16), pltpu.SemaphoreType.DMA((4,))],
        compiler_params=pltpu.CompilerParams(vmem_limit_bytes=VMEM_BYTES),
        cost_estimate=pl.CostEstimate(flops=8 * rows * width * width, bytes_accessed=14 * 2**20, transcendentals=0),
    )(resid, mask, gain, shift, gate, *weights, *ties)


class Pieces:
    def __init__(self, arrays, plan, blocks, piece_rows, tails):
        self.tails = tails
        self.arrays, self.plan, self.blocks, self.piece_rows = arrays, plan, blocks, piece_rows

    def copies(self, refs, held, blocks, sems, shard):
        made = []
        for at, (array, index, kind, owner, place) in enumerate(self.plan):
            if owner != shard:
                continue
            if place is None:
                target = held[kind].at[shard]
            elif isinstance(place, slice):
                target = held[kind].at[shard, place]
            else:
                start = pl.multiple_of(blocks[place] * self.piece_rows, self.piece_rows)
                target = held[kind].at[shard, pl.ds(start, self.piece_rows)]
            source = index(refs[array], blocks) if callable(index) else refs[array].at[index]
            made.append(pltpu.make_async_copy(source, target, sems.at[at]))
        return made

    def tail_specs(self, width):
        return [pl.BlockSpec((16, width), lambda step, last=tail.shape[0] // 16 - 1: (last, 0)) for tail in self.tails]

    def start_and_wait(self, refs, held, blocks, sems, shards):
        step = pl.program_id(0)

        @pl.when(step == 0)
        def _():
            for shard in range(shards):
                for copy in self.copies(refs, held, blocks, sems, shard):
                    copy.start()

        def wait():
            for shard in range(shards):
                @pl.when(step == shard)
                def _():
                    for copy in self.copies(refs, held, blocks, sems, shard):
                        copy.wait()
        return wait


def feed_kernel(layer, pieces, ties, blocks, mixed, gain, shift, b_down, *rest):
    count = len(pieces.arrays)
    tails, rest = rest[:len(pieces.tails)], rest[len(pieces.tails):]
    refs, rest = rest[:count], rest[count + ties:]
    result, active_out, slope_out, up, down, low, total, bias, sems = rest
    shards, width = up.shape[0], up.shape[2]
    step = pl.program_id(0)
    wait = pieces.start_and_wait(refs, (up, down), blocks, sems, shards)

    @pl.when(step == 0)
    def _():
        white, _ = whiten(mixed[...])
        low[...] = (white * gain[layer:layer + 1] + shift[layer:layer + 1]).astype(BF16)
        total[...] = mixed[...] + b_down[layer:layer + 1]
        for at, tail in enumerate(tails):
            bias[at] = column_sum(tail[...].astype(F32))

    wait()
    parts = 3
    part = width // parts
    for at in range(parts):
        cols = slice(at * part, (at + 1) * part)
        upper = dot(low[...], up[step, :, cols], 1, 0) + bias[step, :, cols]
        active, slope = gelu_and_slope(upper)
        active = active.astype(BF16)
        active_out[0, :, cols] = active
        slope_out[0, :, cols] = slope.astype(BF16)
        total[...] += dot(active, down[step, cols, :], 1, 0)

    @pl.when(step == shards - 1)
    def _():
        result[...] = total[...].astype(result.dtype)


def feed(layer, mixed, gain, shift, b_down, pieces, out_type, ties):
    rows, width = mixed.shape
    shards = len(pieces.tails)
    whole = lambda shape: pl.BlockSpec(shape, lambda step: (0,) * len(shape))
    each = lambda shape: pl.BlockSpec((1,) + shape, lambda step: (step,) + (0,) * len(shape))
    return pl.pallas_call(
        functools.partial(feed_kernel, layer, pieces, len(ties)),
        grid=(shards,),
        out_shape=[jax.ShapeDtypeStruct((rows, width), out_type)]
        + [jax.ShapeDtypeStruct((shards, rows, width), BF16)] * 2,
        in_specs=[pl.BlockSpec(memory_space=pltpu.SMEM), whole((rows, width)), whole(gain.shape), whole(shift.shape),
                  whole(b_down.shape)] + pieces.tail_specs(width)
        + [pl.BlockSpec(memory_space=pl.ANY)] * (len(pieces.arrays) + len(ties)),
        out_specs=[whole((rows, width)), each((rows, width)), each((rows, width))],
        scratch_shapes=[pltpu.VMEM((shards, width, width), BF16), pltpu.VMEM((shards, width, width), BF16),
                        pltpu.VMEM((rows, width), BF16), pltpu.VMEM((rows, width), F32),
                        pltpu.VMEM((shards, 1, width), F32), pltpu.SemaphoreType.DMA((len(pieces.plan),))],
        compiler_params=pltpu.CompilerParams(vmem_limit_bytes=VMEM_BYTES),
        cost_estimate=pl.CostEstimate(flops=16 * rows * width * width, bytes_accessed=20 * 2**20, transcendentals=0),
    )(pieces.blocks, mixed, gain, shift, b_down, *pieces.tails, *pieces.arrays, *ties)


ROWS_FIRST = ((0, 4, 2, 6, 1, 5, 3, 7), (0, 2, 4, 6, 1, 3, 5, 7))
PART_ORDERS = (0, 1, 0)
PART_STAGES = ("xyvu", "yuxv", "uxyv")
SHARD_ORDER = (0, 2, 1, 3)
LINKS = {"c": ("dp", 1), "x": ("dp", 2), "y": ("dp", 4), "u": ("mp", 1), "v": ("mp", 2), "w": ("mp", 3)}


def turn_rows(held, turned, blocks, order):
    if order is None:
        turned[...] = held[...]
        return
    size = held.shape[0] // len(order)
    for at, place in enumerate(order):
        start = pl.multiple_of(blocks[place] * size, size)
        turned[at * size:(at + 1) * size] = held[pl.ds(start, size)]


def put_blocks(made, keep, keep_at, send, send_at):
    rows = made.shape[0] // 8
    for half, (out, place) in enumerate(((keep, keep_at), (send, send_at))):
        for first in range(2):
            for second in range(2):
                at = (4 * half + 2 * first + second) * rows
                out[place(first, second)] = made[at:at + rows]


def feed_back_kernel(layer, pieces, joint, ties, blocks, grad_out, mixed, gain, shift, active, slope, *rest):
    count = len(pieces.arrays)
    refs, rest = rest[:count], rest[count + ties:]
    grads_count = 1 if joint else 4
    grad_mixed, sums, up_sums, *grads = rest[:3 + grads_count]
    up, down, low, low_turned, normed_turned, held, total, sems, *leaving = rest[3 + grads_count:]
    shards, width = up.shape[0], up.shape[2]
    part = width // 3
    step = pl.program_id(0)
    wait = pieces.start_and_wait(refs, (up, down), blocks, sems, shards)

    def put(kind, turned, right):
        if joint:
            grads[0][0, kind] = dot(turned[0], right, 1, 0).astype(BF16)
            return
        for at in range(3):
            made = dot(turned[PART_ORDERS[at]], right[:, at * part:(at + 1) * part], 1, 0).astype(BF16)
            place = ((lambda first, second: (first, second, 0, 0, kind)), (lambda first, second: (first, 0, second, 0, kind)),
                     (lambda first, second: (0, first, second, 0, kind)))[at]
            put_blocks(made, grads[at], place, leaving[0], lambda first, second: (step % 2, at, first, second, kind))

    def leave(step, at):
        place = ((at, slice(None), slice(None), step % 2, step // 2), (at, slice(None), step // 2, slice(None), step % 2),
                 (at, step // 2, slice(None), slice(None), step % 2))[at]
        return pltpu.make_async_copy(leaving[0].at[step % 2, at], grads[3].at[place], leaving[1].at[step % 2, at])

    if not joint:
        @pl.when(step >= 2)
        def _():
            for at in range(3):
                leave(step - 2, at).wait()

    @pl.when(step == 0)
    def _():
        rows = grad_out[...].astype(F32)
        low[...] = rows.astype(BF16)
        sums[...] = jnp.zeros_like(sums)
        sums[0:1] = column_sum(rows)
        white, _ = whiten(mixed[...])
        normed = (white * gain[layer:layer + 1] + shift[layer:layer + 1]).astype(BF16)
        for value, turned in ((low[...], low_turned), (normed, normed_turned)):
            held[...] = value.T
            for at in range(turned.shape[0]):
                turn_rows(held, turned.at[at], blocks, None if joint else ROWS_FIRST[at])
        total[...] = jnp.zeros_like(total)

    wait()
    put(1, low_turned, active[0])
    upper = dot(low[...], down[step], 1, 1) * slope[0].astype(F32)
    up_sums[0] = column_sum(upper)
    upper_low = upper.astype(BF16)
    put(0, normed_turned, upper_low)
    if not joint:
        for at in range(3):
            leave(step, at).start()
    total[...] += dot(upper_low, up[step], 1, 1)

    @pl.when(step == shards - 1)
    def _():
        white, inverse = whiten(mixed[...])
        grad = total[...]
        sums[1:2] = column_sum(grad * white)
        sums[2:3] = column_sum(grad)
        grad_mixed[...] = grad_out[...].astype(F32) + whiten_back(white, inverse, gain[layer:layer + 1], grad)
        if not joint:
            for before in (1, 0):
                for at in range(3):
                    leave(step - before, at).wait()


def feed_back(layer, grad_out, mixed, gain, shift, active, slope, pieces, joint, ties):
    rows, width = mixed.shape
    shards = active.shape[0]
    whole = lambda shape: pl.BlockSpec(shape, lambda step: (0,) * len(shape))
    each = lambda shape: pl.BlockSpec((1,) + shape, lambda step: (step,) + (0,) * len(shape))
    if joint:
        grads, specs = [jax.ShapeDtypeStruct((shards, 2, width, width), BF16)], [each((2, width, width))]
        leaving = []
    else:
        tile = (width // 8, width // 3)
        grads = [jax.ShapeDtypeStruct((2,) * 5 + tile, BF16)] * 3 + [jax.ShapeDtypeStruct((3,) + (2,) * 5 + tile, BF16)]
        leaving = [pltpu.VMEM((2, 3, 2, 2, 2) + tile, BF16), pltpu.SemaphoreType.DMA((2, 3))]
        specs = [
            pl.BlockSpec((2, 2, 1, 1, 2) + tile, lambda step: (0, 0, step % 2, step // 2, 0, 0, 0)),
            pl.BlockSpec((2, 1, 2, 1, 2) + tile, lambda step: (0, step // 2, 0, step % 2, 0, 0, 0)),
            pl.BlockSpec((1, 2, 2, 1, 2) + tile, lambda step: (step // 2, 0, 0, step % 2, 0, 0, 0)),
            pl.BlockSpec(memory_space=pl.ANY),
        ]
    turned = pltpu.VMEM((1 if joint else 2, width, rows), BF16)
    return pl.pallas_call(
        functools.partial(feed_back_kernel, layer, pieces, joint, len(ties)),
        grid=(shards,),
        out_shape=[jax.ShapeDtypeStruct((rows, width), F32), jax.ShapeDtypeStruct((8, width), F32),
                   jax.ShapeDtypeStruct((shards, 1, width), F32)] + grads,
        in_specs=[pl.BlockSpec(memory_space=pltpu.SMEM), whole((rows, width)), whole((rows, width)), whole(gain.shape),
                  whole(shift.shape), each((rows, width)), each((rows, width))]
        + [pl.BlockSpec(memory_space=pl.ANY)] * (len(pieces.arrays) + len(ties)),
        out_specs=[whole((rows, width)), whole((8, width)), each((1, width))] + specs,
        scratch_shapes=[pltpu.VMEM((shards, width, width), BF16), pltpu.VMEM((shards, width, width), BF16),
                        pltpu.VMEM((rows, width), BF16), turned, turned, pltpu.VMEM((width, rows), BF16),
                        pltpu.VMEM((rows, width), F32), pltpu.SemaphoreType.DMA((len(pieces.plan),))] + leaving,
        compiler_params=pltpu.CompilerParams(vmem_limit_bytes=VMEM_BYTES),
        cost_estimate=pl.CostEstimate(flops=32 * rows * width * width, bytes_accessed=30 * 2**20, transcendentals=0),
    )(pieces.blocks, grad_out, mixed, gain, shift, active, slope, *pieces.arrays, *ties)


def attend_back_kernel(layer, crossed, joint, blocks, grad_mixed, resid, gain, shift, gate, q, k, v, p, context, branch,
                       wq, wk, wv, wo, grad_resid, sums, grads,
                       held, turning, turned, gc, gq, gk, gv, sems):
    pages, slots = p.shape[0], p.shape[3]
    width = resid.shape[1]
    pairs = HEADS // 2
    pair_width = width // pairs
    scale = 1.0 / (width // HEADS) ** 0.5
    copies = start_copies(
        [w.at[layer] for w in (wo, wq, wk, wv)], [held.at[at] for at in range(4)], sems
    )
    sums[...] = jnp.zeros_like(sums)

    def put(at, right):
        made = dot(turned[...], right, 1, 0).astype(BF16)
        if joint:
            grads[0][at] = made
            return
        tile = width // 3
        for col in range(3):
            put_blocks(made[:, col * tile:(col + 1) * tile], grads[at // 2], lambda first, second: (first, second, at % 2, col),
                       grads[2], lambda first, second: (at // 2, first, second, at % 2, col))

    def turn(rows, order):
        turning[...] = rows.T
        turn_rows(turning, turned, blocks, None if joint else ROWS_FIRST[order])

    grad = grad_mixed[...]
    if crossed:
        opened = jax.nn.sigmoid(gate[...])
        sums[2:3] = column_sum(grad * branch[...].astype(F32)) * (opened * (1.0 - opened))
        low = (grad * opened).astype(BF16)
    else:
        low = grad.astype(BF16)
    turn(context[...], 1)
    put(3, low)
    copies[0].wait()
    gc[...] = dot(low, held[0], 1, 1).astype(BF16)

    for page in range(pages):
        rows = slice(page * slots, (page + 1) * slots)
        for pair in range(pairs):
            cols = slice(pair * pair_width, (pair + 1) * pair_width)
            probs_low = p[page, pair]
            probs = probs_low.astype(F32).reshape(2, slots, slots)
            grad_probs = dot(split_heads(v[rows, cols]), gc[rows, cols], 1, 1).reshape(2, slots, slots)
            delta = jnp.sum(probs * grad_probs, axis=1, keepdims=True)
            grad_scores = (probs * (grad_probs - delta)).astype(BF16).reshape(2 * slots, slots)
            gq[rows, cols] = (dot(grad_scores, split_heads(k[rows, cols]), 0, 0) * scale).astype(BF16)
            gk[rows, cols] = join_heads(dot(grad_scores, q[rows, cols], 1, 0)).astype(BF16)
            gv[rows, cols] = join_heads(dot(probs_low, gc[rows, cols], 1, 0)).astype(BF16)

    white, inverse = whiten(resid[...].astype(F32))
    normed = (white * gain[layer:layer + 1] + shift[layer:layer + 1]).astype(BF16)
    turn(normed, 1)
    put(2, gv[...])
    if not joint:
        turn_rows(turning, turned, blocks, ROWS_FIRST[0])
    put(0, gq[...])
    put(1, gk[...])
    for copy in copies[1:]:
        copy.wait()
    total = dot(gq[...], held[1], 1, 1) + dot(gk[...], held[2], 1, 1) + dot(gv[...], held[3], 1, 1)
    sums[0:1] = column_sum(total * white)
    sums[1:2] = column_sum(total)
    grad_resid[...] = grad + whiten_back(white, inverse, gain[layer:layer + 1], total)


def attend_back(layer, crossed, grad_mixed, resid, gain, shift, gate, kept, weights, blocks, joint, ties):
    rows, width = resid.shape
    vmem = pl.BlockSpec(memory_space=pltpu.VMEM)
    kept = list(kept)
    given = 6 + len(kept) + 4
    if joint:
        grads = [jax.ShapeDtypeStruct((4, width, width), BF16)]
    else:
        shape = (2, 2, 2, 3, width // 8, width // 3)
        grads = [jax.ShapeDtypeStruct(shape, BF16)] * 2 + [jax.ShapeDtypeStruct((2,) + shape, BF16)]

    def body(*refs):
        ins, rest = list(refs[:given]), refs[given + len(ties):]
        if not crossed:
            ins.insert(11, None)
        attend_back_kernel(layer, crossed, joint, *ins, *rest[:2], rest[2:2 + len(grads)], *rest[2 + len(grads):])

    low = pltpu.VMEM((rows, width), BF16)
    return pl.pallas_call(
        body,
        out_shape=[jax.ShapeDtypeStruct((rows, width), F32), jax.ShapeDtypeStruct((8, width), F32)] + grads,
        in_specs=[pl.BlockSpec(memory_space=pltpu.SMEM)] + [vmem] * (5 + len(kept))
        + [pl.BlockSpec(memory_space=pl.ANY)] * (4 + len(ties)),
        out_specs=[vmem] * (2 + len(grads)),
        scratch_shapes=[pltpu.VMEM((4, width, width), BF16), pltpu.VMEM((width, rows), BF16),
                        pltpu.VMEM((width, rows), BF16), low, low, low, low, pltpu.SemaphoreType.DMA((4,))],
        compiler_params=pltpu.CompilerParams(vmem_limit_bytes=VMEM_BYTES),
        cost_estimate=pl.CostEstimate(flops=16 * rows * width * width, bytes_accessed=24 * 2**20, transcendentals=0),
    )(blocks, grad_mixed, resid, gain, shift, gate, *kept, *weights, *ties)


def pack_kernel(layers, rows, block, bias, w_up, w_down, *rest):
    outs, sems = rest[:layers], rest[layers]
    start = pl.multiple_of(block[0] * rows, rows)
    sources = [w.at[layer, pl.ds(start, rows)] for layer in range(layers) for w in (w_up, w_down)]
    targets = [out.at[pl.ds(kind * rows, rows)] for out in outs for kind in range(2)]
    copies = start_copies(sources, targets, sems)
    for layer, out in enumerate(outs):
        out[2 * rows:] = bias_terms(bias[layer:layer + 1])
    for copy in copies:
        copy.wait()


def bias_terms(bias):
    top = bias.astype(BF16)
    left = bias - top.astype(F32)
    middle = left.astype(BF16)
    bottom = (left - middle.astype(F32)).astype(BF16)
    row = lax.broadcasted_iota(jnp.int32, (16, bias.shape[1]), 0)
    terms = [jnp.broadcast_to(term.astype(F32), row.shape) for term in (top, middle, bottom)]
    zero = jnp.zeros(row.shape, F32)
    chosen = jnp.where(row == 0, terms[0], jnp.where(row == 1, terms[1], jnp.where(row == 2, terms[2], zero)))
    return chosen.astype(BF16)


def pack(w_up, w_down, b_up, block):
    layers, width, shard = w_up.shape
    rows = width // 8
    out = jax.ShapeDtypeStruct((2 * rows + 16, shard), BF16)
    vmem = pl.BlockSpec(memory_space=pltpu.VMEM)
    return pl.pallas_call(
        functools.partial(pack_kernel, layers, rows),
        out_shape=[out] * layers,
        in_specs=[pl.BlockSpec(memory_space=pltpu.SMEM), vmem] + [pl.BlockSpec(memory_space=pl.ANY)] * 2,
        out_specs=[vmem] * layers,
        scratch_shapes=[pltpu.SemaphoreType.DMA((2 * layers,))],
        cost_estimate=pl.CostEstimate(flops=0, bytes_accessed=4 * layers * rows * shard * 4, transcendentals=0),
    )(block, b_up, w_up, w_down)


class Chain:
    def __init__(self, token):
        self.token, self.pending = token, []

    def need(self, *places):
        self.pending += places

    def tie(self, *values):
        count = len(values)
        out = lax.optimization_barrier((*values, self.token, *(held[key] for held, key in self.pending)))
        self.token = out[count]
        for (held, key), value in zip(self.pending, out[count + 1:]):
            held[key] = value
        self.pending = []
        return out[0] if count == 1 else out[:count]

    def ties(self):
        out, self.pending = [self.token] + [held[key] for held, key in self.pending], []
        return out


def places(values):
    return [(values, at) for at in range(len(values))]


def swap(value, axis, bit):
    size = lax.axis_size(axis)
    return lax.ppermute(value, axis, [(at, at ^ bit) for at in range(size)])


class Flow:
    def __init__(self, keep, send, place, size, stages):
        self.terms = [(flat(keep), 0)]
        self.send, self.place, self.size, self.stages = flat(send), place, size, stages

    def crossed(self, arrived):
        self.terms.append((arrived, self.place))


def flat(value):
    return value.reshape((-1,) + value.shape[-2:])


def feed_flows(grads):
    *keeps, send = grads
    size = flat(keeps[0]).shape[0]
    return [Flow(keeps[at], send, at * size, size, PART_STAGES[at]) for at in range(3)]


def attend_flows(grads):
    *keeps, send = grads
    size = flat(keeps[0]).shape[0]
    return [Flow(keeps[at], send, at * size, size, stages) for at, stages in enumerate(("xy", "yx"))]


class Reads:
    def __init__(self):
        self.arrays = []

    def at(self, array):
        for at, known in enumerate(self.arrays):
            if known is array:
                return at
        self.arrays.append(array)
        return len(self.arrays) - 1

    def places(self, terms):
        return [(self.at(array), place) for array, place in terms]


def as_block(value):
    tile = value.shape[1] // 3
    parts = [value[:, at * tile:(at + 1) * tile] for at in range(3)]
    return jnp.concatenate(parts + [jnp.zeros_like(parts[0])], axis=0).astype(BF16)


def from_block(block):
    value = block.astype(F32)
    rows = value.shape[0] // 4
    return jnp.concatenate([value[at * rows:(at + 1) * rows] for at in range(3)], axis=1)


def add_small_parts(parts, blocks, out):
    out[...] = jnp.zeros_like(out)
    for layer in range(2):
        fed, attended, up = parts[3 * layer:3 * layer + 3]
        base = 10 * layer
        out[base:base + 3] = fed[0:3]
        out[base + 3:base + 6] = attended[0:3]
        for slot in range(len(SHARD_ORDER)):
            out[pl.ds(base + 6 + blocks[8 + slot], 1)] = up[slot]


def exchange_kernel(plan, blocks, *refs):
    sends, columns, ends, small, small_terms, small_ends, array_count, small_count, tie_count, out_count = plan
    arrays, refs = refs[:array_count], refs[array_count:]
    small_ins, refs = refs[:small_count], refs[small_count + tie_count:]
    outs, refs = refs[:out_count], list(refs[out_count:])
    own = refs.pop(0) if columns else None
    small_out = refs.pop(0) if small == "new" else None
    out_sems, sems = refs.pop(), refs.pop()
    at, groups = 0, []
    wanted = [(size, terms) for _, _, size, terms in sends] + list(columns)
    if small_terms:
        wanted.append((1, small_terms))
    for size, terms in wanted:
        held, waits = refs.pop(0), []
        for term, (array, place) in enumerate(terms):
            waits.append(pltpu.make_async_copy(arrays[array].at[pl.ds(place, size)], held.at[term], sems.at[at]))
            at += 1
        groups.append((waits, held))
    leaving, ahead = [], 3

    def begin(number):
        if number < len(groups):
            for copy in groups[number][0]:
                copy.start()

    for number in range(ahead):
        begin(number)

    def arrive(number):
        for copy in groups[number][0]:
            copy.wait()
        begin(number + ahead)

    def leave(made, out, place, size):
        leaving.append(pltpu.make_async_copy(made, outs[out].at[pl.ds(place, size)], out_sems.at[len(leaving)]))
        leaving[-1].start()

    for number, (out, place, size, terms) in enumerate(sends):
        held, made = groups[number][1], refs.pop(0)
        arrive(number)

        def add(block, carry, held=held, made=made, terms=terms):
            values = [held[term, block] for term in range(len(terms))]
            while len(values) > 1:
                values = [values[at] + values[at + 1] if at + 1 < len(values) else values[at]
                          for at in range(0, len(values), 2)]
            made[block] = values[0]
            return carry

        lax.fori_loop(0, size, add, 0)
        leave(made, out, place, size)
    if columns:
        turned, far = refs.pop(0), refs.pop(0)
        shards = len(SHARD_ORDER)
        share = turned.shape[2] // 4
        for flow, (size, terms) in enumerate(columns):
            held = groups[len(sends) + flow][1]
            arrive(len(sends) + flow)
            for line in range(2):
                parts = []
                for tile in range(size // 2):
                    total = held[0, line * (size // 2) + tile].astype(F32)
                    for term in range(1, len(terms)):
                        total = total + held[term, line * (size // 2) + tile].astype(F32)
                    parts.append(total)
                whole = jnp.concatenate(parts, axis=1)
                to = (2 * flow + line) * share
                for shard in range(shards):
                    turned[shard ^ blocks[8], :, to:to + share] = whole[:, shard * share:(shard + 1) * share]
        own[...] = turned[0]
        tile = far.shape[3]
        for other in range(1, shards):
            for cut in range(3):
                far[other - 1, cut] = turned[other, :, cut * tile:(cut + 1) * tile].astype(BF16)
            leave(far.at[other - 1], *ends[other - 1], 3)
    if small:
        made = refs.pop(0)
        if small == "new":
            add_small_parts(small_ins, blocks, small_out)
            total = small_out[...]
        else:
            total = small_ins[0][...]
            held = groups[-1][1]
            arrive(len(groups) - 1)
            for term in range(len(small_terms)):
                total = total + from_block(held[term, 0])
        made[0] = as_block(total)
        for out, place in small_ends:
            leave(made, out, place, 1)
    for copy in leaving:
        copy.wait()


class Rounds:
    def __init__(self, blocks):
        self.blocks, self.arrived = blocks, []

    def exchange(self, flows, ending=(), small=None, ties=(), crossing=()):
        reads, sends, sizes = Reads(), [], {}

        def room(letter, size):
            place = sizes.get(letter, 0)
            sizes[letter] = place + size
            return list(sizes).index(letter), place

        moved = []
        for flow in flows:
            letter, flow.stages = flow.stages[0], flow.stages[1:]
            flow.size //= 2
            out, place = room(letter, flow.size)
            for cut in range(0, flow.size, 8):
                sends.append((out, place + cut, min(8, flow.size - cut),
                              [(reads.at(array), start + flow.size + cut) for array, start in flow.terms]))
            moved.append((flow.terms, letter, place))
        tile = flat(flows[0].terms[0][0]).shape[1:]
        width = 3 * tile[1]
        columns = [(flow.size, reads.places(flow.terms)) for pair in ending for flow in pair]
        ends = [room(letter, 3) for letter in "uvw"] if columns else []
        mode, small_terms, small_ins, small_ends = "", [], [], []
        if small is not None:
            mode, letters = small.next()
            small_ins = small.parts if mode == "new" else [small.own]
            small_terms = [] if mode == "new" else reads.places(small.terms)
            small_ends = [room(letter, 1) for letter in letters]
        order = list(sizes)
        outs = [jax.ShapeDtypeStruct((sizes[letter],) + tile, BF16) for letter in order]
        held = [pltpu.VMEM((len(terms), size) + tile, BF16) for _, _, size, terms in sends]
        held += [pltpu.VMEM((len(terms), size) + tile, BF16) for size, terms in columns]
        if small_terms:
            held.append(pltpu.VMEM((len(small_terms), 1) + tile, BF16))
        held += [pltpu.VMEM((size,) + tile, BF16) for _, _, size, _ in sends]
        more = []
        if columns:
            held += [pltpu.VMEM((len(SHARD_ORDER), tile[0], width), F32), pltpu.VMEM((3, 3) + tile, BF16)]
            more.append(jax.ShapeDtypeStruct((tile[0], width), F32))
        if mode:
            held.append(pltpu.VMEM((1,) + tile, BF16))
        if mode == "new":
            more.append(jax.ShapeDtypeStruct((24, width), F32))
        ties = [*self.arrived, *ties]
        copies = sum(len(terms) for *_, terms in sends) + sum(len(terms) for _, terms in columns) + len(small_terms)
        anywhere, vmem = pl.BlockSpec(memory_space=pl.ANY), pl.BlockSpec(memory_space=pltpu.VMEM)
        plan = (sends, columns, ends, mode, small_terms, small_ends, len(reads.arrays), len(small_ins), len(ties), len(outs))
        made = pl.pallas_call(
            functools.partial(exchange_kernel, plan),
            out_shape=outs + more,
            in_specs=[pl.BlockSpec(memory_space=pltpu.SMEM)] + [anywhere] * len(reads.arrays) + [vmem] * len(small_ins)
            + [anywhere] * len(ties),
            out_specs=[anywhere] * len(outs) + [vmem] * len(more),
            scratch_shapes=held + [pltpu.SemaphoreType.DMA((copies,)),
                                   pltpu.SemaphoreType.DMA((len(sends) + len(ends) + len(small_ends),))],
            compiler_params=pltpu.CompilerParams(vmem_limit_bytes=VMEM_BYTES),
        )(self.blocks, *reads.arrays, *small_ins, *ties)
        made = list(made)
        rest = made[len(outs):]
        self.made = made[:len(outs)]
        going = self.made + [flows[0].send for flows in crossing]
        going = lax.optimization_barrier(going)
        arrived = {letter: swap(value, *LINKS[letter]) for letter, value in zip(order, going)}
        self.arrived = list(arrived.values())
        for flows, send in zip(crossing, going[len(outs):]):
            self.arrived.append(swap(send, *LINKS["c"]))
            for flow in flows:
                flow.crossed(self.arrived[-1])
        for terms, letter, place in moved:
            terms.append((arrived[letter], place))
        for pair in ending:
            pair[0].own = rest.pop(0)
            pair[0].far = [(arrived[letter], place) for letter, (_, place) in zip("uvw", ends)]
        if mode:
            if mode == "new":
                small.own = rest.pop(0)
            small.terms += [(arrived[letter], place) for letter, (_, place) in zip(letters, small_ends)]

    def cross(self, flows):
        arrived = swap(flows[0].send, *LINKS["c"])
        for flow in flows:
            flow.crossed(arrived)
        self.arrived.append(arrived)


class Small:
    def __init__(self, parts):
        self.parts, self.terms, self.stages = parts, [], ["c", "x", "y", "uvw"]

    def next(self):
        letters = self.stages.pop(0)
        return ("new" if letters == "c" else "old"), letters


def finish_kernel(plan, array_count, *refs):
    feeds, far, small = plan
    arrays, refs = refs[:array_count], refs[array_count:]
    owns, small_own, refs = refs[:2], refs[2], refs[3:]
    up, down, *attends, both = refs[:7]
    held, held_far, held_small, sems = refs[7:]
    copies = []

    def fetch(array, place, size, target):
        copies.append(pltpu.make_async_copy(arrays[array].at[pl.ds(place, size)], target, sems.at[len(copies)]))
        copies[-1].start()

    for layer, part, term, array, place in feeds:
        fetch(array, place, 2, held.at[layer, part, term])
    for layer, other, array, place in far:
        fetch(array, place, 3, held_far.at[layer, other])
    for term, (array, place) in enumerate(small):
        fetch(array, place, 1, held_small.at[term])
    for copy in copies:
        copy.wait()
    terms, tile = held.shape[2], held.shape[5]
    for layer in range(2):
        for part in range(3):
            total = held[layer, part, 0].astype(F32)
            for term in range(1, terms):
                total = total + held[layer, part, term].astype(F32)
            up[layer, :, part * tile:(part + 1) * tile] = total[0]
            down[layer, part * tile:(part + 1) * tile, :] = total[1].T
        total = owns[layer][...]
        for other in range(3):
            total = total + jnp.concatenate([held_far[layer, other, cut].astype(F32) for cut in range(3)], axis=1)
        share = total.shape[1] // 4
        for at, out in enumerate(attends):
            out[layer] = total[:, at * share:(at + 1) * share]
    total = small_own[...]
    for term in range(len(small)):
        total = total + from_block(held_small[term, 0])
    both[...] = total


def finish(feeds, attends, small):
    reads = Reads()
    feed_plan = [(layer, part, term, reads.at(array), place) for layer, flows in enumerate(feeds)
                 for part, flow in enumerate(flows) for term, (array, place) in enumerate(flow.terms)]
    far_plan = [(layer, other, reads.at(array), place) for layer, pair in enumerate(attends)
                for other, (array, place) in enumerate(pair[0].far)]
    small_plan = reads.places(small.terms)
    rows, tile = feeds[0][0].terms[0][0].shape[1:]
    width, terms = 3 * tile, len(feeds[0][0].terms)
    anywhere, vmem = pl.BlockSpec(memory_space=pl.ANY), pl.BlockSpec(memory_space=pltpu.VMEM)
    return pl.pallas_call(
        functools.partial(finish_kernel, (feed_plan, far_plan, small_plan), len(reads.arrays)),
        out_shape=[jax.ShapeDtypeStruct((2, rows, width), F32), jax.ShapeDtypeStruct((2, width, rows), F32)]
        + [jax.ShapeDtypeStruct((2, rows, width // 4), F32)] * 4 + [jax.ShapeDtypeStruct((24, width), F32)],
        in_specs=[anywhere] * len(reads.arrays) + [vmem] * 3,
        out_specs=[vmem] * 7,
        scratch_shapes=[pltpu.VMEM((2, 3, terms, 2, rows, tile), BF16), pltpu.VMEM((2, 3, 3, rows, tile), BF16),
                        pltpu.VMEM((len(small_plan), 1, rows, tile), BF16),
                        pltpu.SemaphoreType.DMA((len(feed_plan) + len(far_plan) + len(small_plan),))],
        compiler_params=pltpu.CompilerParams(vmem_limit_bytes=VMEM_BYTES),
    )(*reads.arrays, attends[0][0].own, attends[1][0].own, small.own)


def far_pieces(layer, w_up, w_down, owns, halves, crossed, blocks):
    rows = w_up.shape[1] // 8
    arrays = [w_up, w_down] + halves + crossed
    plan = [(0, layer, 0, 0, None), (1, layer, 1, 0, None)]
    for core in range(2):
        for kind, (inner, outer) in enumerate(((2, 4), (4, 2))):
            for second in range(2):
                for first in range(2):
                    for other in (1, 2, 3):
                        place = core + inner * first + outer * second
                        plan.append((2 + 4 * core + 2 * kind + second, (first, other - 1), kind,
                                     SHARD_ORDER.index(other), place))
    return Pieces(arrays, plan, blocks, rows, [owns[at] for at in SHARD_ORDER])


def all_pieces(layer, own, w_up, w_down, blocks):
    rows = w_up.shape[1] // 8
    pieces = lax.all_gather(own, ("dp", "mp"))
    plan = [(0, layer, 0, 0, None), (1, layer, 1, 0, None)]
    for slot in (1, 2, 3):
        for kind in range(2):
            for at in range(8):
                source = lambda ref, held, slot=slot, kind=kind, at=at: ref.at[
                    4 * at + held[8 + slot], pl.ds(kind * rows, rows)]
                plan.append((2, source, kind, slot, slice(at * rows, (at + 1) * rows)))
    tails = [own] + [lax.dynamic_index_in_dim(pieces, blocks[8 + slot], 0, False)[2 * rows:] for slot in (1, 2, 3)]
    return Pieces([w_up, w_down, pieces], plan, blocks, rows, tails)


def gathered_pieces(layer, w_up, w_down, b_up, blocks):
    arrays = [lax.all_gather(w_up[layer], "mp"), lax.all_gather(w_down[layer], "mp")]
    shards = arrays[0].shape[0]
    plan = [(kind, at, kind, at, None) for kind in range(2) for at in range(shards)]
    bias = lax.all_gather(b_up[layer:layer + 1], "mp")
    return Pieces(arrays, plan, blocks, 0, [bias_terms(bias[at]) for at in range(shards)])


def sum_feed_anywhere(grads):
    both = lax.psum_scatter(grads, "mp", scatter_dimension=0, tiled=True)[0]
    both = lax.psum_scatter(both.astype(F32), "dp", scatter_dimension=1, tiled=True)
    return both[0], both[1].T


def sum_attend_anywhere(grads):
    whole = lax.psum_scatter(grads, "mp", scatter_dimension=2, tiled=True)
    return lax.psum_scatter(whole.astype(F32), "dp", scatter_dimension=1, tiled=True)


def shards(inputs, slot_valid, ln1_gain, ln1_bias, w_query, w_key, w_value, w_out, gate_logit,
           ln2_gain, ln2_bias, w_up, b_up, w_down, b_down, cotangent):
    pages, slots, width = inputs.shape
    dp, mp = lax.axis_size("dp"), lax.axis_size("mp")
    paired = dp == 8 and mp == 4 and width % (16 * dp) == 0
    if paired:
        blocks = jnp.concatenate([
            lax.axis_index("dp") ^ jnp.arange(8, dtype=jnp.int32),
            lax.axis_index("mp") ^ jnp.array(SHARD_ORDER, jnp.int32)])
    else:
        blocks = jnp.arange(2, dtype=jnp.int32)

    own_valid = lax.dynamic_slice_in_dim(slot_valid, lax.axis_index("mp") * pages, pages, 0) == 1
    key_text = lax.broadcasted_iota(jnp.int32, (slots, slots), 0) < TEXT
    query_text = lax.broadcasted_iota(jnp.int32, (slots, slots), 1) < TEXT
    live = jnp.broadcast_to(own_valid[:, :, None], (pages, slots, slots))
    masks = [
        jnp.where(jnp.logical_and(live, (key_text != query_text)[None]), 0.0, -1e30).astype(F32),
        jnp.where(live, 0.0, -1e30).astype(F32),
    ]
    gate = gate_logit[None]
    weights = (w_query, w_key, w_value, w_out)
    first_rows = inputs.reshape(pages * slots, width)
    cotangent = cotangent.reshape(pages * slots, width)
    got = {"grad": None}

    def attend_layer(layer, rows, ties):
        return attend(layer, layer == 0, rows, masks[layer], ln1_gain, ln1_bias, gate, weights, ties)

    def feed_layer(layer, rows, pieces, ties):
        return feed(layer, rows, ln2_gain, ln2_bias, b_down, pieces, (F32, BF16)[layer], ties)

    def feed_back_layer(layer, ties):
        rows, active, slope, pieces = got["feed", layer]
        got["mixed_grad"], got["feed_sums", layer], got["up_sums", layer], *got["feed_grads", layer] = feed_back(
            layer, (got["grad"], cotangent)[layer], rows, ln2_gain, ln2_bias, active, slope, pieces, not paired, ties)

    def attend_back_layer(layer, ties):
        rows, kept = got["attend", layer]
        got["grad"], got["attend_sums", layer], *got["attend_grads", layer] = attend_back(
            layer, layer == 0, got["mixed_grad"], rows, ln1_gain, ln1_bias, gate, (*kept[:5], *kept[6:]), weights,
            blocks, not paired, ties)

    if paired:
        owns = pack(w_up, w_down, b_up, blocks)
        rows = width // 8
        chain = Chain(owns[0])
        far = lambda own: [swap(own, "mp", other) for other in (1, 2, 3)]
        split = lambda pieces: (jnp.stack([piece[:rows] for piece in pieces]),
                                jnp.stack([piece[rows:2 * rows] for piece in pieces]))
        other_core = lambda *values: [swap(value, "dp", 1) for value in values]

        far_0 = far(owns[0])
        kept_0 = list(attend_layer(0, first_rows, ()))
        chain.need((kept_0, 5))
        far_0 = list(chain.tie(*far_0))
        ups, downs = chain.tie(*split(far_0))
        near_0 = chain.tie(swap(ups, "dp", 2), swap(downs, "dp", 4))
        ups_0, downs_0 = chain.tie(jnp.stack([ups, near_0[0]]), jnp.stack([downs, near_0[1]]))
        side_0 = [swap(ups_0, "dp", 4), swap(downs_0, "dp", 2)]
        core_0 = other_core(ups_0, downs_0)
        side_0 = chain.tie(*side_0)
        core_0 += other_core(*side_0)
        pieces_0 = far_pieces(0, w_up, w_down, [owns[0]] + far_0, [ups_0, side_0[0], downs_0, side_0[1]],
                              [core_0[at] for at in (0, 2, 1, 3)], blocks)
        result_0, active_0, slope_0 = feed_layer(0, kept_0[5], pieces_0, chain.ties())
        kept_1 = attend_layer(1, result_0, ())
        pieces_1 = all_pieces(1, owns[1], w_up, w_down, blocks)
    else:
        pieces_0 = gathered_pieces(0, w_up, w_down, b_up, blocks)
        pieces_1 = gathered_pieces(1, w_up, w_down, b_up, blocks)
        kept_0 = attend_layer(0, first_rows, ())
        result_0, active_0, slope_0 = feed_layer(0, kept_0[5], pieces_0, ())
        kept_1 = attend_layer(1, result_0, ())

    result_1, active_1, slope_1 = feed_layer(1, kept_1[5], pieces_1, ())
    got["feed", 0] = kept_0[5], active_0, slope_0, pieces_0
    got["feed", 1] = kept_1[5], active_1, slope_1, pieces_1
    got["attend", 0], got["attend", 1] = (first_rows, kept_0), (result_0, kept_1)

    if paired:
        rounds = Rounds(blocks)
        feed_back_layer(1, ())
        feeds, attends = {1: feed_flows(got["feed_grads", 1])}, {}
        rounds.cross(feeds[1])
        attend_back_layer(1, ())
        attends[1] = attend_flows(got["attend_grads", 1])
        rounds.exchange(feeds[1], ties=[got["attend_sums", 1]], crossing=[attends[1]])
        feed_back_layer(0, rounds.made)
        feeds[0] = feed_flows(got["feed_grads", 0])
        rounds.exchange(feeds[1] + attends[1], ties=[got["feed_sums", 0]], crossing=[feeds[0]])
        attend_back_layer(0, rounds.made)
        attends[0] = attend_flows(got["attend_grads", 0])
        small = Small([got[name, layer] for layer in (0, 1) for name in ("feed_sums", "attend_sums", "up_sums")])
        rounds.exchange(feeds[0] + feeds[1] + attends[1], small=small, crossing=[attends[0]])
        rounds.exchange(feeds[0] + attends[0] + feeds[1], [attends[1]], small)
        rounds.exchange(feeds[0] + attends[0], small=small)
        rounds.exchange(feeds[0], [attends[0]], small)
        row_of = lambda row, layer: row + 10 * layer
        up_grad, down_grad, *attend_grads, both = finish([feeds[0], feeds[1]], [attends[0], attends[1]], small)
    else:
        for layer in (1, 0):
            feed_back_layer(layer, ())
            attend_back_layer(layer, ())
        feed_grads = [sum_feed_anywhere(got["feed_grads", layer][0]) for layer in (0, 1)]
        up_grad, down_grad = (jnp.stack([feed_grads[layer][at] for layer in (0, 1)]) for at in range(2))
        sums = [sum_attend_anywhere(got["attend_grads", layer][0]) for layer in (0, 1)]
        attend_grads = [jnp.stack([sums[0][at], sums[1][at]]) for at in range(4)]
        both = lax.psum(jnp.concatenate([part for layer in (0, 1) for part in (
            got["feed_sums", layer][:3], got["attend_sums", layer][:3], got["up_sums", layer][:, 0])]), ("dp", "mp"))
        later = both.shape[0] // 2
        row_of = lambda row, layer: row + later * layer

    lines = width // dp
    mine = lax.dynamic_slice_in_dim(both, lax.axis_index("dp") * lines, lines, 1)
    pick = lambda row: jnp.stack([mine[row_of(row, 0)], mine[row_of(row, 1)]])
    me = lax.axis_index("mp")
    bup_grad = jnp.concatenate([
        lax.dynamic_slice_in_dim(both, row_of(6, 0) + me, 1, 0), lax.dynamic_slice_in_dim(both, row_of(6, 1) + me, 1, 0)])
    return (
        result_1.reshape(pages, slots, width),
        got["grad"].reshape(pages, slots, width),
        pick(3),
        pick(4),
        *attend_grads,
        mine[5],
        pick(1),
        pick(2),
        up_grad,
        bup_grad,
        down_grad,
        pick(0),
    )


def solution(mesh):
    rows = P(("dp", "mp"), None, None)
    return jax.shard_map(
        shards,
        mesh=mesh,
        in_specs=(rows, P("dp", None), P(), P(), P(), P(), P(), P(), P(), P(), P(), P(None, None, "mp"),
                  P(None, "mp"), P(None, "mp", None), P(), rows),
        out_specs=(rows, rows, P(None, "dp"), P(None, "dp"), P(None, "dp", "mp"), P(None, "dp", "mp"),
                   P(None, "dp", "mp"), P(None, "dp", "mp"), P("dp"), P(None, "dp"), P(None, "dp"),
                   P(None, "dp", "mp"), P(None, "mp"), P(None, "mp", "dp"), P(None, "dp")),
        check_vma=False,
    )
```

time: 502 us -> 396 us (0.79)
  waiting for transfers between devices: 208 us -> 144 us
  starting transfers between devices: 95.9 us -> 39.3 us
  Pallas kernels: 107 us -> 157 us
  blocking collectives: 39.6 us -> 0 us
  other arithmetic: 28.5 us -> 6.56 us
  between operations: 1.82 us -> 20.6 us
  local copies, waits for them, and re-layouts: 14.2 us -> 21.7 us
    ppermute x73 -> x37, waiting for transfers between devices: 208 us -> 134 us  [swap(): return lax.ppermute(value, axis, [(at, at ^ bit) for at in range(size)])]
    ppermute x73 -> x37, starting transfers between devices: 95.9 us -> 39.3 us  [swap(): return lax.ppermute(value, axis, [(at, at ^ bit) for at in range(size)])]
    pallas_call x6 -> x14, Pallas kernels: 88.5 us -> 139 us  [the longest x6 38.5 us: exchange(): pl.pallas_call(functools.partial(exchange_kernel, plan), out_shape=outs +...]
    psum x1 -> x0, blocking collectives: 39.6 us -> none  [shards(): both = lax.psum(jnp.concatenate(sums), ('dp', 'mp'))]
    unnamed x48 -> x71, local copies, waits for them, and re-layouts: 2.03 us -> 16 us
    convert_element_type x16 -> x0, other arithmetic: 11.3 us -> none  [add_rows(): sum((term[:, start:2 * start].astype(F32) for term in terms)).astype(BF16)]
    all_gather x0 -> x1, waiting for transfers between devices: none -> 9.41 us  [all_pieces(): pieces = lax.all_gather(own, ('dp', 'mp'))]
    add x12 -> x0, other arithmetic: 6 us -> none  [the longest x4 4.6 us: add_columns(): whole = sum((term.astype(F32) for term in terms))]
  transfers between devices with their start and end apart: 73 -> 38, of which waited for: 32 -> 19; matrix products, arithmetic and copies ran while one was open for 8% -> 1% of each run, Pallas kernels for 13% -> 20%
where the time goes in v2:
time: 396 us; the launch traced here: 389 us
  Pallas kernels  157 us (40%)
  waiting for transfers between devices  144 us (36%)
  starting transfers between devices  39.3 us (10%)
  local copies, waits for them, and re-layouts  21.7 us (5%)
  between operations  20.6 us (5%)
  other arithmetic  6.56 us (2%)
    ppermute x37, waiting for transfers between devices, swap(): return lax.ppermute(value, axis, [(at, at ^ bit) for at in range(size)])  134 us
    ppermute x37, starting transfers between devices, swap(): return lax.ppermute(value, axis, [(at, at ^ bit) for at in range(size)])  39.3 us
    pallas_call x6, Pallas kernels, exchange(): pl.pallas_call(functools.partial(exchange_kernel, plan), out_shape=outs +...  38.5 us
    pallas_call x2, Pallas kernels, feed_back(): pl.pallas_call(functools.partial(feed_back_kernel, layer, pieces, joint,...  36.8 us
    pallas_call x2, Pallas kernels, attend_back(): pl.pallas_call(body, out_shape=[jax.ShapeDtypeStruct((rows, width), F32),...  28.6 us
    pallas_call x2, Pallas kernels, feed(): pl.pallas_call(functools.partial(feed_kernel, layer, pieces, len(ties)),...  26.6 us
    pallas_call x2, Pallas kernels, attend(): pl.pallas_call(body, out_shape=outs, in_specs=[vmem] * 5 + [pl.BlockSpec(...  18.3 us
    unnamed x71, local copies, waits for them, and re-layouts  16 us
  transfers between devices with their start and end apart: 38, of which 19 were waited for; matrix products, arithmetic and copies ran while one was open for 1% of the time, Pallas kernels for 20%

profile of v2, /device:TPU:0, one launch (start us, length us, event | category | flops | bytes accessed | tf_op | source)
XLA Modules:
  0.0 388.9 jit_solution(1295499811797943629)
XLA Ops:
  19.2 9.1 %shard_map.281 = (bf16[384,768]{1,0:T(8,128)(2,1)}, bf16[384,768]{1,0:T(8,128)(2,1)}, bf16[384,768]{1,0:T(8,128)(2,1)}, bf16[3,6,256,128]{3,2,1,0:T(8,128)(2,1)}...) custom-call(bf16[384,768]{1,0:T(8,128)(2,1)} %bitcast.91, ...), custom_call_target="tpu_custom_call" | custom-call | flops 1811939328 | bytes 14680064 | tf_op jit(solution)/shard_map/pallas_call | solution.py:132
  29.6 13.4 %collective-permute-done.1.rest_1_ = bf16[208,768]{1,0:T(8,128)(2,1)S(1)} collective-permute-done((bf16[208,768]{1,0:T(8,128)(2,1)}, bf16[208,768]{1,0:T(8,128)(2,1)S(1)}, u32[]{:S(2)}, u32[]{:S(2)}) %collective-permute-start.1) | collective-permute-done | bytes 319520 | tf_op jit(solution)/shard_map/ppermute | solution.py:538
  46.9 6.6 %collective-permute-done.3 = bf16[3,96,768]{2,1,0:T(8,128)(2,1)S(1)} collective-permute-done((bf16[3,96,768]{2,1,0:T(8,128)(2,1)S(1)}, bf16[3,96,768]{2,1,0:T(8,128)(2,1)S(1)}, u32[]{:S(2)}, u32[]{:S(2)}) %collective-permute-start.3) | collective-permute-done | bytes 442400 | tf_op jit(solution)/shard_map/ppermute | solution.py:538
  58.3 20.0 %collective-permute-done.5.rest_7_.rest_3_ = bf16[2,3,96,768]{3,2,1,0:T(8,128)(2,1)S(1)} collective-permute-done((bf16[2,3,96,768]{3,2,1,0:T(8,128)(2,1)S(1)}, bf16[2,3,96,768]{3,2,1,0:T(8,128)(2,1)S(1)}, u32[]{:S(2)}, u32[]{:S(2)}) %collective-permute-start.5) | collective-permute-done | bytes 884768 | tf_op jit(solution)/shard_map/ppermute | solution.py:538
  90.4 13.5 %shard_map.282 = (f32[384,768]{1,0:T(8,128)}, bf16[4,384,768]{2,1,0:T(8,128)(2,1)}, bf16[4,384,768]{2,1,0:T(8,128)(2,1)}) custom-call(s32[12]{0:T(128)} %pad_add_fusion.block.blocks.refs_0_, f32[384,768]{1,0:T(8,128)} %get-tuple-element.133.mixed, f32[2,768]{1,0:T(2,128)} %gain.7, f32[2,768]{1,0:T(2,128)} %shift.7, f32[2,768]{1,0:T(2,128)} %b_down.3, ...), custom_call_target="tpu_custom_call" | custom-call | flops 3623878656 | bytes 20971520 | tf_op jit(solution)/shard_map/pallas_call | solution.py:224
  104.7 9.2 %shard_map.283 = (bf16[384,768]{1,0:T(8,128)(2,1)}, bf16[384,768]{1,0:T(8,128)(2,1)}, bf16[384,768]{1,0:T(8,128)(2,1)}, bf16[3,6,256,128]{3,2,1,0:T(8,128)(2,1)}...) custom-call(f32[384,768]{1,0:T(8,128)} %get-tuple-element.150.refs_0_.refs_2_, f32[3,128,128]{2,1,0:T(8,128)} %broadcast_in_dim.32.refs_1_, ...), custom_call_target="tpu_custom_call" | custom-call | flops 1811939328 | bytes 14680064 | tf_op jit(solution)/shard_map/pallas_call | solution.py:132
  113.9 9.4 %all-gather.3.cloned.1.call-done = bf16[6656,768]{1,0:T(8,128)(2,1)} async-done(((bf16[208,768]{1,0:T(8,128)(2,1)}), bf16[6656,768]{1,0:T(8,128)(2,1)}) %all-gather.3.cloned.1.call-update) | async-done | bytes 10223632 | tf_op jit(solution)/shard_map/all_gather | solution.py:874
  124.7 13.1 %shard_map.284 = (bf16[384,768]{1,0:T(8,128)(2,1)}, bf16[4,384,768]{2,1,0:T(8,128)(2,1)}, bf16[4,384,768]{2,1,0:T(8,128)(2,1)}) custom-call(s32[12]{0:T(128)} %pad_add_fusion.block.blocks.refs_0_, f32[384,768]{1,0:T(8,128)} %get-tuple-element.151.mixed, f32[2,768]{1,0:T(2,128)} %gain.7, f32[2,768]{1,0:T(2,128)} %shift.7, f32[2,768]{1,0:T(2,128)} %b_down.3, ...), custom_call_target="tpu_custom_call" | custom-call | flops 3623878656 | bytes 20971520 | tf_op jit(solution)/shard_map/pallas_call | solution.py:224
  137.8 18.5 %shard_map.285 = (f32[384,768]{1,0:T(8,128)}, f32[8,768]{1,0:T(8,128)}, f32[4,1,768]{2,1,0:T(1,128)}, bf16[2,2,2,2,2,96,256]{6,5,4,3,2,1,0:T(8,128)(2,1)}, bf16[...) custom-call(s32[12]{0:T(128)} %pad_add_fusion.block.blocks.refs_0_, ...), custom_call_target="tpu_custom_call" | custom-call | flops 7247757312 | bytes 31457280 | tf_op jit(solution)/shard_map/pallas_call | solution.py:356
  156.6 14.3 %shard_map.286 = (f32[384,768]{1,0:T(8,128)}, f32[8,768]{1,0:T(8,128)}, bf16[2,2,2,3,96,256]{5,4,3,2,1,0:T(8,128)(2,1)}, bf16[2,2,2,3,96,256]{5,4,3,2,1,0:T(8,128)(2,1)}, bf16[2,2,2,2,3,96,256]{6,5,4,3,2,1,0:T(8,128)(2,1)}) custom-call(s32[12]{0:T(128)} %pad_add_fusion.block.blocks.refs_0_, f32[384,768]{1,0:T(8,128)} %get-tuple-element.156.refs_1_, ...), custom_call_target="tpu_custom_call" | custom-call | flops 3623878656 | bytes 25165824 | tf_op jit(solution)/shard_map/pallas_call | solution.py:459
  181.3 5.1 %collective-permute-start.14 = (bf16[16,96,256]{2,1,0:T(8,128)(2,1)}, bf16[16,96,256]{2,1,0:T(8,128)(2,1)S(1)}, u32[]{:S(2)}, u32[]{:S(2)}) collective-permute-start(bf16[16,96,256]{2,1,0:T(8,128)(2,1)} %get-tuple-element.183.rest_12_), channel_id=1, source_target_pairs={{0,1},{1,0},{2,3},{3,2},{4,5},{5,4},{6,7},{7,6},{8,9},{9,8},{10,11... | collective-permute-start | bytes 2359304 | tf_op jit(solution)/shard_map/ppermute | solution.py:538
  186.4 18.3 %shard_map.288 = (f32[384,768]{1,0:T(8,128)}, f32[8,768]{1,0:T(8,128)}, f32[4,1,768]{2,1,0:T(1,128)}, bf16[2,2,2,2,2,96,256]{6,5,4,3,2,1,0:T(8,128)(2,1)}, bf16[...) custom-call(s32[12]{0:T(128)} %pad_add_fusion.block.blocks.refs_0_, ...), custom_call_target="tpu_custom_call" | custom-call | flops 7247757312 | bytes 31457280 | tf_op jit(solution)/shard_map/pallas_call | solution.py:356
  206.9 5.6 %shard_map.289 = (bf16[20,96,256]{2,1,0:T(8,128)(2,1)}, bf16[8,96,256]{2,1,0:T(8,128)(2,1)}, bf16[20,96,256]{2,1,0:T(8,128)(2,1)}) custom-call(s32[12]{0:T(128)} %pad_add_fusion.block.blocks.refs_0_, bf16[32,96,256]{2,1,0:T(8,128)(2,1)} %bitcast.47, bf16[96,96,256]{2,1,0:T(8,128)(2,1)} %copy-done, bf16[16,96,256]{2,1,0:T(8,128)(2,1)} %copy-done.6, ...), custom_call_target="tpu_custom_call" | custom-call | tf_op jit(solution)/shard_map/pallas_call | solution.py:747
  214.0 14.3 %shard_map.290 = (f32[384,768]{1,0:T(8,128)}, f32[8,768]{1,0:T(8,128)}, bf16[2,2,2,3,96,256]{5,4,3,2,1,0:T(8,128)(2,1)}, bf16[2,2,2,3,96,256]{5,4,3,2,1,0:T(8,128)(2,1)}, bf16[2,2,2,2,3,96,256]{6,5,4,3,2,1,0:T(8,128)(2,1)}) custom-call(s32[12]{0:T(128)} %pad_add_fusion.block.blocks.refs_0_, f32[384,768]{1,0:T(8,128)} %get-tuple-element.173.refs_1_, ...), custom_call_target="tpu_custom_call" | custom-call | flops 3623878656 | bytes 25165824 | tf_op jit(solution)/shard_map/pallas_call | solution.py:459
  228.4 8.6 %collective-permute-done.17.refs_7_.refs_23_.refs_13_.refs_18_ = bf16[20,96,256]{2,1,0:T(8,128)(2,1)S(1)} collective-permute-done((bf16[20,96,256]{2,1,0:T(8,128)(2,1)}, bf16[20,96,256]{2,1,0:T(8,128)(2,1)S(1)}, u32[]{:S(2)}, u32[]{:S(2)}) %collective-permute-start.17) | collective-permute-done | bytes 983072 | tf_op jit(solution)/shard_map/ppermute | solution.py:538
  239.8 8.5 %shard_map.291 = (bf16[26,96,256]{2,1,0:T(8,128)(2,1)}, bf16[26,96,256]{2,1,0:T(8,128)(2,1)}, bf16[16,96,256]{2,1,0:T(8,128)(2,1)}, bf16[4,96,256]{2,1,0:T(8,128...) custom-call(s32[12]{0:T(128)} %pad_add_fusion.block.blocks.refs_0_, bf16[32,96,256]{2,1,0:T(8,128)(2,1)} %bitcast.61, ...), custom_call_target="tpu_custom_call" | custom-call | tf_op jit(solution)/shard_map/pallas_call | solution.py:747
  254.6 17.3 %collective-permute-done.24.refs_14_.refs_29_.refs_19_ = bf16[4,96,256]{2,1,0:T(8,128)(2,1)S(1)} collective-permute-done((bf16[4,96,256]{2,1,0:T(8,128)(2,1)}, bf16[4,96,256]{2,1,0:T(8,128)(2,1)S(1)}, u32[]{:S(2)}, u32[]{:S(2)}) %collective-permute-start.24) | collective-permute-done | bytes 196640 | tf_op jit(solution)/shard_map/ppermute | solution.py:538
  273.9 5.1 %collective-permute-done.20.refs_2_.refs_26_ = bf16[26,96,256]{2,1,0:T(8,128)(2,1)S(1)} collective-permute-done((bf16[26,96,256]{2,1,0:T(8,128)(2,1)}, bf16[26,96,256]{2,1,0:T(8,128)(2,1)S(1)}, u32[]{:S(2)}, u32[]{:S(2)}) %collective-permute-start.20) | collective-permute-done | bytes 1277984 | tf_op jit(solution)/shard_map/ppermute | solution.py:538
  281.3 9.0 %shard_map.292 = (bf16[20,96,256]{2,1,0:T(8,128)(2,1)}, bf16[13,96,256]{2,1,0:T(8,128)(2,1)}, bf16[21,96,256]{2,1,0:T(8,128)(2,1)}, bf16[7,96,256]{2,1,0:T(8,128...) custom-call(s32[12]{0:T(128)} %pad_add_fusion.block.blocks.refs_0_, bf16[32,96,256]{2,1,0:T(8,128)(2,1)} %bitcast.62, ...), custom_call_target="tpu_custom_call" | custom-call | tf_op jit(solution)/shard_map/pallas_call | solution.py:747
  297.5 22.2 %collective-permute-done.30.refs_19_.refs_28_ = bf16[3,96,256]{2,1,0:T(8,128)(2,1)S(1)} collective-permute-done((bf16[3,96,256]{2,1,0:T(8,128)(2,1)}, bf16[3,96,256]{2,1,0:T(8,128)(2,1)S(1)}, u32[]{:S(2)}, u32[]{:S(2)}) %collective-permute-start.30) | collective-permute-done | bytes 147488 | tf_op jit(solution)/shard_map/ppermute | solution.py:538
  328.6 8.0 %collective-permute-done.31.refs_4_.refs_18_ = bf16[4,96,256]{2,1,0:T(8,128)(2,1)S(1)} collective-permute-done((bf16[4,96,256]{2,1,0:T(8,128)(2,1)}, bf16[4,96,256]{2,1,0:T(8,128)(2,1)S(1)}, u32[]{:S(2)}, u32[]{:S(2)}) %collective-permute-start.31) | collective-permute-done | bytes 196640 | tf_op jit(solution)/shard_map/ppermute | solution.py:538
  339.8 5.8 %shard_map.294 = (bf16[6,96,256]{2,1,0:T(8,128)(2,1)}, bf16[8,96,256]{2,1,0:T(8,128)(2,1)}, bf16[4,96,256]{2,1,0:T(8,128)(2,1)}, f32[96,768]{1,0:T(8,128)}) custom-call(s32[12]{0:T(128)} %pad_add_fusion.block.blocks.refs_0_, bf16[32,96,256]{2,1,0:T(8,128)(2,1)} %bitcast.64, bf16[96,96,256]{2,1,0:T(8,128)(2,1)} %copy-done.1, bf16[26,96,256]{2,1,0:T(8,128)(2,1)} %copy-done.4, ...), custom_call_target="tpu_custom_call" | custom-call | tf_op jit(solution)/shard_map/pallas_call | solution.py:747
  350.1 15.5 %collective-permute-done.36.refs_27_ = bf16[4,96,256]{2,1,0:T(8,128)(2,1)S(1)} collective-permute-done((bf16[4,96,256]{2,1,0:T(8,128)(2,1)}, bf16[4,96,256]{2,1,0:T(8,128)(2,1)S(1)}, u32[]{:S(2)}, u32[]{:S(2)}) %collective-permute-start.36) | collective-permute-done | bytes 196640 | tf_op jit(solution)/shard_map/ppermute | solution.py:538
  368.5 5.4 %shard_map.295 = (f32[2,96,768]{2,1,0:T(8,128)}, f32[2,768,96]{2,1,0:T(8,128)}, f32[2,96,192]{2,1,0:T(8,128)}, f32[2,96,192]{2,1,0:T(8,128)}, f32[2,96,192]{2,1,...) custom-call(bf16[32,96,256]{2,1,0:T(8,128)(2,1)} %bitcast.65, bf16[96,96,256]{2,1,0:T(8,128)(2,1)} %copy-done.1, ...), custom_call_target="tpu_custom_call" | custom-call | tf_op jit(solution)/shard_map/pallas_call | solution.py:844
  (165 shorter events, 92.4 us)
Async XLA Ops:
  7.2 116.2 %all-gather.3.cloned.1.call-start = ((), (), s32[]{:S(2)}) async-start(), calls=%async_computation | async-start | bytes 10543104 | tf_op jit(solution)/shard_map/all_gather | solution.py:874
  14.4 28.7 %collective-permute-start.1 = (bf16[208,768]{1,0:T(8,128)(2,1)}, bf16[208,768]{1,0:T(8,128)(2,1)S(1)}, u32[]{:S(2)}, u32[]{:S(2)}) collective-permute-start(bf16[208,768]{1,0:T(8,128)(2,1)} %get-tuple-element.149.rest_0_.rest_14_), channel_id=1, source_target_pairs={{0,2},{1,3},{2,0},{3,1},{4,6},{5,7},{6,4},{7,5},{8,10},{9,11},{10,... | collective-permute-start | bytes 958472 | tf_op jit(solution)/shard_map/ppermute | solution.py:538
  17.0 26.1 %collective-permute-start.2 = (bf16[208,768]{1,0:T(8,128)(2,1)}, bf16[208,768]{1,0:T(8,128)(2,1)S(1)}, u32[]{:S(2)}, u32[]{:S(2)}) collective-permute-start(bf16[208,768]{1,0:T(8,128)(2,1)} %get-tuple-element.149.rest_0_.rest_14_), channel_id=1, source_target_pairs={{0,3},{1,2},{2,1},{3,0},{4,7},{5,6},{6,5},{7,4},{8,11},{9,10},{10,... | collective-permute-start | bytes 958472 | tf_op jit(solution)/shard_map/ppermute | solution.py:538
  55.7 22.6 %collective-permute-start.5 = (bf16[2,3,96,768]{3,2,1,0:T(8,128)(2,1)S(1)}, bf16[2,3,96,768]{3,2,1,0:T(8,128)(2,1)S(1)}, u32[]{:S(2)}, u32[]{:S(2)}) collective-permute-start(bf16[2,3,96,768]{3,2,1,0:T(8,128)(2,1)S(1)} %pad_maximum_fusion.rest_6_.rest_2_), channel_id=1, source_target_pairs={{0,16},{4,20},{8,24},{12,28},{16,0},{20,4},{24,8},{28,12},{1,17},{... | collective-permute-start | bytes 2654216 | tf_op jit(solution)/shard_map/ppermute | solution.py:538
  57.3 26.1 %collective-permute-start.6 = (bf16[2,3,96,768]{3,2,1,0:T(8,128)(2,1)S(1)}, bf16[2,3,96,768]{3,2,1,0:T(8,128)(2,1)S(1)}, u32[]{:S(2)}, u32[]{:S(2)}) collective-permute-start(bf16[2,3,96,768]{3,2,1,0:T(8,128)(2,1)S(1)} %pad_maximum_fusion.1.rest_8_.rest_4_), channel_id=1, source_target_pairs={{0,8},{4,12},{8,0},{12,4},{16,24},{20,28},{24,16},{28,20},{1,9},{5... | collective-permute-start | bytes 2654216 | tf_op jit(solution)/shard_map/ppermute | solution.py:538
  57.8 32.5 %collective-permute-start.7 = (bf16[2,3,96,768]{3,2,1,0:T(8,128)(2,1)S(1)}, bf16[2,3,96,768]{3,2,1,0:T(8,128)(2,1)}, u32[]{:S(2)}, u32[]{:S(2)}) collective-permute-start(bf16[2,3,96,768]{3,2,1,0:T(8,128)(2,1)S(1)} %pad_maximum_fusion.rest_6_.rest_2_), channel_id=1, source_target_pairs={{0,4},{4,0},{8,12},{12,8},{16,20},{20,16},{24,28},{28,24},{1,5},{5... | collective-permute-start | bytes 2654216 | tf_op jit(solution)/shard_map/ppermute | solution.py:538
  57.8 32.5 %collective-permute-start.9 = (bf16[2,3,96,768]{3,2,1,0:T(8,128)(2,1)S(1)}, bf16[2,3,96,768]{3,2,1,0:T(8,128)(2,1)}, u32[]{:S(2)}, u32[]{:S(2)}) collective-permute-start(bf16[2,3,96,768]{3,2,1,0:T(8,128)(2,1)S(1)} %pad_maximum_fusion.1.rest_8_.rest_4_), channel_id=1, source_target_pairs={{0,4},{4,0},{8,12},{12,8},{16,20},{20,16},{24,28},{28,24},{1,5},{5... | collective-permute-start | bytes 2654216 | tf_op jit(solution)/shard_map/ppermute | solution.py:538
  178.0 26.7 %collective-permute-start.15 = (bf16[48,96,256]{2,1,0:T(8,128)(2,1)S(1)}, bf16[48,96,256]{2,1,0:T(8,128)(2,1)S(1)}, u32[]{:S(2)}, u32[]{:S(2)}) collective-permute-start(bf16[48,96,256]{2,1,0:T(8,128)(2,1)S(1)} %bitcast.100), channel_id=1, source_target_pairs={{0,4},{4,0},{8,12},{12,8},{16,20},{20,16},{24,28},{28,24},{1,5},{5... | collective-permute-start | bytes 7077896 | tf_op jit(solution)/shard_map/ppermute | solution.py:538
  178.4 26.4 %collective-permute-start.12 = (bf16[16,96,256]{2,1,0:T(8,128)(2,1)}, bf16[16,96,256]{2,1,0:T(8,128)(2,1)S(1)}, u32[]{:S(2)}, u32[]{:S(2)}) collective-permute-start(bf16[16,96,256]{2,1,0:T(8,128)(2,1)} %get-tuple-element.181.rest_10_), channel_id=1, source_target_pairs={{0,8},{4,12},{8,0},{12,4},{16,24},{20,28},{24,16},{28,20},{1,9},{5... | collective-permute-start | bytes 2359304 | tf_op jit(solution)/shard_map/ppermute | solution.py:538
  179.8 24.9 %collective-permute-start.13 = (bf16[16,96,256]{2,1,0:T(8,128)(2,1)}, bf16[16,96,256]{2,1,0:T(8,128)(2,1)S(1)}, u32[]{:S(2)}, u32[]{:S(2)}) collective-permute-start(bf16[16,96,256]{2,1,0:T(8,128)(2,1)} %get-tuple-element.182.rest_11_), channel_id=1, source_target_pairs={{0,16},{4,20},{8,24},{12,28},{16,0},{20,4},{24,8},{28,12},{1,17},{... | collective-permute-start | bytes 2359304 | tf_op jit(solution)/shard_map/ppermute | solution.py:538
  181.3 23.5 %collective-permute-start.14 = (bf16[16,96,256]{2,1,0:T(8,128)(2,1)}, bf16[16,96,256]{2,1,0:T(8,128)(2,1)S(1)}, u32[]{:S(2)}, u32[]{:S(2)}) collective-permute-start(bf16[16,96,256]{2,1,0:T(8,128)(2,1)} %get-tuple-element.183.rest_12_), channel_id=1, source_target_pairs={{0,1},{1,0},{2,3},{3,2},{4,5},{5,4},{6,7},{7,6},{8,9},{9,8},{10,11... | collective-permute-start | bytes 2359304 | tf_op jit(solution)/shard_map/ppermute | solution.py:538
  212.5 24.6 %collective-permute-start.16 = (bf16[96,96,256]{2,1,0:T(8,128)(2,1)}, bf16[96,96,256]{2,1,0:T(8,128)(2,1)S(1)}, u32[]{:S(2)}, u32[]{:S(2)}) collective-permute-start(bf16[96,96,256]{2,1,0:T(8,128)(2,1)} %bitcast.97), channel_id=1, source_target_pairs={{0,4},{4,0},{8,12},{12,8},{16,20},{20,16},{24,28},{28,24},{1,5},{5... | collective-permute-start | bytes 14155784 | tf_op jit(solution)/shard_map/ppermute | solution.py:538
  212.6 24.4 %collective-permute-start.17 = (bf16[20,96,256]{2,1,0:T(8,128)(2,1)}, bf16[20,96,256]{2,1,0:T(8,128)(2,1)S(1)}, u32[]{:S(2)}, u32[]{:S(2)}) collective-permute-start(bf16[20,96,256]{2,1,0:T(8,128)(2,1)} %get-tuple-element.197.refs_16_), channel_id=1, source_target_pairs={{0,16},{4,20},{8,24},{12,28},{16,0},{20,4},{24,8},{28,12},{1,17},{... | collective-permute-start | bytes 2949128 | tf_op jit(solution)/shard_map/ppermute | solution.py:538
  213.1 24.0 %collective-permute-start.19 = (bf16[20,96,256]{2,1,0:T(8,128)(2,1)}, bf16[20,96,256]{2,1,0:T(8,128)(2,1)S(1)}, u32[]{:S(2)}, u32[]{:S(2)}) collective-permute-start(bf16[20,96,256]{2,1,0:T(8,128)(2,1)} %get-tuple-element.199.refs_18_), channel_id=1, source_target_pairs={{0,8},{4,12},{8,0},{12,4},{16,24},{20,28},{24,16},{28,20},{1,9},{5... | collective-permute-start | bytes 2949128 | tf_op jit(solution)/shard_map/ppermute | solution.py:538
  248.2 30.8 %collective-permute-start.23 = (bf16[48,96,256]{2,1,0:T(8,128)(2,1)}, bf16[48,96,256]{2,1,0:T(8,128)(2,1)S(1)}, u32[]{:S(2)}, u32[]{:S(2)}) collective-permute-start(bf16[48,96,256]{2,1,0:T(8,128)(2,1)} %bitcast.99), channel_id=1, source_target_pairs={{0,4},{4,0},{8,12},{12,8},{16,20},{20,16},{24,28},{28,24},{1,5},{5... | collective-permute-start | bytes 7077896 | tf_op jit(solution)/shard_map/ppermute | solution.py:538
  248.3 30.7 %collective-permute-start.20 = (bf16[26,96,256]{2,1,0:T(8,128)(2,1)}, bf16[26,96,256]{2,1,0:T(8,128)(2,1)S(1)}, u32[]{:S(2)}, u32[]{:S(2)}) collective-permute-start(bf16[26,96,256]{2,1,0:T(8,128)(2,1)} %get-tuple-element.210), channel_id=1, source_target_pairs={{0,8},{4,12},{8,0},{12,4},{16,24},{20,28},{24,16},{28,20},{1,9},{5... | collective-permute-start | bytes 3833864 | tf_op jit(solution)/shard_map/ppermute | solution.py:538
  248.6 30.5 %collective-permute-start.21 = (bf16[26,96,256]{2,1,0:T(8,128)(2,1)}, bf16[26,96,256]{2,1,0:T(8,128)(2,1)S(1)}, u32[]{:S(2)}, u32[]{:S(2)}) collective-permute-start(bf16[26,96,256]{2,1,0:T(8,128)(2,1)} %get-tuple-element.211), channel_id=1, source_target_pairs={{0,16},{4,20},{8,24},{12,28},{16,0},{20,4},{24,8},{28,12},{1,17},{... | collective-permute-start | bytes 3833864 | tf_op jit(solution)/shard_map/ppermute | solution.py:538
  250.1 23.8 %collective-permute-start.22 = (bf16[16,96,256]{2,1,0:T(8,128)(2,1)}, bf16[16,96,256]{2,1,0:T(8,128)(2,1)S(1)}, u32[]{:S(2)}, u32[]{:S(2)}) collective-permute-start(bf16[16,96,256]{2,1,0:T(8,128)(2,1)} %get-tuple-element.212), channel_id=1, source_target_pairs={{0,1},{1,0},{2,3},{3,2},{4,5},{5,4},{6,7},{7,6},{8,9},{9,8},{10,11... | collective-permute-start | bytes 2359304 | tf_op jit(solution)/shard_map/ppermute | solution.py:538
  290.3 29.5 %collective-permute-start.28 = (bf16[21,96,256]{2,1,0:T(8,128)(2,1)}, bf16[21,96,256]{2,1,0:T(8,128)(2,1)S(1)}, u32[]{:S(2)}, u32[]{:S(2)}) collective-permute-start(bf16[21,96,256]{2,1,0:T(8,128)(2,1)} %get-tuple-element.226), channel_id=1, source_target_pairs={{0,8},{4,12},{8,0},{12,4},{16,24},{20,28},{24,16},{28,20},{1,9},{5... | collective-permute-start | bytes 3096584 | tf_op jit(solution)/shard_map/ppermute | solution.py:538
  291.7 28.1 %collective-permute-start.26 = (bf16[20,96,256]{2,1,0:T(8,128)(2,1)}, bf16[20,96,256]{2,1,0:T(8,128)(2,1)S(1)}, u32[]{:S(2)}, u32[]{:S(2)}) collective-permute-start(bf16[20,96,256]{2,1,0:T(8,128)(2,1)} %get-tuple-element.224), channel_id=1, source_target_pairs={{0,16},{4,20},{8,24},{12,28},{16,0},{20,4},{24,8},{28,12},{1,17},{... | collective-permute-start | bytes 2949128 | tf_op jit(solution)/shard_map/ppermute | solution.py:538
  293.1 26.6 %collective-permute-start.27 = (bf16[13,96,256]{2,1,0:T(8,128)(2,1)}, bf16[13,96,256]{2,1,0:T(8,128)(2,1)S(1)}, u32[]{:S(2)}, u32[]{:S(2)}) collective-permute-start(bf16[13,96,256]{2,1,0:T(8,128)(2,1)} %get-tuple-element.225), channel_id=1, source_target_pairs={{0,1},{1,0},{2,3},{3,2},{4,5},{5,4},{6,7},{7,6},{8,9},{9,8},{10,11... | collective-permute-start | bytes 1916936 | tf_op jit(solution)/shard_map/ppermute | solution.py:538
  293.5 26.2 %collective-permute-start.29 = (bf16[7,96,256]{2,1,0:T(8,128)(2,1)}, bf16[7,96,256]{2,1,0:T(8,128)(2,1)S(1)}, u32[]{:S(2)}, u32[]{:S(2)}) collective-permute-start(bf16[7,96,256]{2,1,0:T(8,128)(2,1)} %get-tuple-element.227), channel_id=1, source_target_pairs={{0,2},{1,3},{2,0},{3,1},{4,6},{5,7},{6,4},{7,5},{8,10},{9,11},{10,... | collective-permute-start | bytes 1032200 | tf_op jit(solution)/shard_map/ppermute | solution.py:538
  296.2 23.6 %collective-permute-start.30 = (bf16[3,96,256]{2,1,0:T(8,128)(2,1)}, bf16[3,96,256]{2,1,0:T(8,128)(2,1)S(1)}, u32[]{:S(2)}, u32[]{:S(2)}) collective-permute-start(bf16[3,96,256]{2,1,0:T(8,128)(2,1)} %get-tuple-element.228), channel_id=1, source_target_pairs={{0,3},{1,2},{2,1},{3,0},{4,7},{5,6},{6,5},{7,4},{8,11},{9,10},{10,... | collective-permute-start | bytes 442376 | tf_op jit(solution)/shard_map/ppermute | solution.py:538
  345.6 22.1 %collective-permute-start.35 = (bf16[8,96,256]{2,1,0:T(8,128)(2,1)}, bf16[8,96,256]{2,1,0:T(8,128)(2,1)S(1)}, u32[]{:S(2)}, u32[]{:S(2)}) collective-permute-start(bf16[8,96,256]{2,1,0:T(8,128)(2,1)} %get-tuple-element.236), channel_id=1, source_target_pairs={{0,2},{1,3},{2,0},{3,1},{4,6},{5,7},{6,4},{7,5},{8,10},{9,11},{10,... | collective-permute-start | bytes 1179656 | tf_op jit(solution)/shard_map/ppermute | solution.py:538
  (49 other events, 366.6 us)
Sparse Core Ops, SparseCore 0:
  11.4 111.8 all-gather.2

commit v3 on v2

v3 whole, which is shorter than its diff:
```python
import functools

import jax
import jax.numpy as jnp
from jax import lax
from jax.experimental import pallas as pl
from jax.experimental.pallas import tpu as pltpu
from jax.sharding import PartitionSpec as P

HEADS = 12
TEXT = 112
F32 = jnp.float32
BF16 = jnp.bfloat16
VMEM_BYTES = 56 * 2**20


def dot(a, b, a_dim, b_dim):
    return lax.dot_general(a, b, (((a_dim,), (b_dim,)), ((), ())), preferred_element_type=F32)


def whiten(rows):
    centered = rows - jnp.mean(rows, axis=-1, keepdims=True)
    spread = jnp.mean(centered * centered, axis=-1, keepdims=True)
    inverse = lax.rsqrt(spread + 1e-05)
    return centered * inverse, inverse


def whiten_back(white, inverse, gain, grad):
    scaled = grad * gain
    first = jnp.mean(scaled, axis=-1, keepdims=True)
    second = jnp.mean(scaled * white, axis=-1, keepdims=True)
    return inverse * (scaled - first - white * second)


def column_sum(rows):
    return jnp.sum(rows, axis=0, keepdims=True)


def gelu_and_slope(values):
    size = jnp.abs(values)
    t = 1.0 / (1.0 + (0.3275911 * 0.7071067811865476) * size)
    bell = jnp.exp(-0.5 * values * values)
    poly = 0.5 * 1.061405429
    poly = poly * t + 0.5 * -1.453152027
    poly = poly * t + 0.5 * 1.421413741
    poly = poly * t + 0.5 * -0.284496736
    poly = poly * t + 0.5 * 0.254829592
    tail = poly * t * bell
    phi = jnp.where(values >= 0.0, 1.0 - tail, tail)
    return values * phi, phi + values * bell * 0.3989422804014327


def split_heads(pair):
    lane = lax.broadcasted_iota(jnp.int32, pair.shape, 1)
    first = lane < pair.shape[1] // 2
    zero = jnp.zeros_like(pair)
    return jnp.concatenate([jnp.where(first, pair, zero), jnp.where(first, zero, pair)], axis=0)


def join_heads(both):
    slots = both.shape[0] // 2
    lane = lax.broadcasted_iota(jnp.int32, (slots, both.shape[1]), 1)
    return jnp.where(lane < both.shape[1] // 2, both[:slots], both[slots:])


def start_copies(sources, targets, sems):
    copies = [
        pltpu.make_async_copy(source, target, sems.at[at])
        for at, (source, target) in enumerate(zip(sources, targets))
    ]
    for copy in copies:
        copy.start()
    return copies


class Arriving:
    def __init__(self, source, held, sem):
        self.copy, self.held, self.here = pltpu.make_async_copy(source, held, sem), held, False
        self.copy.start()

    def __getitem__(self, at):
        if not self.here:
            self.copy.wait()
            self.here = True
        return self.held[at]


class Leaving:
    def __init__(self, sems):
        self.sems, self.copies = sems, []

    def send(self, held, target):
        self.copies.append(pltpu.make_async_copy(held, target, self.sems.at[len(self.copies)]))
        self.copies[-1].start()

    def wait(self):
        for copy in self.copies:
            copy.wait()


def attend_kernel(layer, crossed, resid, mask, gain, shift, gate, wq, wk, wv, wo,
                  outs, made, held, sems, out_sems):
    q_out, k_out, v_out, p_out, c_out, mixed, *branch_out = made
    leaving = Leaving(out_sems)
    pages, slots = mask.shape[0], mask.shape[1]
    width = resid.shape[1]
    pairs = HEADS // 2
    pair_width = width // pairs
    scale = 1.0 / (width // HEADS) ** 0.5
    copies = start_copies(
        [w.at[layer] for w in (wq, wk, wv, wo)], [held.at[at] for at in range(4)], sems
    )
    white, _ = whiten(resid[...].astype(F32))
    normed = (white * gain[layer:layer + 1] + shift[layer:layer + 1]).astype(BF16)
    copies[0].wait()
    q_out[...] = (dot(normed, held[0], 1, 0).astype(BF16).astype(F32) * scale).astype(BF16)
    leaving.send(q_out, outs[0])
    copies[1].wait()
    k_out[...] = dot(normed, held[1], 1, 0).astype(BF16)
    leaving.send(k_out, outs[1])
    copies[2].wait()
    v_out[...] = dot(normed, held[2], 1, 0).astype(BF16)
    leaving.send(v_out, outs[2])

    for page in range(pages):
        rows = slice(page * slots, (page + 1) * slots)
        bias = mask[page]
        for pair in range(pairs):
            cols = slice(pair * pair_width, (pair + 1) * pair_width)
            scores = dot(split_heads(k_out[rows, cols]), q_out[rows, cols], 1, 1)
            scores = scores.reshape(2, slots, slots) + bias[None]
            top = jnp.max(scores, axis=1, keepdims=True)
            raised = jnp.exp(scores - top)
            probs = raised * (1.0 / jnp.sum(raised, axis=1, keepdims=True))
            probs = probs.reshape(2 * slots, slots).astype(BF16)
            p_out[page, pair] = probs
            c_out[rows, cols] = dot(probs, split_heads(v_out[rows, cols]), 0, 0).astype(BF16)
        leaving.send(p_out.at[page], outs[3].at[page])
    leaving.send(c_out, outs[4])
    copies[3].wait()
    for page in range(pages):
        rows = slice(page * slots, (page + 1) * slots)
        branch = dot(c_out[rows], held[3], 1, 0)
        if crossed:
            branch_out[0][rows] = branch.astype(BF16)
            branch = branch * jax.nn.sigmoid(gate[...])
            leaving.send(branch_out[0].at[rows], outs[6].at[rows])
        mixed[rows] = resid[rows].astype(F32) + branch
        leaving.send(mixed.at[rows], outs[5].at[rows])
    leaving.wait()


def attend(layer, crossed, resid, mask, gain, shift, gate, weights, ties):
    rows, width = resid.shape
    pages, slots = mask.shape[:2]
    low = jax.ShapeDtypeStruct((rows, width), BF16)
    vmem = pl.BlockSpec(memory_space=pltpu.VMEM)
    outs = [low, low, low, jax.ShapeDtypeStruct((pages, HEADS // 2, 2 * slots, slots), BF16), low,
            jax.ShapeDtypeStruct((rows, width), F32)]
    if crossed:
        outs.append(low)

    def body(*refs):
        ins, rest = refs[:9], refs[9 + len(ties):]
        attend_kernel(layer, crossed, *ins, rest[:len(outs)], rest[len(outs):2 * len(outs)], *rest[2 * len(outs):])

    return pl.pallas_call(
        body,
        out_shape=outs,
        in_specs=[vmem] * 5 + [pl.BlockSpec(memory_space=pl.ANY)] * (4 + len(ties)),
        out_specs=[pl.BlockSpec(memory_space=pl.ANY)] * len(outs),
        scratch_shapes=[pltpu.VMEM(out.shape, out.dtype) for out in outs]
        + [pltpu.VMEM((4, width, width), BF16), pltpu.SemaphoreType.DMA((4,)),
           pltpu.SemaphoreType.DMA((4 + (2 + crossed) * pages,))],
        compiler_params=pltpu.CompilerParams(vmem_limit_bytes=VMEM_BYTES),
        cost_estimate=pl.CostEstimate(flops=8 * rows * width * width, bytes_accessed=14 * 2**20, transcendentals=0),
    )(resid, mask, gain, shift, gate, *weights, *ties)


class Pieces:
    def __init__(self, arrays, plan, blocks, tails):
        self.arrays, self.plan, self.blocks, self.tails = arrays, plan, blocks, tails

    def copies(self, refs, held, blocks, sems, first=0, last=None):
        return [
            pltpu.make_async_copy(refs[array] if index is None else refs[array].at[index],
                                  held[kind].at[target(blocks[0])], sems.at[at])
            for at, (array, index, kind, target) in list(enumerate(self.plan))[first:last]
        ]

    def held(self, width):
        shape = (2, 2, 2, len(self.tails), width // 8, width)
        return [pltpu.VMEM(shape, BF16), pltpu.VMEM(shape, BF16)]

    def tail_specs(self, width):
        return [pl.BlockSpec((16, width), lambda step, last=tail.shape[0] // 16 - 1: (last, 0)) for tail in self.tails]

    def start_and_wait(self, refs, held, blocks, sems):
        step = pl.program_id(0)

        @pl.when(step == 0)
        def _():
            for copy in self.copies(refs, held, blocks, sems):
                copy.start()

        def wait():
            @pl.when(step == 0)
            def _():
                for copy in self.copies(refs, held, blocks, sems, 0, 2):
                    copy.wait()

            @pl.when(step == 1)
            def _():
                for copy in self.copies(refs, held, blocks, sems, 2):
                    copy.wait()
        return wait


def feed_kernel(layer, pieces, ties, blocks, mixed, gain, shift, b_down, *rest):
    count = len(pieces.arrays)
    tails, rest = rest[:len(pieces.tails)], rest[len(pieces.tails):]
    refs, rest = rest[:count], rest[count + ties:]
    result, active_out, slope_out, up, down, low, total, bias, sems = rest
    shards, width = up.shape[3], up.shape[5]
    step = pl.program_id(0)
    wait = pieces.start_and_wait(refs, (up, down), blocks, sems)

    @pl.when(step == 0)
    def _():
        white, _ = whiten(mixed[...])
        low[...] = (white * gain[layer:layer + 1] + shift[layer:layer + 1]).astype(BF16)
        total[...] = mixed[...] + b_down[layer:layer + 1]
        for at, tail in enumerate(tails):
            bias[at] = column_sum(tail[...].astype(F32))

    wait()
    parts = 3
    part = width // parts
    for at in range(parts):
        cols = slice(at * part, (at + 1) * part)
        upper = dot(low[...], up[:, :, :, step, :, cols].reshape(width, part), 1, 0) + bias[step, :, cols]
        active, slope = gelu_and_slope(upper)
        active = active.astype(BF16)
        active_out[0, :, cols] = active
        slope_out[0, :, cols] = slope.astype(BF16)
        total[...] += dot(active, down[:, :, :, step].reshape(width, width)[cols], 1, 0)

    @pl.when(step == shards - 1)
    def _():
        result[...] = total[...].astype(result.dtype)


def feed(layer, mixed, gain, shift, b_down, pieces, out_type, ties):
    rows, width = mixed.shape
    shards = len(pieces.tails)
    whole = lambda shape: pl.BlockSpec(shape, lambda step: (0,) * len(shape))
    each = lambda shape: pl.BlockSpec((1,) + shape, lambda step: (step,) + (0,) * len(shape))
    return pl.pallas_call(
        functools.partial(feed_kernel, layer, pieces, len(ties)),
        grid=(shards,),
        out_shape=[jax.ShapeDtypeStruct((rows, width), out_type)]
        + [jax.ShapeDtypeStruct((shards, rows, width), BF16)] * 2,
        in_specs=[pl.BlockSpec(memory_space=pltpu.SMEM), whole((rows, width)), whole(gain.shape), whole(shift.shape),
                  whole(b_down.shape)] + pieces.tail_specs(width)
        + [pl.BlockSpec(memory_space=pl.ANY)] * (len(pieces.arrays) + len(ties)),
        out_specs=[whole((rows, width)), each((rows, width)), each((rows, width))],
        scratch_shapes=[*pieces.held(width),
                        pltpu.VMEM((rows, width), BF16), pltpu.VMEM((rows, width), F32),
                        pltpu.VMEM((shards, 1, width), F32), pltpu.SemaphoreType.DMA((len(pieces.plan),))],
        compiler_params=pltpu.CompilerParams(vmem_limit_bytes=VMEM_BYTES),
        cost_estimate=pl.CostEstimate(flops=16 * rows * width * width, bytes_accessed=20 * 2**20, transcendentals=0),
    )(pieces.blocks, mixed, gain, shift, b_down, *pieces.tails, *pieces.arrays, *ties)


ROWS_FIRST = ((0, 4, 2, 6, 1, 5, 3, 7), (0, 2, 4, 6, 1, 3, 5, 7))
PART_ORDERS = (0, 1, 0)
PART_STAGES = ("xyvu", "yuxv", "uxyv")
SHARD_ORDER = (0, 2, 1, 3)
LINKS = {"c": ("dp", 1), "x": ("dp", 2), "y": ("dp", 4), "u": ("mp", 1), "v": ("mp", 2), "w": ("mp", 3)}


def turn_rows(held, turned, blocks, order):
    if order is None:
        turned[...] = held[...]
        return
    size = held.shape[0] // len(order)
    for at, place in enumerate(order):
        start = pl.multiple_of(blocks[place] * size, size)
        turned[at * size:(at + 1) * size] = held[pl.ds(start, size)]


def put_blocks(made, keep, send, place):
    rows = made.shape[0] // 8
    for half, out in enumerate((keep, send)):
        for first in range(2):
            for second in range(2):
                at = (4 * half + 2 * first + second) * rows
                out[place(first, second)] = made[at:at + rows]


def feed_back_kernel(layer, pieces, joint, ties, blocks, grad_out, mixed, gain, shift, active, slope, *rest):
    count = len(pieces.arrays)
    refs, rest = rest[:count], rest[count + ties:]
    grads_count = 1 if joint else 2
    grad_mixed, sums, up_sums, *grads = rest[:3 + grads_count]
    up, down, low, low_turned, normed_turned, held, total, sems = rest[3 + grads_count:]
    shards, width = up.shape[3], up.shape[5]
    part = width // 3
    step = pl.program_id(0)
    wait = pieces.start_and_wait(refs, (up, down), blocks, sems)

    def put(kind, turned, right):
        if joint:
            grads[0][0, kind] = dot(turned[0], right, 1, 0).astype(BF16)
            return
        for at in range(3):
            made = dot(turned[PART_ORDERS[at]], right[:, at * part:(at + 1) * part], 1, 0).astype(BF16)
            put_blocks(made, *grads, lambda first, second: (0, at, kind, first, second))

    @pl.when(step == 0)
    def _():
        rows = grad_out[...].astype(F32)
        low[...] = rows.astype(BF16)
        sums[...] = jnp.zeros_like(sums)
        sums[0:1] = column_sum(rows)
        white, _ = whiten(mixed[...])
        normed = (white * gain[layer:layer + 1] + shift[layer:layer + 1]).astype(BF16)
        for value, turned in ((low[...], low_turned), (normed, normed_turned)):
            held[...] = value.T
            for at in range(turned.shape[0]):
                turn_rows(held, turned.at[at], blocks, None if joint else ROWS_FIRST[at])
        total[...] = jnp.zeros_like(total)

    wait()
    put(1, low_turned, active[0])
    upper = dot(low[...], down[:, :, :, step].reshape(width, width), 1, 1) * slope[0].astype(F32)
    up_sums[0] = column_sum(upper)
    upper_low = upper.astype(BF16)
    put(0, normed_turned, upper_low)
    total[...] += dot(upper_low, up[:, :, :, step].reshape(width, width), 1, 1)

    @pl.when(step == shards - 1)
    def _():
        white, inverse = whiten(mixed[...])
        grad = total[...]
        sums[1:2] = column_sum(grad * white)
        sums[2:3] = column_sum(grad)
        grad_mixed[...] = grad_out[...].astype(F32) + whiten_back(white, inverse, gain[layer:layer + 1], grad)


def feed_back(layer, grad_out, mixed, gain, shift, active, slope, pieces, joint, ties):
    rows, width = mixed.shape
    shards = active.shape[0]
    whole = lambda shape: pl.BlockSpec(shape, lambda step: (0,) * len(shape))
    each = lambda shape: pl.BlockSpec((1,) + shape, lambda step: (step,) + (0,) * len(shape))
    if joint:
        grads = [(2, width, width)]
    else:
        grads = [(3, 2, 2, 2, width // 8, width // 3)] * 2
    turned = pltpu.VMEM((1 if joint else 2, width, rows), BF16)
    return pl.pallas_call(
        functools.partial(feed_back_kernel, layer, pieces, joint, len(ties)),
        grid=(shards,),
        out_shape=[jax.ShapeDtypeStruct((rows, width), F32), jax.ShapeDtypeStruct((8, width), F32),
                   jax.ShapeDtypeStruct((shards, 1, width), F32)]
        + [jax.ShapeDtypeStruct((shards,) + shape, BF16) for shape in grads],
        in_specs=[pl.BlockSpec(memory_space=pltpu.SMEM), whole((rows, width)), whole((rows, width)), whole(gain.shape),
                  whole(shift.shape), each((rows, width)), each((rows, width))]
        + [pl.BlockSpec(memory_space=pl.ANY)] * (len(pieces.arrays) + len(ties)),
        out_specs=[whole((rows, width)), whole((8, width)), each((1, width))] + [each(shape) for shape in grads],
        scratch_shapes=[*pieces.held(width),
                        pltpu.VMEM((rows, width), BF16), turned, turned, pltpu.VMEM((width, rows), BF16),
                        pltpu.VMEM((rows, width), F32), pltpu.SemaphoreType.DMA((len(pieces.plan),))],
        compiler_params=pltpu.CompilerParams(vmem_limit_bytes=VMEM_BYTES),
        cost_estimate=pl.CostEstimate(flops=32 * rows * width * width, bytes_accessed=30 * 2**20, transcendentals=0),
    )(pieces.blocks, grad_out, mixed, gain, shift, active, slope, *pieces.arrays, *ties)


def attend_back_kernel(layer, crossed, joint, blocks, grad_mixed, resid, gain, shift, gate, q, k, v, p, context, branch,
                       wq, wk, wv, wo, resid_out, sums, outs, grad_resid, grads, landing,
                       held, turning, turned, gc, gq, gk, gv, sems, out_sems):
    pages, slots = p.shape[0], p.shape[3]
    width = resid.shape[1]
    pairs = HEADS // 2
    pair_width = width // pairs
    scale = 1.0 / (width // HEADS) ** 0.5
    number = iter(range(16))
    arrive = lambda source, target: Arriving(source, target, sems.at[next(number)])
    land = iter(landing)
    context, grad_mixed = arrive(context, next(land)), arrive(grad_mixed, next(land))
    if crossed:
        branch = arrive(branch, next(land))
    w_out = arrive(wo.at[layer], held.at[0])
    v, p, k, q = (arrive(value, next(land)) for value in (v, p, k, q))
    resid = arrive(resid, next(land))
    w_query, w_key, w_value = (arrive(w.at[layer], held.at[at + 1]) for at, w in enumerate((wq, wk, wv)))
    leaving = Leaving(out_sems)
    sums[...] = jnp.zeros_like(sums)

    def put(at, right):
        made = dot(turned[...], right, 1, 0).astype(BF16)
        if joint:
            grads[0][at] = made
            return
        tile = width // 3
        for col in range(3):
            put_blocks(made[:, col * tile:(col + 1) * tile], *grads,
                       lambda first, second: (at // 2, first, second, at % 2, col))

    def turn(rows, order):
        turning[...] = rows.T
        turn_rows(turning, turned, blocks, None if joint else ROWS_FIRST[order])

    grad = grad_mixed[...]
    if crossed:
        opened = jax.nn.sigmoid(gate[...])
        sums[2:3] = column_sum(grad * branch[...].astype(F32)) * (opened * (1.0 - opened))
        low = (grad * opened).astype(BF16)
    else:
        low = grad.astype(BF16)
    turn(context[...], 1)
    put(3, low)
    gc[...] = dot(low, w_out[...], 1, 1).astype(BF16)

    for page in range(pages):
        rows = slice(page * slots, (page + 1) * slots)
        for pair in range(pairs):
            cols = slice(pair * pair_width, (pair + 1) * pair_width)
            probs_low = p[page, pair]
            probs = probs_low.astype(F32).reshape(2, slots, slots)
            grad_probs = dot(split_heads(v[rows, cols]), gc[rows, cols], 1, 1).reshape(2, slots, slots)
            delta = jnp.sum(probs * grad_probs, axis=1, keepdims=True)
            grad_scores = (probs * (grad_probs - delta)).astype(BF16).reshape(2 * slots, slots)
            gq[rows, cols] = (dot(grad_scores, split_heads(k[rows, cols]), 0, 0) * scale).astype(BF16)
            gk[rows, cols] = join_heads(dot(grad_scores, q[rows, cols], 1, 0)).astype(BF16)
            gv[rows, cols] = join_heads(dot(probs_low, gc[rows, cols], 1, 0)).astype(BF16)

    white, inverse = whiten(resid[...].astype(F32))
    normed = (white * gain[layer:layer + 1] + shift[layer:layer + 1]).astype(BF16)
    turn(normed, 1)
    put(2, gv[...])
    if not joint:
        for made, out in zip(grads, outs):
            leaving.send(made.at[1], out.at[1])
    if not joint:
        turn_rows(turning, turned, blocks, ROWS_FIRST[0])
    put(0, gq[...])
    put(1, gk[...])
    for made, out in zip(grads, outs):
        if joint:
            leaving.send(made, out)
        else:
            leaving.send(made.at[0], out.at[0])
    total = dot(gq[...], w_query[...], 1, 1) + dot(gk[...], w_key[...], 1, 1) + dot(gv[...], w_value[...], 1, 1)
    sums[0:1] = column_sum(total * white)
    sums[1:2] = column_sum(total)
    grad_resid[...] = grad + whiten_back(white, inverse, gain[layer:layer + 1], total)
    leaving.send(grad_resid, resid_out)
    leaving.wait()


def attend_back(layer, crossed, grad_mixed, resid, gain, shift, gate, kept, weights, blocks, joint, ties):
    rows, width = resid.shape
    vmem = pl.BlockSpec(memory_space=pltpu.VMEM)
    kept = list(kept)
    given = 6 + len(kept) + 4
    if joint:
        grads = [jax.ShapeDtypeStruct((4, width, width), BF16)]
    else:
        grads = [jax.ShapeDtypeStruct((2, 2, 2, 2, 3, width // 8, width // 3), BF16)] * 2

    def body(*refs):
        ins, rest = list(refs[:given]), refs[given + len(ties):]
        if not crossed:
            ins.insert(11, None)
        count = len(grads)
        resid_out, sums, outs, resid_made, rest = rest[0], rest[1], rest[2:2 + count], rest[2 + count], rest[3 + count:]
        attend_back_kernel(layer, crossed, joint, *ins, resid_out, sums, outs, resid_made, rest[:count],
                           rest[count:count + len(landing)], *rest[count + len(landing):])

    low = pltpu.VMEM((rows, width), BF16)
    like = lambda value: pltpu.VMEM(value.shape, value.dtype)
    q, k, v, p, context, *branch = kept
    landing = [like(value) for value in (context, grad_mixed, *branch, v, p, k, q, resid)]
    anywhere = pl.BlockSpec(memory_space=pl.ANY)
    return pl.pallas_call(
        body,
        out_shape=[jax.ShapeDtypeStruct((rows, width), F32), jax.ShapeDtypeStruct((8, width), F32)] + grads,
        in_specs=[pl.BlockSpec(memory_space=pltpu.SMEM)] + [anywhere] * 2 + [vmem] * 3
        + [anywhere] * (len(kept) + 4 + len(ties)),
        out_specs=[anywhere, vmem] + [anywhere] * len(grads),
        scratch_shapes=[pltpu.VMEM((rows, width), F32)] + [like(grad) for grad in grads] + landing
        + [pltpu.VMEM((4, width, width), BF16), pltpu.VMEM((width, rows), BF16), pltpu.VMEM((width, rows), BF16),
           low, low, low, low, pltpu.SemaphoreType.DMA((16,)), pltpu.SemaphoreType.DMA((5,))],
        compiler_params=pltpu.CompilerParams(vmem_limit_bytes=VMEM_BYTES),
        cost_estimate=pl.CostEstimate(flops=16 * rows * width * width, bytes_accessed=24 * 2**20, transcendentals=0),
    )(blocks, grad_mixed, resid, gain, shift, gate, *kept, *weights, *ties)


def pack_kernel(layers, rows, block, bias, w_up, w_down, *rest):
    outs, sems = rest[:layers], rest[layers]
    start = pl.multiple_of(block[0] * rows, rows)
    sources = [w.at[layer, pl.ds(start, rows)] for layer in range(layers) for w in (w_up, w_down)]
    targets = [out.at[pl.ds(kind * rows, rows)] for out in outs for kind in range(2)]
    copies = start_copies(sources, targets, sems)
    for layer, out in enumerate(outs):
        out[2 * rows:] = bias_terms(bias[layer:layer + 1])
    for copy in copies:
        copy.wait()


def bias_terms(bias):
    top = bias.astype(BF16)
    left = bias - top.astype(F32)
    middle = left.astype(BF16)
    bottom = (left - middle.astype(F32)).astype(BF16)
    row = lax.broadcasted_iota(jnp.int32, (16, bias.shape[1]), 0)
    terms = [jnp.broadcast_to(term.astype(F32), row.shape) for term in (top, middle, bottom)]
    zero = jnp.zeros(row.shape, F32)
    chosen = jnp.where(row == 0, terms[0], jnp.where(row == 1, terms[1], jnp.where(row == 2, terms[2], zero)))
    return chosen.astype(BF16)


def pack(w_up, w_down, b_up, block):
    layers, width, shard = w_up.shape
    rows = width // 8
    out = jax.ShapeDtypeStruct((2 * rows + 16, shard), BF16)
    vmem = pl.BlockSpec(memory_space=pltpu.VMEM)
    return pl.pallas_call(
        functools.partial(pack_kernel, layers, rows),
        out_shape=[out] * layers,
        in_specs=[pl.BlockSpec(memory_space=pltpu.SMEM), vmem] + [pl.BlockSpec(memory_space=pl.ANY)] * 2,
        out_specs=[vmem] * layers,
        scratch_shapes=[pltpu.SemaphoreType.DMA((2 * layers,))],
        cost_estimate=pl.CostEstimate(flops=0, bytes_accessed=4 * layers * rows * shard * 4, transcendentals=0),
    )(block, b_up, w_up, w_down)


class Chain:
    def __init__(self, token):
        self.token, self.pending = token, []

    def need(self, *places):
        self.pending += places

    def tie(self, *values):
        count = len(values)
        out = lax.optimization_barrier((*values, self.token, *(held[key] for held, key in self.pending)))
        self.token = out[count]
        for (held, key), value in zip(self.pending, out[count + 1:]):
            held[key] = value
        self.pending = []
        return out[0] if count == 1 else out[:count]

    def ties(self):
        out, self.pending = [self.token] + [held[key] for held, key in self.pending], []
        return out


def places(values):
    return [(values, at) for at in range(len(values))]


def swap(value, axis, bit):
    size = lax.axis_size(axis)
    return lax.ppermute(value, axis, [(at, at ^ bit) for at in range(size)])


class Flow:
    def __init__(self, keep, index, bits, stages):
        self.wide, self.index, self.bits, self.stages, self.terms = [keep], list(index), bits, stages, []
        self.tile = keep.shape[-2:]

    def halve(self):
        bit, self.bits = self.bits[0], self.bits[1:]
        leaves = list(self.index)
        leaves[bit], self.index[bit] = 1, 0
        return tuple(leaves)

    def order(self, shape):
        open_dims = [dim for dim, at in enumerate(self.index) if at is None]
        ranked = list(self.bits) + [dim for dim in open_dims if dim not in self.bits]
        sizes = [shape[dim] for dim in open_dims]
        places = [()]
        for dim in ranked:
            places = [place + (at,) for place in places for at in range(shape[dim])]
        return sizes, [tuple(place[ranked.index(dim)] for dim in open_dims) for place in places]


def feed_flows(grads):
    keep = grads[0].reshape((2, 2) + grads[0].shape[1:])
    bits = ((4, 5, 1, 0), (4, 0, 5, 1), (0, 4, 5, 1))
    return [Flow(keep, (None, None, at, None, None, None), bits[at], PART_STAGES[at]) for at in range(3)]


def attend_flows(grads):
    return [Flow(grads[0], (at, None, None, None, None), (1, 2), stages) for at, stages in enumerate(("xy", "yx"))]


class Reads:
    def __init__(self):
        self.arrays = []

    def at(self, array):
        for at, known in enumerate(self.arrays):
            if known is array:
                return at
        self.arrays.append(array)
        return len(self.arrays) - 1

    def places(self, terms):
        return [(self.at(array), place) for array, place in terms]


def as_block(value):
    tile = value.shape[1] // 3
    parts = [value[:, at * tile:(at + 1) * tile] for at in range(3)]
    return jnp.concatenate(parts + [jnp.zeros_like(parts[0])], axis=0).astype(BF16)


def from_block(block):
    value = block.astype(F32)
    rows = value.shape[0] // 4
    return jnp.concatenate([value[at * rows:(at + 1) * rows] for at in range(3)], axis=1)


def add_small_parts(parts, blocks, out):
    out[...] = jnp.zeros_like(out)
    for layer in range(2):
        fed, attended, up = parts[3 * layer:3 * layer + 3]
        base = 10 * layer
        out[base:base + 3] = fed[0:3]
        out[base + 3:base + 6] = attended[0:3]
        for slot in range(len(SHARD_ORDER)):
            out[pl.ds(base + 6 + blocks[8 + slot], 1)] = up[slot]


def exchange_kernel(plan, blocks, *refs):
    (sizes, reads, sends, column_count, ends, small, small_terms, small_ends,
     array_count, small_count, tie_count) = plan
    arrays, refs = refs[:array_count], refs[array_count:]
    small_ins, refs = refs[:small_count], refs[small_count + tie_count:]
    outs, refs = refs[:len(sizes)], list(refs[len(sizes):])
    own = refs.pop(0) if column_count else None
    small_out = refs.pop(0) if small == "new" else None
    out_sems, sems = refs.pop(), refs.pop()
    mades = [refs.pop(0) for _ in sizes]
    copies, groups = [], []

    def fetch(source, target):
        copies.append(pltpu.make_async_copy(source, target, sems.at[len(copies)]))
        copies[-1].start()
        return copies[-1]

    for wide, _, terms, size in reads:
        held_wide = refs.pop(0)
        held = refs.pop(0) if terms else None
        waits = [fetch(arrays[array].at[index], held_wide.at[at]) for at, (array, index) in enumerate(wide)]
        waits += [fetch(arrays[array].at[pl.ds(place, size)], held.at[at]) for at, (array, place) in enumerate(terms)]
        groups.append((waits, held_wide, held))
    held_small = refs.pop(0) if small_terms else None
    small_waits = [fetch(arrays[array].at[pl.ds(place, 1)], held_small.at[at]) for at, (array, place) in enumerate(small_terms)]

    def arrive(number):
        waits, held_wide, held = groups[number]
        for copy in waits:
            copy.wait()
        wide, _, terms, _ = reads[number]
        return lambda block, place: [held_wide[(at,) + place] for at in range(len(wide))] + [
            held[at, block] for at in range(len(terms))]

    for number, (out, start, order) in enumerate(sends):
        values_of = arrive(number)
        for block, place in enumerate(order):
            values = values_of(block, place)
            while len(values) > 1:
                values = [values[at] + values[at + 1] if at + 1 < len(values) else values[at]
                          for at in range(0, len(values), 2)]
            mades[out][start + block] = values[0]
    if column_count:
        turned = refs.pop(0)
        shards = len(SHARD_ORDER)
        share = turned.shape[2] // 4
        for flow in range(column_count):
            values_of = arrive(len(sends) + flow)
            lines, tiles = reads[len(sends) + flow][1]
            for line in range(lines):
                parts = []
                for tile in range(tiles):
                    total = None
                    for value in values_of(line * tiles + tile, (line, tile)):
                        total = value.astype(F32) if total is None else total + value.astype(F32)
                    parts.append(total)
                whole = jnp.concatenate(parts, axis=1)
                to = (2 * flow + line) * share
                for shard in range(shards):
                    turned[shard ^ blocks[8], :, to:to + share] = whole[:, shard * share:(shard + 1) * share]
        own[...] = turned[0]
        tile = mades[0].shape[2]
        for other in range(1, shards):
            out, start = ends[other - 1]
            for cut in range(3):
                mades[out][start + cut] = turned[other, :, cut * tile:(cut + 1) * tile].astype(BF16)
    if small:
        if small == "new":
            add_small_parts(small_ins, blocks, small_out)
            total = small_out[...]
        else:
            total = small_ins[0][...]
            for copy in small_waits:
                copy.wait()
            for term in range(len(small_terms)):
                total = total + from_block(held_small[term, 0])
        for out, start in small_ends:
            mades[out][start] = as_block(total)
    leaving = [pltpu.make_async_copy(made, outs[at], out_sems.at[at]) for at, made in enumerate(mades)]
    for copy in leaving:
        copy.start()
    for copy in leaving:
        copy.wait()


class Rounds:
    def __init__(self, blocks):
        self.blocks, self.arrived = blocks, []

    def exchange(self, flows, ending=(), small=None, ties=(), crossing=()):
        known, reads, sends, sizes = Reads(), [], [], {}

        def room(letter, size):
            place = sizes.get(letter, 0)
            sizes[letter] = place + size
            return list(sizes).index(letter), place

        def read(flow, index, skipped):
            shape = flow.wide[0].shape
            open_sizes, order = flow.order(shape)
            size = len(order)
            wide = [(known.at(array), tuple(slice(None) if at is None else at for at in index)) for array in flow.wide]
            reads.append((wide, open_sizes, [(known.at(array), start + skipped * size) for array, start in flow.terms], size))
            return size, order

        moved = []
        for flow in flows:
            letter, flow.stages = flow.stages[0], flow.stages[1:]
            size, order = read(flow, flow.halve(), 1)
            out, place = room(letter, size)
            sends.append((out, place, order))
            moved.append((flow.terms, letter, place))
        tile = flows[0].tile
        width = 3 * tile[1]
        for pair in ending:
            for flow in pair:
                read(flow, flow.index, 0)
        column_count = len(reads) - len(sends)
        ends = [room(letter, 3) for letter in "uvw"] if column_count else []
        mode, small_terms, small_ins, small_ends = "", [], [], []
        if small is not None:
            mode, letters = small.next()
            small_ins = small.parts if mode == "new" else [small.own]
            small_terms = [] if mode == "new" else known.places(small.terms)
            small_ends = [room(letter, 1) for letter in letters]
        order = list(sizes)
        outs = [jax.ShapeDtypeStruct((sizes[letter],) + tile, BF16) for letter in order]
        held = [pltpu.VMEM((sizes[letter],) + tile, BF16) for letter in order]
        for wide, open_sizes, terms, size in reads:
            held.append(pltpu.VMEM((len(wide), *open_sizes) + tile, BF16))
            if terms:
                held.append(pltpu.VMEM((len(terms), size) + tile, BF16))
        if small_terms:
            held.append(pltpu.VMEM((len(small_terms), 1) + tile, BF16))
        more = []
        if column_count:
            held.append(pltpu.VMEM((len(SHARD_ORDER), tile[0], width), F32))
            more.append(jax.ShapeDtypeStruct((tile[0], width), F32))
        if mode == "new":
            more.append(jax.ShapeDtypeStruct((24, width), F32))
        ties = [*self.arrived, *ties]
        copies = sum(len(wide) + len(terms) for wide, _, terms, _ in reads) + len(small_terms)
        anywhere, vmem = pl.BlockSpec(memory_space=pl.ANY), pl.BlockSpec(memory_space=pltpu.VMEM)
        plan = ([sizes[letter] for letter in order], reads, sends, column_count, ends, mode, small_terms, small_ends,
                len(known.arrays), len(small_ins), len(ties))
        made = list(pl.pallas_call(
            functools.partial(exchange_kernel, plan),
            out_shape=outs + more,
            in_specs=[pl.BlockSpec(memory_space=pltpu.SMEM)] + [anywhere] * len(known.arrays) + [vmem] * len(small_ins)
            + [anywhere] * len(ties),
            out_specs=[anywhere] * len(outs) + [vmem] * len(more),
            scratch_shapes=held + [pltpu.SemaphoreType.DMA((copies,)), pltpu.SemaphoreType.DMA((len(outs),))],
            compiler_params=pltpu.CompilerParams(vmem_limit_bytes=VMEM_BYTES),
        )(self.blocks, *known.arrays, *small_ins, *ties))
        rest = made[len(outs):]
        self.made = made[:len(outs)]
        going = lax.optimization_barrier(self.made + [send for _, send in crossing])
        arrived = {letter: swap(value, *LINKS[letter]) for letter, value in zip(order, going)}
        self.arrived = list(arrived.values())
        for (crossed, _), send in zip(crossing, going[len(outs):]):
            self.cross(crossed, send)
        for terms, letter, place in moved:
            terms.append((arrived[letter], place))
        for pair in ending:
            pair[0].own = rest.pop(0)
            pair[0].far = [(arrived[letter], place) for letter, (_, place) in zip("uvw", ends)]
        if mode:
            if mode == "new":
                small.own = rest.pop(0)
            small.terms += [(arrived[letter], place) for letter, (_, place) in zip(letters, small_ends)]

    def cross(self, flows, send):
        arrived = swap(send, *LINKS["c"])
        self.arrived.append(arrived)
        for flow in flows:
            flow.wide.append(arrived.reshape(flow.wide[0].shape))


class Small:
    def __init__(self, parts):
        self.parts, self.terms, self.stages = parts, [], ["c", "x", "y", "uvw"]

    def next(self):
        letters = self.stages.pop(0)
        return ("new" if letters == "c" else "old"), letters


def finish_kernel(plan, array_count, blocks, *refs):
    wides, feeds, far, small = plan
    arrays, refs = refs[:array_count], refs[array_count:]
    owns, small_own, refs = refs[:2], refs[2], refs[3:]
    up, down, *attends = refs[:6]
    smalls, gate, hidden = refs[6:11], refs[11], refs[12]
    held_wide, held, held_far, held_small, sems = refs[13:]
    copies = []

    def fetch(array, place, size, target):
        copies.append(pltpu.make_async_copy(arrays[array].at[pl.ds(place, size)], target, sems.at[len(copies)]))
        copies[-1].start()

    for layer, term, array in wides:
        copies.append(pltpu.make_async_copy(
            arrays[array].at[0, 0, :, :, 0, 0], held_wide.at[layer, term], sems.at[len(copies)]))
        copies[-1].start()
    for layer, part, term, array, place in feeds:
        fetch(array, place, 2, held.at[layer, part, term])
    for layer, other, array, place in far:
        fetch(array, place, 3, held_far.at[layer, other])
    for term, (array, place) in enumerate(small):
        fetch(array, place, 1, held_small.at[term])
    for copy in copies:
        copy.wait()
    terms, tile = held.shape[2], held.shape[5]
    for layer in range(2):
        for part in range(3):
            total = held_wide[layer, 0, part].astype(F32) + held_wide[layer, 1, part].astype(F32)
            for term in range(terms):
                total = total + held[layer, part, term].astype(F32)
            up[layer, :, part * tile:(part + 1) * tile] = total[0]
            down[layer, :, part * tile:(part + 1) * tile] = total[1]
        total = owns[layer][...]
        for other in range(3):
            total = total + jnp.concatenate([held_far[layer, other, cut].astype(F32) for cut in range(3)], axis=1)
        share = total.shape[1] // 4
        for at, out in enumerate(attends):
            out[layer] = total[:, at * share:(at + 1) * share]
    total = small_own[...]
    for term in range(len(small)):
        total = total + from_block(held_small[term, 0])
    lines = total.shape[1] // 8
    mine = jnp.where(blocks[0] == 0, total[:, :lines], 0.0)
    for place in range(1, 8):
        mine = mine + jnp.where(blocks[0] == place, total[:, place * lines:(place + 1) * lines], 0.0)
    for layer in range(2):
        base = 10 * layer
        for row, out in zip((3, 4, 1, 2, 0), smalls):
            out[layer:layer + 1] = mine[base + row:base + row + 1]
        shard = jnp.zeros((1, total.shape[1]), F32)
        for at in range(4):
            shard = shard + jnp.where(blocks[8] == at, total[base + 6 + at:base + 7 + at], 0.0)
        hidden[layer:layer + 1] = shard
    gate[...] = mine[5:6]


def finish(feeds, attends, small, blocks):
    reads = Reads()
    wide_plan = [(layer, term, reads.at(array)) for layer, flows in enumerate(feeds)
                 for term, array in enumerate(flows[0].wide)]
    feed_plan = [(layer, part, term, reads.at(array), place) for layer, flows in enumerate(feeds)
                 for part, flow in enumerate(flows) for term, (array, place) in enumerate(flow.terms)]
    far_plan = [(layer, other, reads.at(array), place) for layer, pair in enumerate(attends)
                for other, (array, place) in enumerate(pair[0].far)]
    small_plan = reads.places(small.terms)
    rows, tile = feeds[0][0].tile
    width, terms = 3 * tile, len(feeds[0][0].terms)
    anywhere, vmem = pl.BlockSpec(memory_space=pl.ANY), pl.BlockSpec(memory_space=pltpu.VMEM)
    return pl.pallas_call(
        functools.partial(finish_kernel, (wide_plan, feed_plan, far_plan, small_plan), len(reads.arrays)),
        out_shape=[jax.ShapeDtypeStruct((2, rows, width), F32)] * 2
        + [jax.ShapeDtypeStruct((2, rows, width // 4), F32)] * 4 + [jax.ShapeDtypeStruct((2, rows), F32)] * 5
        + [jax.ShapeDtypeStruct((1, rows), F32), jax.ShapeDtypeStruct((2, width), F32)],
        in_specs=[pl.BlockSpec(memory_space=pltpu.SMEM)] + [anywhere] * len(reads.arrays) + [vmem] * 3,
        out_specs=[vmem] * 13,
        scratch_shapes=[pltpu.VMEM((2, 2, 3, 2, rows, tile), BF16), pltpu.VMEM((2, 3, terms, 2, rows, tile), BF16),
                        pltpu.VMEM((2, 3, 3, rows, tile), BF16),
                        pltpu.VMEM((len(small_plan), 1, rows, tile), BF16),
                        pltpu.SemaphoreType.DMA((len(wide_plan) + len(feed_plan) + len(far_plan) + len(small_plan),))],
        compiler_params=pltpu.CompilerParams(vmem_limit_bytes=VMEM_BYTES),
    )(blocks, *reads.arrays, attends[0][0].own, attends[1][0].own, small.own)


def eighths(weights):
    return weights.reshape(weights.shape[:-2] + (2, 2, 2, weights.shape[-2] // 8, weights.shape[-1]))


def in_order(bit, own, other):
    first = (lax.axis_index("dp") & bit) == 0
    return jnp.stack([jnp.where(first, own, other), jnp.where(first, other, own)])


def far_pieces(layer, w_up, w_down, tails, halves, crossed, blocks):
    arrays = [eighths(w_up), eighths(w_down)] + halves + crossed
    every, rest = slice(None), pl.ds(1, len(tails) - 1)
    plan = [(kind, layer, kind, lambda me: (every, every, every, 0)) for kind in range(2)]
    for core in range(2):
        for second in range(2):
            plan.append((2 + 4 * core + second, None, 0, lambda me, core=core, second=second: (
                ((me >> 2) & 1) ^ second, every, (me & 1) ^ core, rest)))
            plan.append((4 + 4 * core + second, None, 1, lambda me, core=core, second=second: (
                every, ((me >> 1) & 1) ^ second, (me & 1) ^ core, rest)))
    return Pieces(arrays, plan, blocks, tails)


def gathered_pieces(layer, w_up, w_down, b_up, blocks):
    arrays = [eighths(lax.all_gather(weights[layer], "mp")) for weights in (w_up, w_down)]
    shards = arrays[0].shape[0]
    plan = [(kind, at, kind, lambda me, at=at: (slice(None),) * 3 + (at,)) for at in range(shards) for kind in range(2)]
    bias = lax.all_gather(b_up[layer:layer + 1], "mp")
    return Pieces(arrays, plan, blocks, [bias_terms(bias[at]) for at in range(shards)])


def sum_feed_anywhere(grads):
    both = lax.psum_scatter(grads, "mp", scatter_dimension=0, tiled=True)[0]
    both = lax.psum_scatter(both.astype(F32), "dp", scatter_dimension=1, tiled=True)
    return both[0], both[1].T


def sum_attend_anywhere(grads):
    whole = lax.psum_scatter(grads, "mp", scatter_dimension=2, tiled=True)
    return lax.psum_scatter(whole.astype(F32), "dp", scatter_dimension=1, tiled=True)


def shards(inputs, slot_valid, ln1_gain, ln1_bias, w_query, w_key, w_value, w_out, gate_logit,
           ln2_gain, ln2_bias, w_up, b_up, w_down, b_down, cotangent):
    pages, slots, width = inputs.shape
    dp, mp = lax.axis_size("dp"), lax.axis_size("mp")
    paired = dp == 8 and mp == 4 and width % (16 * dp) == 0
    if paired:
        blocks = jnp.concatenate([
            lax.axis_index("dp") ^ jnp.arange(8, dtype=jnp.int32),
            lax.axis_index("mp") ^ jnp.array(SHARD_ORDER, jnp.int32)])
    else:
        blocks = jnp.arange(2, dtype=jnp.int32)

    own_valid = lax.dynamic_slice_in_dim(slot_valid, lax.axis_index("mp") * pages, pages, 0) == 1
    key_text = lax.broadcasted_iota(jnp.int32, (slots, slots), 0) < TEXT
    query_text = lax.broadcasted_iota(jnp.int32, (slots, slots), 1) < TEXT
    live = jnp.broadcast_to(own_valid[:, :, None], (pages, slots, slots))
    masks = [
        jnp.where(jnp.logical_and(live, (key_text != query_text)[None]), 0.0, -1e30).astype(F32),
        jnp.where(live, 0.0, -1e30).astype(F32),
    ]
    gate = gate_logit[None]
    weights = (w_query, w_key, w_value, w_out)
    first_rows = inputs.reshape(pages * slots, width)
    cotangent = cotangent.reshape(pages * slots, width)
    got = {"grad": None}

    def attend_layer(layer, rows, ties):
        return attend(layer, layer == 0, rows, masks[layer], ln1_gain, ln1_bias, gate, weights, ties)

    def feed_layer(layer, rows, pieces, ties):
        return feed(layer, rows, ln2_gain, ln2_bias, b_down, pieces, (F32, BF16)[layer], ties)

    def feed_back_layer(layer, ties):
        rows, active, slope, pieces = got["feed", layer]
        got["mixed_grad"], got["feed_sums", layer], got["up_sums", layer], *got["feed_grads", layer] = feed_back(
            layer, (got["grad"], cotangent)[layer], rows, ln2_gain, ln2_bias, active, slope, pieces, not paired, ties)

    def attend_back_layer(layer, ties):
        rows, kept = got["attend", layer]
        got["grad"], got["attend_sums", layer], *got["attend_grads", layer] = attend_back(
            layer, layer == 0, got["mixed_grad"], rows, ln1_gain, ln1_bias, gate, (*kept[:5], *kept[6:]), weights,
            blocks, not paired, ties)

    if paired:
        owns = pack(w_up, w_down, b_up, blocks)
        rows = width // 8
        chain = Chain(owns[0])
        far = lambda own: [swap(own, "mp", other) for other in SHARD_ORDER[1:]]
        split = lambda pieces: (jnp.stack([piece[:rows] for piece in pieces]),
                                jnp.stack([piece[rows:2 * rows] for piece in pieces]))
        other_core = lambda *values: [swap(value, "dp", 1) for value in values]

        far_0 = far(owns[0])
        kept_0 = list(attend_layer(0, first_rows, ()))
        chain.need((kept_0, 5))
        far_0 = list(chain.tie(*far_0))
        ups, downs = chain.tie(*split(far_0))
        near_0 = [swap(ups, "dp", 2), swap(downs, "dp", 4)]
        far_1 = far(chain.tie(owns[1]))
        near_0 = chain.tie(*near_0)
        ups_0, downs_0 = chain.tie(in_order(2, ups, near_0[0]), in_order(4, downs, near_0[1]))
        side_0 = [swap(ups_0, "dp", 4), swap(downs_0, "dp", 2)]
        ups_0, downs_0, *side_0 = chain.tie(ups_0, downs_0, *side_0)
        far_1 = list(chain.tie(*far_1))
        ups, downs = chain.tie(*split(far_1))
        near_1 = [swap(ups, "dp", 2), swap(downs, "dp", 4)]
        core_0 = other_core(ups_0, side_0[0], downs_0, side_0[1])
        pieces_0 = far_pieces(0, w_up, w_down, [owns[0]] + far_0, [ups_0, side_0[0], downs_0, side_0[1]], core_0, blocks)
        fed_0 = list(feed_layer(0, kept_0[5], pieces_0, chain.ties()))
        chain.need((fed_0, 0))
        near_1 = chain.tie(*near_1)
        result_0, active_0, slope_0 = fed_0
        ups_1, downs_1 = chain.tie(in_order(2, ups, near_1[0]), in_order(4, downs, near_1[1]))
        side_1 = [swap(ups_1, "dp", 4), swap(downs_1, "dp", 2)]
        kept_1 = list(attend_layer(1, result_0, chain.ties()))
        chain.need((kept_1, 5))
        side_1 = chain.tie(*side_1)
        core_1 = other_core(ups_1, side_1[0], downs_1, side_1[1])
        pieces_1 = far_pieces(1, w_up, w_down, [owns[1]] + far_1, [ups_1, side_1[0], downs_1, side_1[1]], core_1, blocks)
    else:
        pieces_0 = gathered_pieces(0, w_up, w_down, b_up, blocks)
        pieces_1 = gathered_pieces(1, w_up, w_down, b_up, blocks)
        kept_0 = attend_layer(0, first_rows, ())
        result_0, active_0, slope_0 = feed_layer(0, kept_0[5], pieces_0, ())
        kept_1 = attend_layer(1, result_0, ())

    result_1, active_1, slope_1 = feed_layer(1, kept_1[5], pieces_1, ())
    got["feed", 0] = kept_0[5], active_0, slope_0, pieces_0
    got["feed", 1] = kept_1[5], active_1, slope_1, pieces_1
    got["attend", 0], got["attend", 1] = (first_rows, kept_0), (result_0, kept_1)

    if paired:
        rounds = Rounds(blocks)
        feed_back_layer(1, ())
        feeds, attends = {1: feed_flows(got["feed_grads", 1])}, {}
        rounds.cross(feeds[1], got["feed_grads", 1][1])
        attend_back_layer(1, ())
        attends[1] = attend_flows(got["attend_grads", 1])
        rounds.exchange(feeds[1], ties=[got["attend_sums", 1]], crossing=[(attends[1], got["attend_grads", 1][1])])
        feed_back_layer(0, rounds.made)
        feeds[0] = feed_flows(got["feed_grads", 0])
        rounds.exchange(feeds[1] + attends[1], ties=[got["feed_sums", 0]], crossing=[(feeds[0], got["feed_grads", 0][1])])
        attend_back_layer(0, rounds.made)
        attends[0] = attend_flows(got["attend_grads", 0])
        small = Small([got[name, layer] for layer in (0, 1) for name in ("feed_sums", "attend_sums", "up_sums")])
        rounds.exchange(feeds[0] + feeds[1] + attends[1], small=small, crossing=[(attends[0], got["attend_grads", 0][1])])
        rounds.exchange(feeds[0] + attends[0] + feeds[1], [attends[1]], small)
        rounds.exchange(feeds[0] + attends[0], small=small)
        rounds.exchange(feeds[0], [attends[0]], small)
        up_grad, down_turned, *rest = finish([feeds[0], feeds[1]], [attends[0], attends[1]], small, blocks)
        down_grad = jnp.swapaxes(down_turned, 1, 2)
        attend_grads, small_grads, gate_grad, bup_grad = rest[:4], rest[4:9], rest[9][0], rest[10]
    else:
        for layer in (1, 0):
            feed_back_layer(layer, ())
            attend_back_layer(layer, ())
        feed_grads = [sum_feed_anywhere(got["feed_grads", layer][0]) for layer in (0, 1)]
        up_grad, down_grad = (jnp.stack([feed_grads[layer][at] for layer in (0, 1)]) for at in range(2))
        sums = [sum_attend_anywhere(got["attend_grads", layer][0]) for layer in (0, 1)]
        attend_grads = [jnp.stack([sums[0][at], sums[1][at]]) for at in range(4)]
        both = lax.psum(jnp.concatenate([part for layer in (0, 1) for part in (
            got["feed_sums", layer][:3], got["attend_sums", layer][:3], got["up_sums", layer][:, 0])]), ("dp", "mp"))
        later, lines, me = both.shape[0] // 2, width // dp, lax.axis_index("mp")
        mine = lax.dynamic_slice_in_dim(both, lax.axis_index("dp") * lines, lines, 1)
        small_grads = [jnp.stack([mine[row], mine[later + row]]) for row in (3, 4, 1, 2, 0)]
        gate_grad = mine[5]
        bup_grad = jnp.concatenate([lax.dynamic_slice_in_dim(both, row + me, 1, 0) for row in (6, later + 6)])

    return (
        result_1.reshape(pages, slots, width),
        got["grad"].reshape(pages, slots, width),
        small_grads[0],
        small_grads[1],
        *attend_grads,
        gate_grad,
        small_grads[2],
        small_grads[3],
        up_grad,
        bup_grad,
        down_grad,
        small_grads[4],
    )


def solution(mesh):
    rows = P(("dp", "mp"), None, None)
    return jax.shard_map(
        shards,
        mesh=mesh,
        in_specs=(rows, P("dp", None), P(), P(), P(), P(), P(), P(), P(), P(), P(), P(None, None, "mp"),
                  P(None, "mp"), P(None, "mp", None), P(), rows),
        out_specs=(rows, rows, P(None, "dp"), P(None, "dp"), P(None, "dp", "mp"), P(None, "dp", "mp"),
                   P(None, "dp", "mp"), P(None, "dp", "mp"), P("dp"), P(None, "dp"), P(None, "dp"),
                   P(None, "dp", "mp"), P(None, "mp"), P(None, "mp", "dp"), P(None, "dp")),
        check_vma=False,
    )
```

time: 396 us -> 374 us (0.944)
  the two profiles are of different devices: /device:TPU:0 before, /device:TPU:9 now
where the time goes in v3:
time: 374 us; the launch traced here: 368 us
  Pallas kernels  149 us (40%)
  waiting for transfers between devices  141 us (38%)
  starting transfers between devices  53.5 us (14%)
  local copies, waits for them, and re-layouts  17.2 us (5%)
  other arithmetic  5.66 us (2%)
    ppermute x48, waiting for transfers between devices, swap(): return lax.ppermute(value, axis, [(at, at ^ bit) for at in range(size)])  141 us
    ppermute x48, starting transfers between devices, swap(): return lax.ppermute(value, axis, [(at, at ^ bit) for at in range(size)])  53.5 us
    pallas_call x2, Pallas kernels, feed_back(): pl.pallas_call(functools.partial(feed_back_kernel, layer, pieces, joint,...  34.1 us
    pallas_call x6, Pallas kernels, exchange(): pl.pallas_call(functools.partial(exchange_kernel, plan), out_shape=outs +...  34.1 us
    pallas_call x2, Pallas kernels, attend_back(): pl.pallas_call(body, out_shape=[jax.ShapeDtypeStruct((rows, width), F32),...  30.6 us
    pallas_call x2, Pallas kernels, feed(): pl.pallas_call(functools.partial(feed_kernel, layer, pieces, len(ties)),...  25.6 us
    pallas_call x2, Pallas kernels, attend(): pl.pallas_call(body, out_shape=outs, in_specs=[vmem] * 5 + [pl.BlockSpec(...  16.7 us
    unnamed x102, local copies, waits for them, and re-layouts  15.7 us
  transfers between devices with their start and end apart: 48, of which 26 were waited for; matrix products, arithmetic and copies ran while one was open for 1% of the time, Pallas kernels for 21%

profile of v3, /device:TPU:9, one launch (start us, length us, event | category | flops | bytes accessed | tf_op | source)
XLA Modules:
  0.0 368.0 jit_solution(9513241964353295817)
XLA Ops:
  10.5 8.3 %shard_map.281 = (bf16[384,768]{1,0:T(8,128)(2,1)}, bf16[384,768]{1,0:T(8,128)(2,1)}, bf16[384,768]{1,0:T(8,128)(2,1)}, bf16[3,6,256,128]{3,2,1,0:T(8,128)(2,1)}...) custom-call(bf16[384,768]{1,0:T(8,128)(2,1)} %bitcast.96, ...), custom_call_target="tpu_custom_call" | custom-call | flops 1811939328 | bytes 14680064 | tf_op jit(solution)/shard_map/pallas_call | solution.py:167
  22.4 10.8 %collective-permute-done.rest_1_ = bf16[208,768]{1,0:T(8,128)(2,1)S(1)} collective-permute-done((bf16[208,768]{1,0:T(8,128)(2,1)}, bf16[208,768]{1,0:T(8,128)(2,1)S(1)}, u32[]{:S(2)}, u32[]{:S(2)}) %collective-permute-start) | collective-permute-done | bytes 319520 | tf_op jit(solution)/shard_map/ppermute | solution.py:566
  35.8 7.7 %collective-permute-done.6 = bf16[3,96,768]{2,1,0:T(8,128)(2,1)S(1)} collective-permute-done((bf16[3,96,768]{2,1,0:T(8,128)(2,1)S(1)}, bf16[3,96,768]{2,1,0:T(8,128)(2,1)S(1)}, u32[]{:S(2)}, u32[]{:S(2)}) %collective-permute-start.6) | collective-permute-done | bytes 442400 | tf_op jit(solution)/shard_map/ppermute | solution.py:566
  50.9 12.4 %collective-permute-done.8.rest_7_.rest_3_ = bf16[2,3,96,768]{3,2,1,0:T(8,128)(2,1)S(1)} collective-permute-done((bf16[2,3,96,768]{3,2,1,0:T(8,128)(2,1)S(1)}, bf16[2,3,96,768]{3,2,1,0:T(8,128)(2,1)S(1)}, u32[]{:S(2)}, u32[]{:S(2)}) %collective-permute-start.8) | collective-permute-done | bytes 884768 | tf_op jit(solution)/shard_map/ppermute | solution.py:566
  68.9 6.3 %collective-permute-start.12 = (bf16[2,3,96,768]{3,2,1,0:T(8,128)(2,1)S(1)}, bf16[2,3,96,768]{3,2,1,0:T(8,128)(2,1)S(1)}, u32[]{:S(2)}, u32[]{:S(2)}) collective-permute-start(bf16[2,3,96,768]{3,2,1,0:T(8,128)(2,1)S(1)} %pad_maximum_fusion.rest_6_.rest_2_), channel_id=1, source_target_pairs={{0,4},{4,0},{8,12},{12,8},{16,20},{20,16},{24,28},{28,24},{1,5},{5... | collective-permute-start | bytes 2654216 | tf_op jit(solution)/shard_map/ppermute | solution.py:566
  82.0 13.0 %shard_map.282 = (f32[384,768]{1,0:T(8,128)}, bf16[4,384,768]{2,1,0:T(8,128)(2,1)}, bf16[4,384,768]{2,1,0:T(8,128)(2,1)}) custom-call(s32[12]{0:T(128)} %pad_add_fusion.block.blocks.refs_0_, f32[384,768]{1,0:T(8,128)} %get-tuple-element.178.mixed, f32[2,768]{1,0:T(2,128)} %gain.7, f32[2,768]{1,0:T(2,128)} %shift.7, f32[2,768]{1,0:T(2,128)} %b_down.3, ...), custom_call_target="tpu_custom_call" | custom-call | flops 3623878656 | bytes 20971520 | tf_op jit(solution)/shard_map/pallas_call | solution.py:258
  100.7 8.4 %shard_map.283 = (bf16[384,768]{1,0:T(8,128)(2,1)}, bf16[384,768]{1,0:T(8,128)(2,1)}, bf16[384,768]{1,0:T(8,128)(2,1)}, bf16[3,6,256,128]{3,2,1,0:T(8,128)(2,1)}...) custom-call(f32[384,768]{1,0:T(8,128)} %get-tuple-element.190.refs_0_.refs_2_, f32[3,128,128]{2,1,0:T(8,128)} %broadcast_in_dim.32.refs_1_, ...), custom_call_target="tpu_custom_call" | custom-call | flops 1811939328 | bytes 14680064 | tf_op jit(solution)/shard_map/pallas_call | solution.py:167
  109.1 9.3 %collective-permute-done.16.rest_7_.rest_3_ = bf16[2,3,96,768]{3,2,1,0:T(8,128)(2,1)S(1)} collective-permute-done((bf16[2,3,96,768]{3,2,1,0:T(8,128)(2,1)S(1)}, bf16[2,3,96,768]{3,2,1,0:T(8,128)(2,1)S(1)}, u32[]{:S(2)}, u32[]{:S(2)}) %collective-permute-start.16) | collective-permute-done | bytes 884768 | tf_op jit(solution)/shard_map/ppermute | solution.py:566
  124.2 12.6 %shard_map.284 = (bf16[384,768]{1,0:T(8,128)(2,1)}, bf16[4,384,768]{2,1,0:T(8,128)(2,1)}, bf16[4,384,768]{2,1,0:T(8,128)(2,1)}) custom-call(s32[12]{0:T(128)} %pad_add_fusion.block.blocks.refs_0_, f32[384,768]{1,0:T(8,128)} %get-tuple-element.192.mixed, f32[2,768]{1,0:T(2,128)} %gain.7, f32[2,768]{1,0:T(2,128)} %shift.7, f32[2,768]{1,0:T(2,128)} %b_down.3, ...), custom_call_target="tpu_custom_call" | custom-call | flops 3623878656 | bytes 20971520 | tf_op jit(solution)/shard_map/pallas_call | solution.py:258
  136.8 17.2 %shard_map.285 = (f32[384,768]{1,0:T(8,128)}, f32[8,768]{1,0:T(8,128)}, f32[4,1,768]{2,1,0:T(1,128)}, bf16[4,3,2,2,2,96,256]{6,5,4,3,2,1,0:T(8,128)(2,1)}, bf16[4,3,2,2,2,96,256]{6,5,4,3,2,1,0:T(8,128)(2,1)}) custom-call(s32[12]{0:T(128)} %pad_add_fusion.block.blocks.refs_0_, bf16[384,768]{1,0:T(8,128)(2,1)} %bitcast.99, ...), custom_call_target="tpu_custom_call" | custom-call | flops 7247757312 | bytes 31457280 | tf_op jit(solution)/shard_map/pallas_call | solution.py:361
  154.4 15.1 %shard_map.286 = (f32[384,768]{1,0:T(8,128)}, f32[8,768]{1,0:T(8,128)}, bf16[2,2,2,2,3,96,256]{6,5,4,3,2,1,0:T(8,128)(2,1)}, bf16[2,2,2,2,3,96,256]{6,5,4,3,2,1,0:T(8,128)(2,1)}) custom-call(s32[12]{0:T(128)} %pad_add_fusion.block.blocks.refs_0_, f32[384,768]{1,0:T(8,128)} %get-tuple-element.198.refs_1_, f32[384,768]{1,0:T(8,128)} %get-tuple-element.190.refs_0_.refs_2_, ...), custom_call_target="tpu_custom_call" | custom-call | flops 3623878656 | bytes 25165824 | tf_op jit(solution)/shard_map/pallas_call | solution.py:486
  181.8 17.0 %shard_map.288 = (f32[384,768]{1,0:T(8,128)}, f32[8,768]{1,0:T(8,128)}, f32[4,1,768]{2,1,0:T(1,128)}, bf16[4,3,2,2,2,96,256]{6,5,4,3,2,1,0:T(8,128)(2,1)}, bf16[4,3,2,2,2,96,256]{6,5,4,3,2,1,0:T(8,128)(2,1)}) custom-call(s32[12]{0:T(128)} %pad_add_fusion.block.blocks.refs_0_, f32[384,768]{1,0:T(8,128)} %get-tuple-element.204.grad_out, ...), custom_call_target="tpu_custom_call" | custom-call | flops 7247757312 | bytes 31457280 | tf_op jit(solution)/shard_map/pallas_call | solution.py:361
  209.3 15.5 %shard_map.290 = (f32[384,768]{1,0:T(8,128)}, f32[8,768]{1,0:T(8,128)}, bf16[2,2,2,2,3,96,256]{6,5,4,3,2,1,0:T(8,128)(2,1)}, bf16[2,2,2,2,3,96,256]{6,5,4,3,2,1,0:T(8,128)(2,1)}) custom-call(s32[12]{0:T(128)} %pad_add_fusion.block.blocks.refs_0_, f32[384,768]{1,0:T(8,128)} %get-tuple-element.213.refs_1_, bf16[384,768]{1,0:T(8,128)(2,1)} %bitcast.97, ...), custom_call_target="tpu_custom_call" | custom-call | flops 3623878656 | bytes 25165824 | tf_op jit(solution)/shard_map/pallas_call | solution.py:486
  224.8 5.9 %collective-permute-done.28.refs_7_.refs_22_.refs_12_.refs_16_ = bf16[20,96,256]{2,1,0:T(8,128)(2,1)S(1)} collective-permute-done((bf16[20,96,256]{2,1,0:T(8,128)(2,1)}, bf16[20,96,256]{2,1,0:T(8,128)(2,1)S(1)}, u32[]{:S(2)}, u32[]{:S(2)}) %collective-permute-start.28) | collective-permute-done | bytes 983072 | tf_op jit(solution)/shard_map/ppermute | solution.py:566
  233.5 7.2 %shard_map.291 = (bf16[26,96,256]{2,1,0:T(8,128)(2,1)}, bf16[26,96,256]{2,1,0:T(8,128)(2,1)}, bf16[16,96,256]{2,1,0:T(8,128)(2,1)}, bf16[4,96,256]{2,1,0:T(8,128...) custom-call(s32[12]{0:T(128)} %pad_add_fusion.block.blocks.refs_0_, ...), custom_call_target="tpu_custom_call" | custom-call | tf_op jit(solution)/shard_map/pallas_call | solution.py:783
  247.7 18.5 %collective-permute-done.35.refs_13_.refs_27_.refs_17_ = bf16[4,96,256]{2,1,0:T(8,128)(2,1)S(1)} collective-permute-done((bf16[4,96,256]{2,1,0:T(8,128)(2,1)}, bf16[4,96,256]{2,1,0:T(8,128)(2,1)S(1)}, u32[]{:S(2)}, u32[]{:S(2)}) %collective-permute-start.35) | collective-permute-done | bytes 196640 | tf_op jit(solution)/shard_map/ppermute | solution.py:566
  266.2 5.2 %collective-permute-done.31.refs_2_.refs_24_.refs_4_ = bf16[26,96,256]{2,1,0:T(8,128)(2,1)S(1)} collective-permute-done((bf16[26,96,256]{2,1,0:T(8,128)(2,1)}, bf16[26,96,256]{2,1,0:T(8,128)(2,1)S(1)}, u32[]{:S(2)}, u32[]{:S(2)}) %collective-permute-start.31) | collective-permute-done | bytes 1277984 | tf_op jit(solution)/shard_map/ppermute | solution.py:566
  273.6 7.7 %shard_map.292 = (bf16[20,96,256]{2,1,0:T(8,128)(2,1)}, bf16[13,96,256]{2,1,0:T(8,128)(2,1)}, bf16[21,96,256]{2,1,0:T(8,128)(2,1)}, bf16[7,96,256]{2,1,0:T(8,128...) custom-call(s32[12]{0:T(128)} %pad_add_fusion.block.blocks.refs_0_, ...), custom_call_target="tpu_custom_call" | custom-call | tf_op jit(solution)/shard_map/pallas_call | solution.py:783
  285.9 9.5 %collective-permute-done.41.refs_18_.refs_24_ = bf16[3,96,256]{2,1,0:T(8,128)(2,1)S(1)} collective-permute-done((bf16[3,96,256]{2,1,0:T(8,128)(2,1)}, bf16[3,96,256]{2,1,0:T(8,128)(2,1)S(1)}, u32[]{:S(2)}, u32[]{:S(2)}) %collective-permute-start.41) | collective-permute-done | bytes 147488 | tf_op jit(solution)/shard_map/ppermute | solution.py:566
  295.5 9.8 %collective-permute-done.40.refs_17_.refs_20_ = bf16[7,96,256]{2,1,0:T(8,128)(2,1)S(1)} collective-permute-done((bf16[7,96,256]{2,1,0:T(8,128)(2,1)}, bf16[7,96,256]{2,1,0:T(8,128)(2,1)S(1)}, u32[]{:S(2)}, u32[]{:S(2)}) %collective-permute-start.40) | collective-permute-done | bytes 344096 | tf_op jit(solution)/shard_map/ppermute | solution.py:566
  318.1 6.9 %collective-permute-done.42.refs_4_.refs_17_.refs_6_ = bf16[4,96,256]{2,1,0:T(8,128)(2,1)S(1)} collective-permute-done((bf16[4,96,256]{2,1,0:T(8,128)(2,1)}, bf16[4,96,256]{2,1,0:T(8,128)(2,1)S(1)}, u32[]{:S(2)}, u32[]{:S(2)}) %collective-permute-start.42) | collective-permute-done | bytes 196640 | tf_op jit(solution)/shard_map/ppermute | solution.py:566
  326.6 5.2 %shard_map.294 = (bf16[6,96,256]{2,1,0:T(8,128)(2,1)}, bf16[8,96,256]{2,1,0:T(8,128)(2,1)}, bf16[4,96,256]{2,1,0:T(8,128)(2,1)}, f32[96,768]{1,0:T(8,128)}) custom-call(s32[12]{0:T(128)} %pad_add_fusion.block.blocks.refs_0_, bf16[2,2,3,2,2,2,96,256]{7,6,5,4,3,2,1,0:T(8,128)(2,1)} %bitcast.81, bf16[2,2,3,2,2,2,96,256]{7,6,5,4,3,2,1,0:T(8,128)(2,1)} %bitcast.61, ...), custom_call_target="tpu_custom_call" | custom-call | tf_op jit(solution)/shard_map/pallas_call | solution.py:783
  335.9 25.7 %collective-permute-done.47.refs_23_ = bf16[4,96,256]{2,1,0:T(8,128)(2,1)S(1)} collective-permute-done((bf16[4,96,256]{2,1,0:T(8,128)(2,1)}, bf16[4,96,256]{2,1,0:T(8,128)(2,1)S(1)}, u32[]{:S(2)}, u32[]{:S(2)}) %collective-permute-start.47) | collective-permute-done | bytes 196640 | tf_op jit(solution)/shard_map/ppermute | solution.py:566
  362.5 5.2 %shard_map.295 = (f32[2,96,768]{2,1,0:T(8,128)}, f32[2,96,768]{2,1,0:T(8,128)}, f32[2,96,192]{2,1,0:T(8,128)}, f32[2,96,192]{2,1,0:T(8,128)}, f32[2,96,192]{2,1,...) custom-call(s32[12]{0:T(128)} %pad_add_fusion.block.blocks.refs_0_, ...), custom_call_target="tpu_custom_call" | custom-call | tf_op jit(solution)/shard_map/pallas_call | solution.py:894
  (216 shorter events, 106.1 us)
Async XLA Ops:
  8.3 24.9 %collective-permute-start = (bf16[208,768]{1,0:T(8,128)(2,1)}, bf16[208,768]{1,0:T(8,128)(2,1)S(1)}, u32[]{:S(2)}, u32[]{:S(2)}) collective-permute-start(bf16[208,768]{1,0:T(8,128)(2,1)} %get-tuple-element.189.rest_0_.rest_14_.refs_9_), channel_id=1, source_target_pairs={{0,2},{1,3},{2,0},{3,1},{4,6},{5,7},{6,4},{7,5},{8,10},{9,11},{10,... | collective-permute-start | bytes 958472 | tf_op jit(solution)/shard_map/ppermute | solution.py:566
  47.0 19.9 %collective-permute-start.4 = (bf16[208,768]{1,0:T(8,128)(2,1)S(1)}, bf16[208,768]{1,0:T(8,128)(2,1)S(1)}, u32[]{:S(2)}, u32[]{:S(2)}) collective-permute-start(bf16[208,768]{1,0:T(8,128)(2,1)S(1)} %copy-done.46), channel_id=1, source_target_pairs={{0,1},{1,0},{2,3},{3,2},{4,5},{5,4},{6,7},{7,6},{8,9},{9,8},{10,11... | collective-permute-start | bytes 958472 | tf_op jit(solution)/shard_map/ppermute | solution.py:566
  97.5 20.9 %collective-permute-start.16 = (bf16[2,3,96,768]{3,2,1,0:T(8,128)(2,1)S(1)}, bf16[2,3,96,768]{3,2,1,0:T(8,128)(2,1)S(1)}, u32[]{:S(2)}, u32[]{:S(2)}) collective-permute-start(bf16[2,3,96,768]{3,2,1,0:T(8,128)(2,1)S(1)} %pad_maximum_fusion.2.rest_6_.rest_2_), channel_id=1, source_target_pairs={{0,16},{4,20},{8,24},{12,28},{16,0},{20,4},{24,8},{28,12},{1,17},{... | collective-permute-start | bytes 2654216 | tf_op jit(solution)/shard_map/ppermute | solution.py:566
  97.9 20.5 %collective-permute-start.17 = (bf16[2,3,96,768]{3,2,1,0:T(8,128)(2,1)S(1)}, bf16[2,3,96,768]{3,2,1,0:T(8,128)(2,1)S(1)}, u32[]{:S(2)}, u32[]{:S(2)}) collective-permute-start(bf16[2,3,96,768]{3,2,1,0:T(8,128)(2,1)S(1)} %pad_maximum_fusion.3.rest_8_.rest_4_), channel_id=1, source_target_pairs={{0,8},{4,12},{8,0},{12,4},{16,24},{20,28},{24,16},{28,20},{1,9},{5... | collective-permute-start | bytes 2654216 | tf_op jit(solution)/shard_map/ppermute | solution.py:566
  98.9 21.0 %collective-permute-start.18 = (bf16[2,3,96,768]{3,2,1,0:T(8,128)(2,1)S(1)}, bf16[2,3,96,768]{3,2,1,0:T(8,128)(2,1)S(1)}, u32[]{:S(2)}, u32[]{:S(2)}) collective-permute-start(bf16[2,3,96,768]{3,2,1,0:T(8,128)(2,1)S(1)} %pad_maximum_fusion.2.rest_6_.rest_2_), channel_id=1, source_target_pairs={{0,4},{4,0},{8,12},{12,8},{16,20},{20,16},{24,28},{28,24},{1,5},{5... | collective-permute-start | bytes 2654216 | tf_op jit(solution)/shard_map/ppermute | solution.py:566
  99.9 20.1 %collective-permute-start.20 = (bf16[2,3,96,768]{3,2,1,0:T(8,128)(2,1)S(1)}, bf16[2,3,96,768]{3,2,1,0:T(8,128)(2,1)S(1)}, u32[]{:S(2)}, u32[]{:S(2)}) collective-permute-start(bf16[2,3,96,768]{3,2,1,0:T(8,128)(2,1)S(1)} %pad_maximum_fusion.3.rest_8_.rest_4_), channel_id=1, source_target_pairs={{0,4},{4,0},{8,12},{12,8},{16,20},{20,16},{24,28},{28,24},{1,5},{5... | collective-permute-start | bytes 2654216 | tf_op jit(solution)/shard_map/ppermute | solution.py:566
  176.4 22.5 %collective-permute-start.26 = (bf16[2,2,2,2,3,96,256]{6,5,4,3,2,1,0:T(8,128)(2,1)S(1)}, bf16[2,2,2,2,3,96,256]{6,5,4,3,2,1,0:T(8,128)(2,1)S(1)}, u32[]{:S(2)}, u32[]{:S(2)}) collective-permute-start(bf16[2,2,2,2,3,96,256]{6,5,4,3,2,1,0:T(8,128)(2,1)S(1)} %copy-done.50), channel_id=1, source_target_pairs={{0,4},{4,0},{8,12},{12,8},{16,20},{20,16},{24,28},{28,24},{1,5},{5... | collective-permute-start | bytes 7077896 | tf_op jit(solution)/shard_map/ppermute | solution.py:566
  176.6 22.1 %collective-permute-start.23 = (bf16[16,96,256]{2,1,0:T(8,128)(2,1)}, bf16[16,96,256]{2,1,0:T(8,128)(2,1)S(1)}, u32[]{:S(2)}, u32[]{:S(2)}) collective-permute-start(bf16[16,96,256]{2,1,0:T(8,128)(2,1)} %get-tuple-element.221.rest_10_), channel_id=1, source_target_pairs={{0,8},{4,12},{8,0},{12,4},{16,24},{20,28},{24,16},{28,20},{1,9},{5... | collective-permute-start | bytes 2359304 | tf_op jit(solution)/shard_map/ppermute | solution.py:566
  177.7 21.1 %collective-permute-start.24 = (bf16[16,96,256]{2,1,0:T(8,128)(2,1)}, bf16[16,96,256]{2,1,0:T(8,128)(2,1)S(1)}, u32[]{:S(2)}, u32[]{:S(2)}) collective-permute-start(bf16[16,96,256]{2,1,0:T(8,128)(2,1)} %get-tuple-element.222.rest_11_), channel_id=1, source_target_pairs={{0,16},{4,20},{8,24},{12,28},{16,0},{20,4},{24,8},{28,12},{1,17},{... | collective-permute-start | bytes 2359304 | tf_op jit(solution)/shard_map/ppermute | solution.py:566
  178.9 20.0 %collective-permute-start.25 = (bf16[16,96,256]{2,1,0:T(8,128)(2,1)}, bf16[16,96,256]{2,1,0:T(8,128)(2,1)S(1)}, u32[]{:S(2)}, u32[]{:S(2)}) collective-permute-start(bf16[16,96,256]{2,1,0:T(8,128)(2,1)} %get-tuple-element.223.rest_12_), channel_id=1, source_target_pairs={{0,1},{1,0},{2,3},{3,2},{4,5},{5,4},{6,7},{7,6},{8,9},{9,8},{10,11... | collective-permute-start | bytes 2359304 | tf_op jit(solution)/shard_map/ppermute | solution.py:566
  205.9 24.9 %collective-permute-start.27 = (bf16[4,3,2,2,2,96,256]{6,5,4,3,2,1,0:T(8,128)(2,1)}, bf16[4,3,2,2,2,96,256]{6,5,4,3,2,1,0:T(8,128)(2,1)S(1)}, u32[]{:S(2)}, u32[]{:S(2)}) collective-permute-start(bf16[4,3,2,2,2,96,256]{6,5,4,3,2,1,0:T(8,128)(2,1)} %get-tuple-element.233), channel_id=1, source_target_pairs={{0,4},{4,0},{8,12},{12,8},{16,20},{20,16},{24,28},{28,24},{1,5},{5... | collective-permute-start | bytes 14155784 | tf_op jit(solution)/shard_map/ppermute | solution.py:566
  207.2 23.5 %collective-permute-start.28 = (bf16[20,96,256]{2,1,0:T(8,128)(2,1)}, bf16[20,96,256]{2,1,0:T(8,128)(2,1)S(1)}, u32[]{:S(2)}, u32[]{:S(2)}) collective-permute-start(bf16[20,96,256]{2,1,0:T(8,128)(2,1)} %get-tuple-element.234.refs_16_), channel_id=1, source_target_pairs={{0,16},{4,20},{8,24},{12,28},{16,0},{20,4},{24,8},{28,12},{1,17},{... | collective-permute-start | bytes 2949128 | tf_op jit(solution)/shard_map/ppermute | solution.py:566
  207.4 23.3 %collective-permute-start.30 = (bf16[20,96,256]{2,1,0:T(8,128)(2,1)}, bf16[20,96,256]{2,1,0:T(8,128)(2,1)S(1)}, u32[]{:S(2)}, u32[]{:S(2)}) collective-permute-start(bf16[20,96,256]{2,1,0:T(8,128)(2,1)} %get-tuple-element.236.refs_18_), channel_id=1, source_target_pairs={{0,8},{4,12},{8,0},{12,4},{16,24},{20,28},{24,16},{28,20},{1,9},{5... | collective-permute-start | bytes 2949128 | tf_op jit(solution)/shard_map/ppermute | solution.py:566
  240.6 30.8 %collective-permute-start.34 = (bf16[2,2,2,2,3,96,256]{6,5,4,3,2,1,0:T(8,128)(2,1)}, bf16[2,2,2,2,3,96,256]{6,5,4,3,2,1,0:T(8,128)(2,1)S(1)}, u32[]{:S(2)}, u32[]{:S(2)}) collective-permute-start(bf16[2,2,2,2,3,96,256]{6,5,4,3,2,1,0:T(8,128)(2,1)} %get-tuple-element.251), channel_id=1, source_target_pairs={{0,4},{4,0},{8,12},{12,8},{16,20},{20,16},{24,28},{28,24},{1,5},{5... | collective-permute-start | bytes 7077896 | tf_op jit(solution)/shard_map/ppermute | solution.py:566
  241.6 29.9 %collective-permute-start.31 = (bf16[26,96,256]{2,1,0:T(8,128)(2,1)}, bf16[26,96,256]{2,1,0:T(8,128)(2,1)S(1)}, u32[]{:S(2)}, u32[]{:S(2)}) collective-permute-start(bf16[26,96,256]{2,1,0:T(8,128)(2,1)} %get-tuple-element.247), channel_id=1, source_target_pairs={{0,8},{4,12},{8,0},{12,4},{16,24},{20,28},{24,16},{28,20},{1,9},{5... | collective-permute-start | bytes 3833864 | tf_op jit(solution)/shard_map/ppermute | solution.py:566
  241.9 29.5 %collective-permute-start.32 = (bf16[26,96,256]{2,1,0:T(8,128)(2,1)}, bf16[26,96,256]{2,1,0:T(8,128)(2,1)S(1)}, u32[]{:S(2)}, u32[]{:S(2)}) collective-permute-start(bf16[26,96,256]{2,1,0:T(8,128)(2,1)} %get-tuple-element.248), channel_id=1, source_target_pairs={{0,16},{4,20},{8,24},{12,28},{16,0},{20,4},{24,8},{28,12},{1,17},{... | collective-permute-start | bytes 3833864 | tf_op jit(solution)/shard_map/ppermute | solution.py:566
  243.0 23.2 %collective-permute-start.33 = (bf16[16,96,256]{2,1,0:T(8,128)(2,1)}, bf16[16,96,256]{2,1,0:T(8,128)(2,1)S(1)}, u32[]{:S(2)}, u32[]{:S(2)}) collective-permute-start(bf16[16,96,256]{2,1,0:T(8,128)(2,1)} %get-tuple-element.249), channel_id=1, source_target_pairs={{0,1},{1,0},{2,3},{3,2},{4,5},{5,4},{6,7},{7,6},{8,9},{9,8},{10,11... | collective-permute-start | bytes 2359304 | tf_op jit(solution)/shard_map/ppermute | solution.py:566
  281.3 24.9 %collective-permute-start.39 = (bf16[21,96,256]{2,1,0:T(8,128)(2,1)}, bf16[21,96,256]{2,1,0:T(8,128)(2,1)S(1)}, u32[]{:S(2)}, u32[]{:S(2)}) collective-permute-start(bf16[21,96,256]{2,1,0:T(8,128)(2,1)} %get-tuple-element.262), channel_id=1, source_target_pairs={{0,8},{4,12},{8,0},{12,4},{16,24},{20,28},{24,16},{28,20},{1,9},{5... | collective-permute-start | bytes 3096584 | tf_op jit(solution)/shard_map/ppermute | solution.py:566
  282.1 24.1 %collective-permute-start.37 = (bf16[20,96,256]{2,1,0:T(8,128)(2,1)}, bf16[20,96,256]{2,1,0:T(8,128)(2,1)S(1)}, u32[]{:S(2)}, u32[]{:S(2)}) collective-permute-start(bf16[20,96,256]{2,1,0:T(8,128)(2,1)} %get-tuple-element.260), channel_id=1, source_target_pairs={{0,16},{4,20},{8,24},{12,28},{16,0},{20,4},{24,8},{28,12},{1,17},{... | collective-permute-start | bytes 2949128 | tf_op jit(solution)/shard_map/ppermute | solution.py:566
  283.3 23.0 %collective-permute-start.38 = (bf16[13,96,256]{2,1,0:T(8,128)(2,1)}, bf16[13,96,256]{2,1,0:T(8,128)(2,1)S(1)}, u32[]{:S(2)}, u32[]{:S(2)}) collective-permute-start(bf16[13,96,256]{2,1,0:T(8,128)(2,1)} %get-tuple-element.261), channel_id=1, source_target_pairs={{0,1},{1,0},{2,3},{3,2},{4,5},{5,4},{6,7},{7,6},{8,9},{9,8},{10,11... | collective-permute-start | bytes 1916936 | tf_op jit(solution)/shard_map/ppermute | solution.py:566
  284.7 20.5 %collective-permute-start.40 = (bf16[7,96,256]{2,1,0:T(8,128)(2,1)}, bf16[7,96,256]{2,1,0:T(8,128)(2,1)S(1)}, u32[]{:S(2)}, u32[]{:S(2)}) collective-permute-start(bf16[7,96,256]{2,1,0:T(8,128)(2,1)} %get-tuple-element.263), channel_id=1, source_target_pairs={{0,2},{1,3},{2,0},{3,1},{4,6},{5,7},{6,4},{7,5},{8,10},{9,11},{10,... | collective-permute-start | bytes 1032200 | tf_op jit(solution)/shard_map/ppermute | solution.py:566
  331.9 29.7 %collective-permute-start.46 = (bf16[8,96,256]{2,1,0:T(8,128)(2,1)}, bf16[8,96,256]{2,1,0:T(8,128)(2,1)S(1)}, u32[]{:S(2)}, u32[]{:S(2)}) collective-permute-start(bf16[8,96,256]{2,1,0:T(8,128)(2,1)} %get-tuple-element.272), channel_id=1, source_target_pairs={{0,2},{1,3},{2,0},{3,1},{4,6},{5,7},{6,4},{7,5},{8,10},{9,11},{10,... | collective-permute-start | bytes 1179656 | tf_op jit(solution)/shard_map/ppermute | solution.py:566
  334.9 26.6 %collective-permute-start.45 = (bf16[6,96,256]{2,1,0:T(8,128)(2,1)}, bf16[6,96,256]{2,1,0:T(8,128)(2,1)S(1)}, u32[]{:S(2)}, u32[]{:S(2)}) collective-permute-start(bf16[6,96,256]{2,1,0:T(8,128)(2,1)} %get-tuple-element.271), channel_id=1, source_target_pairs={{0,1},{1,0},{2,3},{3,2},{4,5},{5,4},{6,7},{7,6},{8,9},{9,8},{10,11... | collective-permute-start | bytes 884744 | tf_op jit(solution)/shard_map/ppermute | solution.py:566
  334.9 26.6 %collective-permute-start.47 = (bf16[4,96,256]{2,1,0:T(8,128)(2,1)}, bf16[4,96,256]{2,1,0:T(8,128)(2,1)S(1)}, u32[]{:S(2)}, u32[]{:S(2)}) collective-permute-start(bf16[4,96,256]{2,1,0:T(8,128)(2,1)} %get-tuple-element.273), channel_id=1, source_target_pairs={{0,3},{1,2},{2,1},{3,0},{4,7},{5,6},{6,5},{7,4},{8,11},{9,10},{10,... | collective-permute-start | bytes 589832 | tf_op jit(solution)/shard_map/ppermute | solution.py:566
  (75 other events, 676.8 us)

commit v4 on v3

--- a/solution.py
+++ b/solution.py
@@ -11,7 +11,7 @@
 TEXT = 112
 F32 = jnp.float32
 BF16 = jnp.bfloat16
-VMEM_BYTES = 56 * 2**20
+VMEM_BYTES = 62 * 2**20
 
 
 def dot(a, b, a_dim, b_dim):
@@ -272,9 +272,8 @@
     )(pieces.blocks, mixed, gain, shift, b_down, *pieces.tails, *pieces.arrays, *ties)
 
 
-ROWS_FIRST = ((0, 4, 2, 6, 1, 5, 3, 7), (0, 2, 4, 6, 1, 3, 5, 7))
-PART_ORDERS = (0, 1, 0)
-PART_STAGES = ("xyvu", "yuxv", "uxyv")
+ROWS_ORDER = (0, 4, 2, 6, 1, 5, 3, 7)
+PART_STAGES = (("xyvu", "yuxv", "uxyv"), ("xyvu", "yuxv", "uxyv"))
 SHARD_ORDER = (0, 2, 1, 3)
 LINKS = {"c": ("dp", 1), "x": ("dp", 2), "y": ("dp", 4), "u": ("mp", 1), "v": ("mp", 2), "w": ("mp", 3)}
 
@@ -310,12 +309,12 @@
     wait = pieces.start_and_wait(refs, (up, down), blocks, sems)
 
     def put(kind, turned, right):
+        made = dot(turned[...], right, 1, 0).astype(BF16)
         if joint:
-            grads[0][0, kind] = dot(turned[0], right, 1, 0).astype(BF16)
+            grads[0][0, kind] = made
             return
         for at in range(3):
-            made = dot(turned[PART_ORDERS[at]], right[:, at * part:(at + 1) * part], 1, 0).astype(BF16)
-            put_blocks(made, *grads, lambda first, second: (0, at, kind, first, second))
+            put_blocks(made[:, at * part:(at + 1) * part], *grads, lambda first, second: (0, at, kind, first, second))
 
     @pl.when(step == 0)
     def _():
@@ -327,8 +326,7 @@
         normed = (white * gain[layer:layer + 1] + shift[layer:layer + 1]).astype(BF16)
         for value, turned in ((low[...], low_turned), (normed, normed_turned)):
             held[...] = value.T
-            for at in range(turned.shape[0]):
-                turn_rows(held, turned.at[at], blocks, None if joint else ROWS_FIRST[at])
+            turn_rows(held, turned, blocks, None if joint else ROWS_ORDER)
         total[...] = jnp.zeros_like(total)
 
     wait()
@@ -357,7 +355,7 @@
         grads = [(2, width, width)]
     else:
         grads = [(3, 2, 2, 2, width // 8, width // 3)] * 2
-    turned = pltpu.VMEM((1 if joint else 2, width, rows), BF16)
+    turned = pltpu.VMEM((width, rows), BF16)
     return pl.pallas_call(
         functools.partial(feed_back_kernel, layer, pieces, joint, len(ties)),
         grid=(shards,),
@@ -407,9 +405,9 @@
             put_blocks(made[:, col * tile:(col + 1) * tile], *grads,
                        lambda first, second: (at // 2, first, second, at % 2, col))
 
-    def turn(rows, order):
+    def turn(rows):
         turning[...] = rows.T
-        turn_rows(turning, turned, blocks, None if joint else ROWS_FIRST[order])
+        turn_rows(turning, turned, blocks, None if joint else ROWS_ORDER)
 
     grad = grad_mixed[...]
     if crossed:
@@ -418,7 +416,7 @@
         low = (grad * opened).astype(BF16)
     else:
         low = grad.astype(BF16)
-    turn(context[...], 1)
+    turn(context[...])
     put(3, low)
     gc[...] = dot(low, w_out[...], 1, 1).astype(BF16)
 
@@ -437,13 +435,11 @@
 
     white, inverse = whiten(resid[...].astype(F32))
     normed = (white * gain[layer:layer + 1] + shift[layer:layer + 1]).astype(BF16)
-    turn(normed, 1)
+    turn(normed)
     put(2, gv[...])
     if not joint:
         for made, out in zip(grads, outs):
             leaving.send(made.at[1], out.at[1])
-    if not joint:
-        turn_rows(turning, turned, blocks, ROWS_FIRST[0])
     put(0, gq[...])
     put(1, gk[...])
     for made, out in zip(grads, outs):
@@ -587,14 +583,16 @@
         return sizes, [tuple(place[ranked.index(dim)] for dim in open_dims) for place in places]
 
 
-def feed_flows(grads):
+def feed_flows(layer, grads):
     keep = grads[0].reshape((2, 2) + grads[0].shape[1:])
-    bits = ((4, 5, 1, 0), (4, 0, 5, 1), (0, 4, 5, 1))
-    return [Flow(keep, (None, None, at, None, None, None), bits[at], PART_STAGES[at]) for at in range(3)]
+    dims = {"u": 0, "v": 1, "x": 4, "y": 5}
+    return [Flow(keep, (None, None, at, None, None, None), tuple(dims[letter] for letter in stages), stages)
+            for at, stages in enumerate(PART_STAGES[layer])]
 
 
 def attend_flows(grads):
-    return [Flow(grads[0], (at, None, None, None, None), (1, 2), stages) for at, stages in enumerate(("xy", "yx"))]
+    return [Flow(grads[0], (at, None, None, None, None), bits, stages)
+            for at, (bits, stages) in enumerate((((1, 2), "xy"), ((2, 1), "yx")))]
 
 
 class Reads:
@@ -720,11 +718,25 @@
         copy.wait()
 
 
+def pause_kernel(source, out):
+    out[...] = jnp.zeros_like(out)
+
+
+def pause(value):
+    return pl.pallas_call(
+        pause_kernel,
+        out_shape=jax.ShapeDtypeStruct((8, 128), F32),
+        in_specs=[pl.BlockSpec(memory_space=pl.ANY)],
+        out_specs=pl.BlockSpec(memory_space=pltpu.VMEM),
+        compiler_params=pltpu.CompilerParams(vmem_limit_bytes=VMEM_BYTES),
+    )(value)
+
+
 class Rounds:
     def __init__(self, blocks):
         self.blocks, self.arrived = blocks, []
 
-    def exchange(self, flows, ending=(), small=None, ties=(), crossing=()):
+    def exchange(self, flows, ending=(), small=None, ties=(), crossing=(), alone=False):
         known, reads, sends, sizes = Reads(), [], [], {}
 
         def room(letter, size):
@@ -794,6 +806,8 @@
         going = lax.optimization_barrier(self.made + [send for _, send in crossing])
         arrived = {letter: swap(value, *LINKS[letter]) for letter, value in zip(order, going)}
         self.arrived = list(arrived.values())
+        if alone:
+            self.arrived.append(pause(going[0]))
         for (crossed, _), send in zip(crossing, going[len(outs):]):
             self.cross(crossed, send)
         for terms, letter, place in moved:
@@ -815,7 +829,7 @@
 
 class Small:
     def __init__(self, parts):
-        self.parts, self.terms, self.stages = parts, [], ["c", "x", "y", "uvw"]
+        self.parts, self.terms, self.stages = parts, [], ["c", "x", "uvw", "y"]
 
     def next(self):
         letters = self.stages.pop(0)
@@ -1041,21 +1055,21 @@
     if paired:
         rounds = Rounds(blocks)
         feed_back_layer(1, ())
-        feeds, attends = {1: feed_flows(got["feed_grads", 1])}, {}
+        feeds, attends = {1: feed_flows(1, got["feed_grads", 1])}, {}
         rounds.cross(feeds[1], got["feed_grads", 1][1])
         attend_back_layer(1, ())
         attends[1] = attend_flows(got["attend_grads", 1])
         rounds.exchange(feeds[1], ties=[got["attend_sums", 1]], crossing=[(attends[1], got["attend_grads", 1][1])])
         feed_back_layer(0, rounds.made)
-        feeds[0] = feed_flows(got["feed_grads", 0])
+        feeds[0] = feed_flows(0, got["feed_grads", 0])
         rounds.exchange(feeds[1] + attends[1], ties=[got["feed_sums", 0]], crossing=[(feeds[0], got["feed_grads", 0][1])])
         attend_back_layer(0, rounds.made)
         attends[0] = attend_flows(got["attend_grads", 0])
         small = Small([got[name, layer] for layer in (0, 1) for name in ("feed_sums", "attend_sums", "up_sums")])
-        rounds.exchange(feeds[0] + feeds[1] + attends[1], small=small, crossing=[(attends[0], got["attend_grads", 0][1])])
-        rounds.exchange(feeds[0] + attends[0] + feeds[1], [attends[1]], small)
-        rounds.exchange(feeds[0] + attends[0], small=small)
-        rounds.exchange(feeds[0], [attends[0]], small)
+        rounds.exchange(feeds[0] + feeds[1] + attends[1], small=small, crossing=[(attends[0], got["attend_grads", 0][1])], alone=True)
+        rounds.exchange(feeds[0] + attends[0] + feeds[1], [attends[1]], small, alone=True)
+        rounds.exchange(feeds[0] + attends[0], small=small, alone=True)
+        rounds.exchange(feeds[0], [attends[0]], small, alone=True)
         up_grad, down_turned, *rest = finish([feeds[0], feeds[1]], [attends[0], attends[1]], small, blocks)
         down_grad = jnp.swapaxes(down_turned, 1, 2)
         attend_grads, small_grads, gate_grad, bup_grad = rest[:4], rest[4:9], rest[9][0], rest[10]

time: 374 us -> 367 us (0.981)
  the two profiles are of different devices: /device:TPU:9 before, /device:TPU:0 now
where the time goes in v4:
time: 367 us; the launch traced here: 362 us
  Pallas kernels  150 us (41%)
  waiting for transfers between devices  146 us (40%)
  starting transfers between devices  48 us (13%)
  local copies, waits for them, and re-layouts  8.09 us (2%)
  other arithmetic  7.5 us (2%)
    ppermute x51, waiting for transfers between devices, swap(): return lax.ppermute(value, axis, [(at, at ^ bit) for at in range(size)])  146 us
    ppermute x51, starting transfers between devices, swap(): return lax.ppermute(value, axis, [(at, at ^ bit) for at in range(size)])  48 us
    pallas_call x6, Pallas kernels, exchange(): pl.pallas_call(functools.partial(exchange_kernel, plan), out_shape=outs +...  34 us
    pallas_call x2, Pallas kernels, feed_back(): pl.pallas_call(functools.partial(feed_back_kernel, layer, pieces, joint,...  33.5 us
    pallas_call x2, Pallas kernels, attend_back(): pl.pallas_call(body, out_shape=[jax.ShapeDtypeStruct((rows, width), F32),...  30.6 us
    pallas_call x2, Pallas kernels, feed(): pl.pallas_call(functools.partial(feed_kernel, layer, pieces, len(ties)),...  25.7 us
    pallas_call x2, Pallas kernels, attend(): pl.pallas_call(body, out_shape=outs, in_specs=[vmem] * 5 + [pl.BlockSpec(...  16.7 us
  transfers between devices with their start and end apart: 51, of which 30 were waited for; matrix products, arithmetic and copies ran while one was open for 1% of the time, Pallas kernels for 22%

profile of v4, /device:TPU:0, one launch (start us, length us, event | category | flops | bytes accessed | tf_op | source)
XLA Modules:
  0.0 361.6 jit_solution(6188956935654371992)
XLA Ops:
  4.8 5.1 %collective-permute-start.2 = (bf16[208,768]{1,0:T(8,128)(2,1)}, bf16[208,768]{1,0:T(8,128)(2,1)S(1)}, u32[]{:S(2)}, u32[]{:S(2)}) collective-permute-start(bf16[208,768]{1,0:T(8,128)(2,1)} %get-tuple-element.193.rest_0_.rest_14_.refs_9_), channel_id=1, source_target_pairs={{0,3},{1,2},{2,1},{3,0},{4,7},{5,6},{6,5},{7,4},{8,11},{9,10},{10,... | collective-permute-start | bytes 958472 | tf_op jit(solution)/shard_map/ppermute | solution.py:562
  12.7 8.3 %shard_map.281 = (bf16[384,768]{1,0:T(8,128)(2,1)}, bf16[384,768]{1,0:T(8,128)(2,1)}, bf16[384,768]{1,0:T(8,128)(2,1)}, bf16[3,6,256,128]{3,2,1,0:T(8,128)(2,1)}...) custom-call(bf16[384,768]{1,0:T(8,128)(2,1)} %bitcast.70, ...), custom_call_target="tpu_custom_call" | custom-call | flops 1811939328 | bytes 14680064 | tf_op jit(solution)/shard_map/pallas_call | solution.py:167
  25.6 11.7 %collective-permute-done.rest_1_ = bf16[208,768]{1,0:T(8,128)(2,1)S(1)} collective-permute-done((bf16[208,768]{1,0:T(8,128)(2,1)}, bf16[208,768]{1,0:T(8,128)(2,1)S(1)}, u32[]{:S(2)}, u32[]{:S(2)}) %collective-permute-start) | collective-permute-done | bytes 319520 | tf_op jit(solution)/shard_map/ppermute | solution.py:562
  40.6 8.2 %collective-permute-done.6 = bf16[3,96,768]{2,1,0:T(8,128)(2,1)S(1)} collective-permute-done((bf16[3,96,768]{2,1,0:T(8,128)(2,1)S(1)}, bf16[3,96,768]{2,1,0:T(8,128)(2,1)S(1)}, u32[]{:S(2)}, u32[]{:S(2)}) %collective-permute-start.6) | collective-permute-done | bytes 442400 | tf_op jit(solution)/shard_map/ppermute | solution.py:562
  56.9 13.1 %collective-permute-done.8.rest_7_.rest_3_ = bf16[2,3,96,768]{3,2,1,0:T(8,128)(2,1)S(1)} collective-permute-done((bf16[2,3,96,768]{3,2,1,0:T(8,128)(2,1)S(1)}, bf16[2,3,96,768]{3,2,1,0:T(8,128)(2,1)S(1)}, u32[]{:S(2)}, u32[]{:S(2)}) %collective-permute-start.8) | collective-permute-done | bytes 884768 | tf_op jit(solution)/shard_map/ppermute | solution.py:562
  71.2 7.5 %collective-permute-done.3.rest_1_ = bf16[208,768]{1,0:T(8,128)(2,1)S(1)} collective-permute-done((bf16[208,768]{1,0:T(8,128)(2,1)S(1)}, bf16[208,768]{1,0:T(8,128)(2,1)S(1)}, u32[]{:S(2)}, u32[]{:S(2)}) %collective-permute-start.3) | collective-permute-done | bytes 319520 | tf_op jit(solution)/shard_map/ppermute | solution.py:562
  85.9 13.2 %shard_map.282 = (f32[384,768]{1,0:T(8,128)}, bf16[4,384,768]{2,1,0:T(8,128)(2,1)}, bf16[4,384,768]{2,1,0:T(8,128)(2,1)}) custom-call(s32[12]{0:T(128)} %pad_add_fusion.block.blocks.refs_0_, f32[384,768]{1,0:T(8,128)} %get-tuple-element.182.mixed, f32[2,768]{1,0:T(2,128)} %gain.7, f32[2,768]{1,0:T(2,128)} %shift.7, f32[2,768]{1,0:T(2,128)} %b_down.3, ...), custom_call_target="tpu_custom_call" | custom-call | flops 3623878656 | bytes 20971520 | tf_op jit(solution)/shard_map/pallas_call | solution.py:258
  105.1 8.4 %shard_map.283 = (bf16[384,768]{1,0:T(8,128)(2,1)}, bf16[384,768]{1,0:T(8,128)(2,1)}, bf16[384,768]{1,0:T(8,128)(2,1)}, bf16[3,6,256,128]{3,2,1,0:T(8,128)(2,1)}...) custom-call(f32[384,768]{1,0:T(8,128)} %get-tuple-element.194.refs_0_.refs_2_, f32[3,128,128]{2,1,0:T(8,128)} %broadcast_in_dim.32.refs_1_, ...), custom_call_target="tpu_custom_call" | custom-call | flops 1811939328 | bytes 14680064 | tf_op jit(solution)/shard_map/pallas_call | solution.py:167
  113.5 10.1 %collective-permute-done.16.rest_7_.rest_3_ = bf16[2,3,96,768]{3,2,1,0:T(8,128)(2,1)} collective-permute-done((bf16[2,3,96,768]{3,2,1,0:T(8,128)(2,1)S(1)}, bf16[2,3,96,768]{3,2,1,0:T(8,128)(2,1)}, u32[]{:S(2)}, u32[]{:S(2)}) %collective-permute-start.16) | collective-permute-done | bytes 884768 | tf_op jit(solution)/shard_map/ppermute | solution.py:562
  128.0 12.6 %shard_map.284 = (bf16[384,768]{1,0:T(8,128)(2,1)}, bf16[4,384,768]{2,1,0:T(8,128)(2,1)}, bf16[4,384,768]{2,1,0:T(8,128)(2,1)}) custom-call(s32[12]{0:T(128)} %pad_add_fusion.block.blocks.refs_0_, f32[384,768]{1,0:T(8,128)} %get-tuple-element.196.mixed, f32[2,768]{1,0:T(2,128)} %gain.7, f32[2,768]{1,0:T(2,128)} %shift.7, f32[2,768]{1,0:T(2,128)} %b_down.3, ...), custom_call_target="tpu_custom_call" | custom-call | flops 3623878656 | bytes 20971520 | tf_op jit(solution)/shard_map/pallas_call | solution.py:258
  140.6 16.8 %shard_map.285 = (f32[384,768]{1,0:T(8,128)}, f32[8,768]{1,0:T(8,128)}, f32[4,1,768]{2,1,0:T(1,128)}, bf16[4,3,2,2,2,96,256]{6,5,4,3,2,1,0:T(8,128)(2,1)}, bf16[4,3,2,2,2,96,256]{6,5,4,3,2,1,0:T(8,128)(2,1)}) custom-call(s32[12]{0:T(128)} %pad_add_fusion.block.blocks.refs_0_, bf16[384,768]{1,0:T(8,128)(2,1)} %bitcast.73, ...), custom_call_target="tpu_custom_call" | custom-call | flops 7247757312 | bytes 31457280 | tf_op jit(solution)/shard_map/pallas_call | solution.py:359
  157.6 15.1 %shard_map.286 = (f32[384,768]{1,0:T(8,128)}, f32[8,768]{1,0:T(8,128)}, bf16[2,2,2,2,3,96,256]{6,5,4,3,2,1,0:T(8,128)(2,1)}, bf16[2,2,2,2,3,96,256]{6,5,4,3,2,1,0:T(8,128)(2,1)}) custom-call(s32[12]{0:T(128)} %pad_add_fusion.block.blocks.refs_0_, f32[384,768]{1,0:T(8,128)} %get-tuple-element.202.refs_1_, f32[384,768]{1,0:T(8,128)} %get-tuple-element.194.refs_0_.refs_2_, ...), custom_call_target="tpu_custom_call" | custom-call | flops 3623878656 | bytes 25165824 | tf_op jit(solution)/shard_map/pallas_call | solution.py:482
  180.6 16.7 %shard_map.288 = (f32[384,768]{1,0:T(8,128)}, f32[8,768]{1,0:T(8,128)}, f32[4,1,768]{2,1,0:T(1,128)}, bf16[4,3,2,2,2,96,256]{6,5,4,3,2,1,0:T(8,128)(2,1)}, bf16[4,3,2,2,2,96,256]{6,5,4,3,2,1,0:T(8,128)(2,1)}) custom-call(s32[12]{0:T(128)} %pad_add_fusion.block.blocks.refs_0_, f32[384,768]{1,0:T(8,128)} %get-tuple-element.208.grad_out, ...), custom_call_target="tpu_custom_call" | custom-call | flops 7247757312 | bytes 31457280 | tf_op jit(solution)/shard_map/pallas_call | solution.py:359
  200.0 5.0 %shard_map.289 = (bf16[20,96,256]{2,1,0:T(8,128)(2,1)}, bf16[8,96,256]{2,1,0:T(8,128)(2,1)}, bf16[20,96,256]{2,1,0:T(8,128)(2,1)}) custom-call(s32[12]{0:T(128)} %pad_add_fusion.block.blocks.refs_0_, bf16[2,2,3,2,2,2,96,256]{7,6,5,4,3,2,1,0:T(8,128)(2,1)} %bitcast.58, ...), custom_call_target="tpu_custom_call" | custom-call | tf_op jit(solution)/shard_map/pallas_call | solution.py:795
  206.8 15.5 %shard_map.290 = (f32[384,768]{1,0:T(8,128)}, f32[8,768]{1,0:T(8,128)}, bf16[2,2,2,2,3,96,256]{6,5,4,3,2,1,0:T(8,128)(2,1)}, bf16[2,2,2,2,3,96,256]{6,5,4,3,2,1,0:T(8,128)(2,1)}) custom-call(s32[12]{0:T(128)} %pad_add_fusion.block.blocks.refs_0_, f32[384,768]{1,0:T(8,128)} %get-tuple-element.217.refs_1_, bf16[384,768]{1,0:T(8,128)(2,1)} %bitcast.71, ...), custom_call_target="tpu_custom_call" | custom-call | flops 3623878656 | bytes 25165824 | tf_op jit(solution)/shard_map/pallas_call | solution.py:482
  222.3 7.1 %collective-permute-done.28.refs_7_.refs_22_.refs_12_.refs_16_ = bf16[20,96,256]{2,1,0:T(8,128)(2,1)S(1)} collective-permute-done((bf16[20,96,256]{2,1,0:T(8,128)(2,1)}, bf16[20,96,256]{2,1,0:T(8,128)(2,1)S(1)}, u32[]{:S(2)}, u32[]{:S(2)}) %collective-permute-start.28) | collective-permute-done | bytes 983072 | tf_op jit(solution)/shard_map/ppermute | solution.py:562
  231.1 7.0 %shard_map.291 = (bf16[26,96,256]{2,1,0:T(8,128)(2,1)}, bf16[26,96,256]{2,1,0:T(8,128)(2,1)}, bf16[16,96,256]{2,1,0:T(8,128)(2,1)}, bf16[4,96,256]{2,1,0:T(8,128...) custom-call(s32[12]{0:T(128)} %pad_add_fusion.block.blocks.refs_0_, ...), custom_call_target="tpu_custom_call" | custom-call | tf_op jit(solution)/shard_map/pallas_call | solution.py:795
  244.2 17.6 %collective-permute-done.35.refs_13_.refs_27_.refs_17_ = bf16[4,96,256]{2,1,0:T(8,128)(2,1)S(1)} collective-permute-done((bf16[4,96,256]{2,1,0:T(8,128)(2,1)}, bf16[4,96,256]{2,1,0:T(8,128)(2,1)S(1)}, u32[]{:S(2)}, u32[]{:S(2)}) %collective-permute-start.35) | collective-permute-done | bytes 196640 | tf_op jit(solution)/shard_map/ppermute | solution.py:562
  263.7 5.2 %collective-permute-done.32.refs_4_.refs_25_.refs_5_.refs_6_.refs_8_ = bf16[26,96,256]{2,1,0:T(8,128)(2,1)S(1)} collective-permute-done((bf16[26,96,256]{2,1,0:T(8,128)(2,1)}, bf16[26,96,256]{2,1,0:T(8,128)(2,1)S(1)}, u32[]{:S(2)}, u32[]{:S(2)}) %collective-permute-start.32) | collective-permute-done | bytes 1277984 | tf_op jit(solution)/shard_map/ppermute | solution.py:562
  270.0 7.7 %shard_map.293 = (bf16[20,96,256]{2,1,0:T(8,128)(2,1)}, bf16[13,96,256]{2,1,0:T(8,128)(2,1)}, bf16[21,96,256]{2,1,0:T(8,128)(2,1)}, bf16[7,96,256]{2,1,0:T(8,128...) custom-call(s32[12]{0:T(128)} %pad_add_fusion.block.blocks.refs_0_, ...), custom_call_target="tpu_custom_call" | custom-call | tf_op jit(solution)/shard_map/pallas_call | solution.py:795
  284.3 21.6 %collective-permute-done.41.refs_18_.refs_24_ = bf16[3,96,256]{2,1,0:T(8,128)(2,1)} collective-permute-done((bf16[3,96,256]{2,1,0:T(8,128)(2,1)}, bf16[3,96,256]{2,1,0:T(8,128)(2,1)}, u32[]{:S(2)}, u32[]{:S(2)}) %collective-permute-start.41) | collective-permute-done | bytes 147488 | tf_op jit(solution)/shard_map/ppermute | solution.py:562
  329.0 5.2 %shard_map.297 = (bf16[5,96,256]{2,1,0:T(8,128)(2,1)}, bf16[7,96,256]{2,1,0:T(8,128)(2,1)}, bf16[3,96,256]{2,1,0:T(8,128)(2,1)}, bf16[1,96,256]{2,1,0:T(8,128)(2,1)}, f32[96,768]{1,0:T(8,128)}) custom-call(s32[12]{0:T(128)} %pad_add_fusion.block.blocks.refs_0_, bf16[2,2,3,2,2,2,96,256]{7,6,5,4,3,2,1,0:T(8,128)(2,1)} %bitcast.55, ...), custom_call_target="tpu_custom_call" | custom-call | tf_op jit(solution)/shard_map/pallas_call | solution.py:795
  342.9 10.4 %collective-permute-done.49.refs_23_ = bf16[3,96,256]{2,1,0:T(8,128)(2,1)S(1)} collective-permute-done((bf16[3,96,256]{2,1,0:T(8,128)(2,1)}, bf16[3,96,256]{2,1,0:T(8,128)(2,1)S(1)}, u32[]{:S(2)}, u32[]{:S(2)}) %collective-permute-start.49) | collective-permute-done | bytes 147488 | tf_op jit(solution)/shard_map/ppermute | solution.py:562
  356.2 5.1 %shard_map.298 = (f32[2,96,768]{2,1,0:T(8,128)}, f32[2,96,768]{2,1,0:T(8,128)}, f32[2,96,192]{2,1,0:T(8,128)}, f32[2,96,192]{2,1,0:T(8,128)}, f32[2,96,192]{2,1,...) custom-call(s32[12]{0:T(128)} %pad_add_fusion.block.blocks.refs_0_, ...), custom_call_target="tpu_custom_call" | custom-call | tf_op jit(solution)/shard_map/pallas_call | solution.py:908
  (195 shorter events, 105.9 us)
Async XLA Ops:
  9.9 27.4 %collective-permute-start = (bf16[208,768]{1,0:T(8,128)(2,1)}, bf16[208,768]{1,0:T(8,128)(2,1)S(1)}, u32[]{:S(2)}, u32[]{:S(2)}) collective-permute-start(bf16[208,768]{1,0:T(8,128)(2,1)} %get-tuple-element.193.rest_0_.rest_14_.refs_9_), channel_id=1, source_target_pairs={{0,2},{1,3},{2,0},{3,1},{4,6},{5,7},{6,4},{7,5},{8,10},{9,11},{10,... | collective-permute-start | bytes 958472 | tf_op jit(solution)/shard_map/ppermute | solution.py:562
  50.4 19.6 %collective-permute-start.8 = (bf16[2,3,96,768]{3,2,1,0:T(8,128)(2,1)S(1)}, bf16[2,3,96,768]{3,2,1,0:T(8,128)(2,1)S(1)}, u32[]{:S(2)}, u32[]{:S(2)}) collective-permute-start(bf16[2,3,96,768]{3,2,1,0:T(8,128)(2,1)S(1)} %pad_maximum_fusion.rest_6_.rest_2_), channel_id=1, source_target_pairs={{0,16},{4,20},{8,24},{12,28},{16,0},{20,4},{24,8},{28,12},{1,17},{... | collective-permute-start | bytes 2654216 | tf_op jit(solution)/shard_map/ppermute | solution.py:562
  54.8 23.9 %collective-permute-start.3 = (bf16[208,768]{1,0:T(8,128)(2,1)S(1)}, bf16[208,768]{1,0:T(8,128)(2,1)S(1)}, u32[]{:S(2)}, u32[]{:S(2)}) collective-permute-start(bf16[208,768]{1,0:T(8,128)(2,1)S(1)} %copy-done.31), channel_id=1, source_target_pairs={{0,2},{1,3},{2,0},{3,1},{4,6},{5,7},{6,4},{7,5},{8,10},{9,11},{10,... | collective-permute-start | bytes 958472 | tf_op jit(solution)/shard_map/ppermute | solution.py:562
  101.8 21.9 %collective-permute-start.16 = (bf16[2,3,96,768]{3,2,1,0:T(8,128)(2,1)S(1)}, bf16[2,3,96,768]{3,2,1,0:T(8,128)(2,1)}, u32[]{:S(2)}, u32[]{:S(2)}) collective-permute-start(bf16[2,3,96,768]{3,2,1,0:T(8,128)(2,1)S(1)} %pad_maximum_fusion.2.rest_6_.rest_2_), channel_id=1, source_target_pairs={{0,16},{4,20},{8,24},{12,28},{16,0},{20,4},{24,8},{28,12},{1,17},{... | collective-permute-start | bytes 2654216 | tf_op jit(solution)/shard_map/ppermute | solution.py:562
  102.5 21.5 %collective-permute-start.17 = (bf16[2,3,96,768]{3,2,1,0:T(8,128)(2,1)S(1)}, bf16[2,3,96,768]{3,2,1,0:T(8,128)(2,1)}, u32[]{:S(2)}, u32[]{:S(2)}) collective-permute-start(bf16[2,3,96,768]{3,2,1,0:T(8,128)(2,1)S(1)} %pad_maximum_fusion.3.rest_8_.rest_4_), channel_id=1, source_target_pairs={{0,8},{4,12},{8,0},{12,4},{16,24},{20,28},{24,16},{28,20},{1,9},{5... | collective-permute-start | bytes 2654216 | tf_op jit(solution)/shard_map/ppermute | solution.py:562
  103.8 20.7 %collective-permute-start.18 = (bf16[2,3,96,768]{3,2,1,0:T(8,128)(2,1)S(1)}, bf16[2,3,96,768]{3,2,1,0:T(8,128)(2,1)}, u32[]{:S(2)}, u32[]{:S(2)}) collective-permute-start(bf16[2,3,96,768]{3,2,1,0:T(8,128)(2,1)S(1)} %pad_maximum_fusion.2.rest_6_.rest_2_), channel_id=1, source_target_pairs={{0,4},{4,0},{8,12},{12,8},{16,20},{20,16},{24,28},{28,24},{1,5},{5... | collective-permute-start | bytes 2654216 | tf_op jit(solution)/shard_map/ppermute | solution.py:562
  103.8 20.7 %collective-permute-start.20 = (bf16[2,3,96,768]{3,2,1,0:T(8,128)(2,1)S(1)}, bf16[2,3,96,768]{3,2,1,0:T(8,128)(2,1)}, u32[]{:S(2)}, u32[]{:S(2)}) collective-permute-start(bf16[2,3,96,768]{3,2,1,0:T(8,128)(2,1)S(1)} %pad_maximum_fusion.3.rest_8_.rest_4_), channel_id=1, source_target_pairs={{0,4},{4,0},{8,12},{12,8},{16,20},{20,16},{24,28},{28,24},{1,5},{5... | collective-permute-start | bytes 2654216 | tf_op jit(solution)/shard_map/ppermute | solution.py:562
  177.3 22.7 %collective-permute-start.26 = (bf16[2,2,2,2,3,96,256]{6,5,4,3,2,1,0:T(8,128)(2,1)}, bf16[2,2,2,2,3,96,256]{6,5,4,3,2,1,0:T(8,128)(2,1)}, u32[]{:S(2)}, u32[]{:S(2)}) collective-permute-start(bf16[2,2,2,2,3,96,256]{6,5,4,3,2,1,0:T(8,128)(2,1)} %get-tuple-element.229), channel_id=1, source_target_pairs={{0,4},{4,0},{8,12},{12,8},{16,20},{20,16},{24,28},{28,24},{1,5},{5... | collective-permute-start | bytes 7077896 | tf_op jit(solution)/shard_map/ppermute | solution.py:562
  177.7 19.8 %collective-permute-start.23 = (bf16[16,96,256]{2,1,0:T(8,128)(2,1)}, bf16[16,96,256]{2,1,0:T(8,128)(2,1)S(1)}, u32[]{:S(2)}, u32[]{:S(2)}) collective-permute-start(bf16[16,96,256]{2,1,0:T(8,128)(2,1)} %get-tuple-element.225.rest_10_), channel_id=1, source_target_pairs={{0,8},{4,12},{8,0},{12,4},{16,24},{20,28},{24,16},{28,20},{1,9},{5... | collective-permute-start | bytes 2359304 | tf_op jit(solution)/shard_map/ppermute | solution.py:562
  179.1 19.5 %collective-permute-start.24 = (bf16[16,96,256]{2,1,0:T(8,128)(2,1)}, bf16[16,96,256]{2,1,0:T(8,128)(2,1)S(1)}, u32[]{:S(2)}, u32[]{:S(2)}) collective-permute-start(bf16[16,96,256]{2,1,0:T(8,128)(2,1)} %get-tuple-element.226.rest_11_), channel_id=1, source_target_pairs={{0,16},{4,20},{8,24},{12,28},{16,0},{20,4},{24,8},{28,12},{1,17},{... | collective-permute-start | bytes 2359304 | tf_op jit(solution)/shard_map/ppermute | solution.py:562
  180.6 19.4 %collective-permute-start.25 = (bf16[16,96,256]{2,1,0:T(8,128)(2,1)}, bf16[16,96,256]{2,1,0:T(8,128)(2,1)}, u32[]{:S(2)}, u32[]{:S(2)}) collective-permute-start(bf16[16,96,256]{2,1,0:T(8,128)(2,1)} %get-tuple-element.227.rest_12_), channel_id=1, source_target_pairs={{0,1},{1,0},{2,3},{3,2},{4,5},{5,4},{6,7},{7,6},{8,9},{9,8},{10,11... | collective-permute-start | bytes 2359304 | tf_op jit(solution)/shard_map/ppermute | solution.py:562
  204.9 25.2 %collective-permute-start.27 = (bf16[4,3,2,2,2,96,256]{6,5,4,3,2,1,0:T(8,128)(2,1)}, bf16[4,3,2,2,2,96,256]{6,5,4,3,2,1,0:T(8,128)(2,1)}, u32[]{:S(2)}, u32[]{:S(2)}) collective-permute-start(bf16[4,3,2,2,2,96,256]{6,5,4,3,2,1,0:T(8,128)(2,1)} %get-tuple-element.237), channel_id=1, source_target_pairs={{0,4},{4,0},{8,12},{12,8},{16,20},{20,16},{24,28},{28,24},{1,5},{5... | collective-permute-start | bytes 14155784 | tf_op jit(solution)/shard_map/ppermute | solution.py:562
  205.0 24.4 %collective-permute-start.28 = (bf16[20,96,256]{2,1,0:T(8,128)(2,1)}, bf16[20,96,256]{2,1,0:T(8,128)(2,1)S(1)}, u32[]{:S(2)}, u32[]{:S(2)}) collective-permute-start(bf16[20,96,256]{2,1,0:T(8,128)(2,1)} %get-tuple-element.238.refs_16_), channel_id=1, source_target_pairs={{0,16},{4,20},{8,24},{12,28},{16,0},{20,4},{24,8},{28,12},{1,17},{... | collective-permute-start | bytes 2949128 | tf_op jit(solution)/shard_map/ppermute | solution.py:562
  206.1 24.0 %collective-permute-start.30 = (bf16[20,96,256]{2,1,0:T(8,128)(2,1)}, bf16[20,96,256]{2,1,0:T(8,128)(2,1)S(1)}, u32[]{:S(2)}, u32[]{:S(2)}) collective-permute-start(bf16[20,96,256]{2,1,0:T(8,128)(2,1)} %get-tuple-element.240.refs_18_), channel_id=1, source_target_pairs={{0,8},{4,12},{8,0},{12,4},{16,24},{20,28},{24,16},{28,20},{1,9},{5... | collective-permute-start | bytes 2949128 | tf_op jit(solution)/shard_map/ppermute | solution.py:562
  238.2 31.6 %collective-permute-start.34 = (bf16[2,2,2,2,3,96,256]{6,5,4,3,2,1,0:T(8,128)(2,1)}, bf16[2,2,2,2,3,96,256]{6,5,4,3,2,1,0:T(8,128)(2,1)}, u32[]{:S(2)}, u32[]{:S(2)}) collective-permute-start(bf16[2,2,2,2,3,96,256]{6,5,4,3,2,1,0:T(8,128)(2,1)} %get-tuple-element.255), channel_id=1, source_target_pairs={{0,4},{4,0},{8,12},{12,8},{16,20},{20,16},{24,28},{28,24},{1,5},{5... | collective-permute-start | bytes 7077896 | tf_op jit(solution)/shard_map/ppermute | solution.py:562
  238.3 30.7 %collective-permute-start.32 = (bf16[26,96,256]{2,1,0:T(8,128)(2,1)}, bf16[26,96,256]{2,1,0:T(8,128)(2,1)S(1)}, u32[]{:S(2)}, u32[]{:S(2)}) collective-permute-start(bf16[26,96,256]{2,1,0:T(8,128)(2,1)} %get-tuple-element.252), channel_id=1, source_target_pairs={{0,16},{4,20},{8,24},{12,28},{16,0},{20,4},{24,8},{28,12},{1,17},{... | collective-permute-start | bytes 3833864 | tf_op jit(solution)/shard_map/ppermute | solution.py:562
  239.3 30.5 %collective-permute-start.31 = (bf16[26,96,256]{2,1,0:T(8,128)(2,1)}, bf16[26,96,256]{2,1,0:T(8,128)(2,1)}, u32[]{:S(2)}, u32[]{:S(2)}) collective-permute-start(bf16[26,96,256]{2,1,0:T(8,128)(2,1)} %get-tuple-element.251.source), channel_id=1, source_target_pairs={{0,8},{4,12},{8,0},{12,4},{16,24},{20,28},{24,16},{28,20},{1,9},{5... | collective-permute-start | bytes 3833864 | tf_op jit(solution)/shard_map/ppermute | solution.py:562
  239.9 23.9 %collective-permute-start.33 = (bf16[16,96,256]{2,1,0:T(8,128)(2,1)}, bf16[16,96,256]{2,1,0:T(8,128)(2,1)}, u32[]{:S(2)}, u32[]{:S(2)}) collective-permute-start(bf16[16,96,256]{2,1,0:T(8,128)(2,1)} %get-tuple-element.253), channel_id=1, source_target_pairs={{0,1},{1,0},{2,3},{3,2},{4,5},{5,4},{6,7},{7,6},{8,9},{9,8},{10,11... | collective-permute-start | bytes 2359304 | tf_op jit(solution)/shard_map/ppermute | solution.py:562
  277.7 28.2 %collective-permute-start.39 = (bf16[21,96,256]{2,1,0:T(8,128)(2,1)}, bf16[21,96,256]{2,1,0:T(8,128)(2,1)S(1)}, u32[]{:S(2)}, u32[]{:S(2)}) collective-permute-start(bf16[21,96,256]{2,1,0:T(8,128)(2,1)} %get-tuple-element.266), channel_id=1, source_target_pairs={{0,8},{4,12},{8,0},{12,4},{16,24},{20,28},{24,16},{28,20},{1,9},{5... | collective-permute-start | bytes 3096584 | tf_op jit(solution)/shard_map/ppermute | solution.py:562
  278.4 27.6 %collective-permute-start.37 = (bf16[20,96,256]{2,1,0:T(8,128)(2,1)}, bf16[20,96,256]{2,1,0:T(8,128)(2,1)S(1)}, u32[]{:S(2)}, u32[]{:S(2)}) collective-permute-start(bf16[20,96,256]{2,1,0:T(8,128)(2,1)} %get-tuple-element.264.source), channel_id=1, source_target_pairs={{0,16},{4,20},{8,24},{12,28},{16,0},{20,4},{24,8},{28,12},{1,17},{... | collective-permute-start | bytes 2949128 | tf_op jit(solution)/shard_map/ppermute | solution.py:562
  279.3 26.6 %collective-permute-start.38 = (bf16[13,96,256]{2,1,0:T(8,128)(2,1)}, bf16[13,96,256]{2,1,0:T(8,128)(2,1)}, u32[]{:S(2)}, u32[]{:S(2)}) collective-permute-start(bf16[13,96,256]{2,1,0:T(8,128)(2,1)} %get-tuple-element.265), channel_id=1, source_target_pairs={{0,1},{1,0},{2,3},{3,2},{4,5},{5,4},{6,7},{7,6},{8,9},{9,8},{10,11... | collective-permute-start | bytes 1916936 | tf_op jit(solution)/shard_map/ppermute | solution.py:562
  279.9 26.0 %collective-permute-start.40 = (bf16[7,96,256]{2,1,0:T(8,128)(2,1)}, bf16[7,96,256]{2,1,0:T(8,128)(2,1)}, u32[]{:S(2)}, u32[]{:S(2)}) collective-permute-start(bf16[7,96,256]{2,1,0:T(8,128)(2,1)} %get-tuple-element.267), channel_id=1, source_target_pairs={{0,2},{1,3},{2,0},{3,1},{4,6},{5,7},{6,4},{7,5},{8,10},{9,11},{10,... | collective-permute-start | bytes 1032200 | tf_op jit(solution)/shard_map/ppermute | solution.py:562
  281.6 24.3 %collective-permute-start.41 = (bf16[3,96,256]{2,1,0:T(8,128)(2,1)}, bf16[3,96,256]{2,1,0:T(8,128)(2,1)}, u32[]{:S(2)}, u32[]{:S(2)}) collective-permute-start(bf16[3,96,256]{2,1,0:T(8,128)(2,1)} %get-tuple-element.268), channel_id=1, source_target_pairs={{0,3},{1,2},{2,1},{3,0},{4,7},{5,6},{6,5},{7,4},{8,11},{9,10},{10,... | collective-permute-start | bytes 442376 | tf_op jit(solution)/shard_map/ppermute | solution.py:562
  334.2 21.3 %collective-permute-start.48 = (bf16[7,96,256]{2,1,0:T(8,128)(2,1)}, bf16[7,96,256]{2,1,0:T(8,128)(2,1)S(1)}, u32[]{:S(2)}, u32[]{:S(2)}) collective-permute-start(bf16[7,96,256]{2,1,0:T(8,128)(2,1)} %get-tuple-element.279), channel_id=1, source_target_pairs={{0,2},{1,3},{2,0},{3,1},{4,6},{5,7},{6,4},{7,5},{8,10},{9,11},{10,... | collective-permute-start | bytes 1032200 | tf_op jit(solution)/shard_map/ppermute | solution.py:562
  (63 other events, 604.9 us)

commit v5 on v4

--- a/solution.py
+++ b/solution.py
@@ -806,6 +806,7 @@
         going = lax.optimization_barrier(self.made + [send for _, send in crossing])
         arrived = {letter: swap(value, *LINKS[letter]) for letter, value in zip(order, going)}
         self.arrived = list(arrived.values())
+        self.going = going[0]
         if alone:
             self.arrived.append(pause(going[0]))
         for (crossed, _), send in zip(crossing, going[len(outs):]):
@@ -836,88 +837,98 @@
         return ("new" if letters == "c" else "old"), letters
 
 
-def finish_kernel(plan, array_count, blocks, *refs):
+def finish_kernel(plan, layer, counts, blocks, *refs):
     wides, feeds, far, small = plan
-    arrays, refs = refs[:array_count], refs[array_count:]
-    owns, small_own, refs = refs[:2], refs[2], refs[3:]
-    up, down, *attends = refs[:6]
-    smalls, gate, hidden = refs[6:11], refs[11], refs[12]
-    held_wide, held, held_far, held_small, sems = refs[13:]
+    array_count, other_count = counts
+    arrays, own, refs = refs[:array_count], refs[array_count], refs[array_count + 1:]
+    if small:
+        small_own, refs = refs[0], refs[1:]
+    refs = refs[other_count:]
+    outs, refs = refs[:6], refs[6:]
+    if small:
+        smalls, gate, hidden, refs = refs[:5], refs[5], refs[6], refs[7:]
+    up, down, attends, held_wide, held, held_far, held_small, sems, out_sems = refs
     copies = []
 
-    def fetch(array, place, size, target):
-        copies.append(pltpu.make_async_copy(arrays[array].at[pl.ds(place, size)], target, sems.at[len(copies)]))
+    def fetch(source, target):
+        copies.append(pltpu.make_async_copy(source, target, sems.at[len(copies)]))
         copies[-1].start()
 
-    for layer, term, array in wides:
-        copies.append(pltpu.make_async_copy(
-            arrays[array].at[0, 0, :, :, 0, 0], held_wide.at[layer, term], sems.at[len(copies)]))
-        copies[-1].start()
-    for layer, part, term, array, place in feeds:
-        fetch(array, place, 2, held.at[layer, part, term])
-    for layer, other, array, place in far:
-        fetch(array, place, 3, held_far.at[layer, other])
+    for term, array in wides:
+        fetch(arrays[array].at[0, 0, :, :, 0, 0], held_wide.at[term])
+    for part, term, array, place in feeds:
+        fetch(arrays[array].at[pl.ds(place, 2)], held.at[part, term])
+    for other, array, place in far:
+        fetch(arrays[array].at[pl.ds(place, 3)], held_far.at[other])
     for term, (array, place) in enumerate(small):
-        fetch(array, place, 1, held_small.at[term])
+        fetch(arrays[array].at[pl.ds(place, 1)], held_small.at[term])
     for copy in copies:
         copy.wait()
-    terms, tile = held.shape[2], held.shape[5]
-    for layer in range(2):
-        for part in range(3):
-            total = held_wide[layer, 0, part].astype(F32) + held_wide[layer, 1, part].astype(F32)
-            for term in range(terms):
-                total = total + held[layer, part, term].astype(F32)
-            up[layer, :, part * tile:(part + 1) * tile] = total[0]
-            down[layer, :, part * tile:(part + 1) * tile] = total[1]
-        total = owns[layer][...]
-        for other in range(3):
-            total = total + jnp.concatenate([held_far[layer, other, cut].astype(F32) for cut in range(3)], axis=1)
-        share = total.shape[1] // 4
-        for at, out in enumerate(attends):
-            out[layer] = total[:, at * share:(at + 1) * share]
-    total = small_own[...]
-    for term in range(len(small)):
-        total = total + from_block(held_small[term, 0])
-    lines = total.shape[1] // 8
-    mine = jnp.where(blocks[0] == 0, total[:, :lines], 0.0)
-    for place in range(1, 8):
-        mine = mine + jnp.where(blocks[0] == place, total[:, place * lines:(place + 1) * lines], 0.0)
-    for layer in range(2):
-        base = 10 * layer
-        for row, out in zip((3, 4, 1, 2, 0), smalls):
-            out[layer:layer + 1] = mine[base + row:base + row + 1]
-        shard = jnp.zeros((1, total.shape[1]), F32)
-        for at in range(4):
-            shard = shard + jnp.where(blocks[8] == at, total[base + 6 + at:base + 7 + at], 0.0)
-        hidden[layer:layer + 1] = shard
-    gate[...] = mine[5:6]
-
-
-def finish(feeds, attends, small, blocks):
+    leaving = Leaving(out_sems)
+    terms, tile = held.shape[1], held.shape[4]
+    for part in range(3):
+        total = held_wide[0, part].astype(F32) + held_wide[1, part].astype(F32)
+        for term in range(terms):
+            total = total + held[part, term].astype(F32)
+        up[:, part * tile:(part + 1) * tile] = total[0]
+        down[:, part * tile:(part + 1) * tile] = total[1]
+    leaving.send(up, outs[0].at[layer])
+    leaving.send(down, outs[1].at[layer])
+    total = own[...]
+    for other in range(3):
+        total = total + jnp.concatenate([held_far[other, cut].astype(F32) for cut in range(3)], axis=1)
+    share = total.shape[1] // 4
+    for at in range(4):
+        attends[at] = total[:, at * share:(at + 1) * share]
+        leaving.send(attends.at[at], outs[2 + at].at[layer])
+    if small:
+        total = small_own[...]
+        for term in range(len(small)):
+            total = total + from_block(held_small[term, 0])
+        lines = total.shape[1] // 8
+        mine = jnp.where(blocks[0] == 0, total[:, :lines], 0.0)
+        for place in range(1, 8):
+            mine = mine + jnp.where(blocks[0] == place, total[:, place * lines:(place + 1) * lines], 0.0)
+        for at in range(2):
+            base = 10 * at
+            for row, out in zip((3, 4, 1, 2, 0), smalls):
+                out[at:at + 1] = mine[base + row:base + row + 1]
+            shard = jnp.zeros((1, total.shape[1]), F32)
+            for index in range(4):
+                shard = shard + jnp.where(blocks[8] == index, total[base + 6 + index:base + 7 + index], 0.0)
+            hidden[at:at + 1] = shard
+        gate[...] = mine[5:6]
+    leaving.wait()
+
+
+def finish(layer, feeds, attends, blocks, before, small=None):
     reads = Reads()
-    wide_plan = [(layer, term, reads.at(array)) for layer, flows in enumerate(feeds)
-                 for term, array in enumerate(flows[0].wide)]
-    feed_plan = [(layer, part, term, reads.at(array), place) for layer, flows in enumerate(feeds)
-                 for part, flow in enumerate(flows) for term, (array, place) in enumerate(flow.terms)]
-    far_plan = [(layer, other, reads.at(array), place) for layer, pair in enumerate(attends)
-                for other, (array, place) in enumerate(pair[0].far)]
-    small_plan = reads.places(small.terms)
-    rows, tile = feeds[0][0].tile
-    width, terms = 3 * tile, len(feeds[0][0].terms)
+    wide_plan = [(term, reads.at(array)) for term, array in enumerate(feeds[0].wide)]
+    feed_plan = [(part, term, reads.at(array), place) for part, flow in enumerate(feeds)
+                 for term, (array, place) in enumerate(flow.terms)]
+    far_plan = [(other, reads.at(array), place) for other, (array, place) in enumerate(attends[0].far)]
+    small_plan = reads.places(small.terms) if small else []
+    rows, tile = feeds[0].tile
+    width, terms = 3 * tile, len(feeds[0].terms)
     anywhere, vmem = pl.BlockSpec(memory_space=pl.ANY), pl.BlockSpec(memory_space=pltpu.VMEM)
+    outs = [jax.ShapeDtypeStruct((2, rows, width), F32)] * 2 + [jax.ShapeDtypeStruct((2, rows, width // 4), F32)] * 4
+    more = [jax.ShapeDtypeStruct((2, rows), F32)] * 5 + [
+        jax.ShapeDtypeStruct((1, rows), F32), jax.ShapeDtypeStruct((2, width), F32)] if small else []
+    given = 2 + len(reads.arrays) + (1 if small else 0)
     return pl.pallas_call(
-        functools.partial(finish_kernel, (wide_plan, feed_plan, far_plan, small_plan), len(reads.arrays)),
-        out_shape=[jax.ShapeDtypeStruct((2, rows, width), F32)] * 2
-        + [jax.ShapeDtypeStruct((2, rows, width // 4), F32)] * 4 + [jax.ShapeDtypeStruct((2, rows), F32)] * 5
-        + [jax.ShapeDtypeStruct((1, rows), F32), jax.ShapeDtypeStruct((2, width), F32)],
-        in_specs=[pl.BlockSpec(memory_space=pltpu.SMEM)] + [anywhere] * len(reads.arrays) + [vmem] * 3,
-        out_specs=[vmem] * 13,
-        scratch_shapes=[pltpu.VMEM((2, 2, 3, 2, rows, tile), BF16), pltpu.VMEM((2, 3, terms, 2, rows, tile), BF16),
-                        pltpu.VMEM((2, 3, 3, rows, tile), BF16),
-                        pltpu.VMEM((len(small_plan), 1, rows, tile), BF16),
-                        pltpu.SemaphoreType.DMA((len(wide_plan) + len(feed_plan) + len(far_plan) + len(small_plan),))],
+        functools.partial(finish_kernel, (wide_plan, feed_plan, far_plan, small_plan), layer, (len(reads.arrays), len(before))),
+        out_shape=outs + more,
+        in_specs=[pl.BlockSpec(memory_space=pltpu.SMEM)] + [anywhere] * len(reads.arrays) + [vmem] * (given - 1 - len(reads.arrays))
+        + [anywhere] * len(before),
+        out_specs=[anywhere] * 6 + [vmem] * len(more),
+        scratch_shapes=[pltpu.VMEM((rows, width), F32), pltpu.VMEM((rows, width), F32), pltpu.VMEM((4, rows, width // 4), F32),
+                        pltpu.VMEM((2, 3, 2, rows, tile), BF16), pltpu.VMEM((3, terms, 2, rows, tile), BF16),
+                        pltpu.VMEM((3, 3, rows, tile), BF16), pltpu.VMEM((max(len(small_plan), 1), 1, rows, tile), BF16),
+                        pltpu.SemaphoreType.DMA((len(wide_plan) + len(feed_plan) + len(far_plan) + len(small_plan),)),
+                        pltpu.SemaphoreType.DMA((6,))],
+        input_output_aliases={given + at: at for at in range(6)} if small else {},
         compiler_params=pltpu.CompilerParams(vmem_limit_bytes=VMEM_BYTES),
-    )(blocks, *reads.arrays, attends[0][0].own, attends[1][0].own, small.own)
+    )(blocks, *reads.arrays, attends[0].own, *([small.own] if small else []), *before)
 
 
 def eighths(weights):
@@ -967,9 +978,9 @@
     dp, mp = lax.axis_size("dp"), lax.axis_size("mp")
     paired = dp == 8 and mp == 4 and width % (16 * dp) == 0
     if paired:
-        blocks = jnp.concatenate([
-            lax.axis_index("dp") ^ jnp.arange(8, dtype=jnp.int32),
-            lax.axis_index("mp") ^ jnp.array(SHARD_ORDER, jnp.int32)])
+        place = jnp.arange(12, dtype=jnp.int32)
+        slot = place & 3
+        blocks = jnp.where(place < 8, lax.axis_index("dp") ^ place, lax.axis_index("mp") ^ ((slot & 1) * 2 + slot // 2))
     else:
         blocks = jnp.arange(2, dtype=jnp.int32)
 
@@ -1069,8 +1080,9 @@
         rounds.exchange(feeds[0] + feeds[1] + attends[1], small=small, crossing=[(attends[0], got["attend_grads", 0][1])], alone=True)
         rounds.exchange(feeds[0] + attends[0] + feeds[1], [attends[1]], small, alone=True)
         rounds.exchange(feeds[0] + attends[0], small=small, alone=True)
-        rounds.exchange(feeds[0], [attends[0]], small, alone=True)
-        up_grad, down_turned, *rest = finish([feeds[0], feeds[1]], [attends[0], attends[1]], small, blocks)
+        rounds.exchange(feeds[0], [attends[0]], small)
+        made = finish(1, feeds[1], attends[1], blocks, [rounds.going])
+        up_grad, down_turned, *rest = finish(0, feeds[0], attends[0], blocks, made, small)
         down_grad = jnp.swapaxes(down_turned, 1, 2)
         attend_grads, small_grads, gate_grad, bup_grad = rest[:4], rest[4:9], rest[9][0], rest[10]
     else:

time: 367 us -> 366 us (level)
    pallas_call x1 -> x2, Pallas kernels: 5.11 us -> 8.36 us  [finish(): pl.pallas_call(functools.partial(finish_kernel, (wide_plan, feed_plan, fa...]
  transfers between devices with their start and end apart: 51 -> 51, of which waited for: 30 -> 29; matrix products, arithmetic and copies ran while one was open for 1% -> 1% of each run, Pallas kernels for 22% -> 23%
where the time goes in v5:
time: 366 us; the launch traced here: 360 us
  Pallas kernels  153 us (42%)
  waiting for transfers between devices  143 us (39%)
  starting transfers between devices  47.9 us (13%)
  local copies, waits for them, and re-layouts  8.15 us (2%)
  other arithmetic  6.8 us (2%)
    ppermute x51, waiting for transfers between devices, swap(): return lax.ppermute(value, axis, [(at, at ^ bit) for at in range(size)])  143 us
    ppermute x51, starting transfers between devices, swap(): return lax.ppermute(value, axis, [(at, at ^ bit) for at in range(size)])  47.9 us
    pallas_call x6, Pallas kernels, exchange(): pl.pallas_call(functools.partial(exchange_kernel, plan), out_shape=outs +...  33.8 us
    pallas_call x2, Pallas kernels, feed_back(): pl.pallas_call(functools.partial(feed_back_kernel, layer, pieces, joint,...  33.5 us
    pallas_call x2, Pallas kernels, attend_back(): pl.pallas_call(body, out_shape=[jax.ShapeDtypeStruct((rows, width), F32),...  30.6 us
    pallas_call x2, Pallas kernels, feed(): pl.pallas_call(functools.partial(feed_kernel, layer, pieces, len(ties)),...  25.7 us
    pallas_call x2, Pallas kernels, attend(): pl.pallas_call(body, out_shape=outs, in_specs=[vmem] * 5 + [pl.BlockSpec(...  16.7 us
    pallas_call x2, Pallas kernels, finish(): pl.pallas_call(functools.partial(finish_kernel, (wide_plan, feed_plan, fa...  8.36 us
  transfers between devices with their start and end apart: 51, of which 29 were waited for; matrix products, arithmetic and copies ran while one was open for 1% of the time, Pallas kernels for 23%

profile of v5, /device:TPU:0, one launch (start us, length us, event | category | flops | bytes accessed | tf_op | source)
XLA Modules:
  0.0 360.4 jit_solution(2198615864912479527)
XLA Ops:
  4.0 5.1 %collective-permute-start.2 = (bf16[208,768]{1,0:T(8,128)(2,1)}, bf16[208,768]{1,0:T(8,128)(2,1)S(1)}, u32[]{:S(2)}, u32[]{:S(2)}) collective-permute-start(bf16[208,768]{1,0:T(8,128)(2,1)} %get-tuple-element.199.rest_0_.rest_14_.refs_9_), channel_id=1, source_target_pairs={{0,3},{1,2},{2,1},{3,0},{4,7},{5,6},{6,5},{7,4},{8,11},{9,10},{10,... | collective-permute-start | bytes 958472 | tf_op jit(solution)/shard_map/ppermute | solution.py:562
  12.0 8.3 %shard_map.272 = (bf16[384,768]{1,0:T(8,128)(2,1)}, bf16[384,768]{1,0:T(8,128)(2,1)}, bf16[384,768]{1,0:T(8,128)(2,1)}, bf16[3,6,256,128]{3,2,1,0:T(8,128)(2,1)}...) custom-call(bf16[384,768]{1,0:T(8,128)(2,1)} %bitcast.70, ...), custom_call_target="tpu_custom_call" | custom-call | flops 1811939328 | bytes 14680064 | tf_op jit(solution)/shard_map/pallas_call | solution.py:167
  24.9 11.7 %collective-permute-done.rest_1_ = bf16[208,768]{1,0:T(8,128)(2,1)S(1)} collective-permute-done((bf16[208,768]{1,0:T(8,128)(2,1)}, bf16[208,768]{1,0:T(8,128)(2,1)S(1)}, u32[]{:S(2)}, u32[]{:S(2)}) %collective-permute-start) | collective-permute-done | bytes 319520 | tf_op jit(solution)/shard_map/ppermute | solution.py:562
  39.9 8.2 %collective-permute-done.6 = bf16[3,96,768]{2,1,0:T(8,128)(2,1)S(1)} collective-permute-done((bf16[3,96,768]{2,1,0:T(8,128)(2,1)S(1)}, bf16[3,96,768]{2,1,0:T(8,128)(2,1)S(1)}, u32[]{:S(2)}, u32[]{:S(2)}) %collective-permute-start.6) | collective-permute-done | bytes 442400 | tf_op jit(solution)/shard_map/ppermute | solution.py:562
  56.2 13.1 %collective-permute-done.8.rest_7_.rest_3_ = bf16[2,3,96,768]{3,2,1,0:T(8,128)(2,1)S(1)} collective-permute-done((bf16[2,3,96,768]{3,2,1,0:T(8,128)(2,1)S(1)}, bf16[2,3,96,768]{3,2,1,0:T(8,128)(2,1)S(1)}, u32[]{:S(2)}, u32[]{:S(2)}) %collective-permute-start.8) | collective-permute-done | bytes 884768 | tf_op jit(solution)/shard_map/ppermute | solution.py:562
  70.5 7.5 %collective-permute-done.3.rest_1_ = bf16[208,768]{1,0:T(8,128)(2,1)S(1)} collective-permute-done((bf16[208,768]{1,0:T(8,128)(2,1)S(1)}, bf16[208,768]{1,0:T(8,128)(2,1)S(1)}, u32[]{:S(2)}, u32[]{:S(2)}) %collective-permute-start.3) | collective-permute-done | bytes 319520 | tf_op jit(solution)/shard_map/ppermute | solution.py:562
  85.2 13.2 %shard_map.273 = (f32[384,768]{1,0:T(8,128)}, bf16[4,384,768]{2,1,0:T(8,128)(2,1)}, bf16[4,384,768]{2,1,0:T(8,128)(2,1)}) custom-call(s32[12]{0:T(128)} %compare_select_fusion.block.blocks.refs_0_, f32[384,768]{1,0:T(8,128)} %get-tuple-element.188.mixed, f32[2,768]{1,0:T(2,128)} %gain.7, f32[2,768]{1,0:T(2,128)} %shift.7, f32[2,768]{1,0:T(2,128)} %b_down.3, ...), custom_call_target="tpu_custom_call" | custom-call | flops 3623878656 | bytes 20971520 | tf_op jit(solution)/shard_map/pallas_call | solution.py:258
  104.4 8.4 %shard_map.274 = (bf16[384,768]{1,0:T(8,128)(2,1)}, bf16[384,768]{1,0:T(8,128)(2,1)}, bf16[384,768]{1,0:T(8,128)(2,1)}, bf16[3,6,256,128]{3,2,1,0:T(8,128)(2,1)}...) custom-call(f32[384,768]{1,0:T(8,128)} %get-tuple-element.200.refs_0_.refs_2_, f32[3,128,128]{2,1,0:T(8,128)} %broadcast_in_dim.32.refs_1_, ...), custom_call_target="tpu_custom_call" | custom-call | flops 1811939328 | bytes 14680064 | tf_op jit(solution)/shard_map/pallas_call | solution.py:167
  112.8 10.1 %collective-permute-done.16.rest_7_.rest_3_ = bf16[2,3,96,768]{3,2,1,0:T(8,128)(2,1)} collective-permute-done((bf16[2,3,96,768]{3,2,1,0:T(8,128)(2,1)S(1)}, bf16[2,3,96,768]{3,2,1,0:T(8,128)(2,1)}, u32[]{:S(2)}, u32[]{:S(2)}) %collective-permute-start.16) | collective-permute-done | bytes 884768 | tf_op jit(solution)/shard_map/ppermute | solution.py:562
  127.3 12.6 %shard_map.275 = (bf16[384,768]{1,0:T(8,128)(2,1)}, bf16[4,384,768]{2,1,0:T(8,128)(2,1)}, bf16[4,384,768]{2,1,0:T(8,128)(2,1)}) custom-call(s32[12]{0:T(128)} %compare_select_fusion.block.blocks.refs_0_, f32[384,768]{1,0:T(8,128)} %get-tuple-element.202.mixed, f32[2,768]{1,0:T(2,128)} %gain.7, f32[2,768]{1,0:T(2,128)} %shift.7, f32[2,768]{1,0:T(2,128)} %b_down.3, ...), custom_call_target="tpu_custom_call" | custom-call | flops 3623878656 | bytes 20971520 | tf_op jit(solution)/shard_map/pallas_call | solution.py:258
  139.9 16.8 %shard_map.276 = (f32[384,768]{1,0:T(8,128)}, f32[8,768]{1,0:T(8,128)}, f32[4,1,768]{2,1,0:T(1,128)}, bf16[4,3,2,2,2,96,256]{6,5,4,3,2,1,0:T(8,128)(2,1)}, bf16[4,3,2,2,2,96,256]{6,5,4,3,2,1,0:T(8,128)(2,1)}) custom-call(s32[12]{0:T(128)} %compare_select_fusion.block.blocks.refs_0_, bf16[384,768]{1,0:T(8,128)(2,1)} %bitcast.74, ...), custom_call_target="tpu_custom_call" | custom-call | flops 7247757312 | bytes 31457280 | tf_op jit(solution)/shard_map/pallas_call | solution.py:359
  156.9 15.1 %shard_map.277 = (f32[384,768]{1,0:T(8,128)}, f32[8,768]{1,0:T(8,128)}, bf16[2,2,2,2,3,96,256]{6,5,4,3,2,1,0:T(8,128)(2,1)}, bf16[2,2,2,2,3,96,256]{6,5,4,3,2,1,0:T(8,128)(2,1)}) custom-call(s32[12]{0:T(128)} %compare_select_fusion.block.blocks.refs_0_, f32[384,768]{1,0:T(8,128)} %get-tuple-element.208.refs_1_, ...), custom_call_target="tpu_custom_call" | custom-call | flops 3623878656 | bytes 25165824 | tf_op jit(solution)/shard_map/pallas_call | solution.py:482
  179.8 16.7 %shard_map.279 = (f32[384,768]{1,0:T(8,128)}, f32[8,768]{1,0:T(8,128)}, f32[4,1,768]{2,1,0:T(1,128)}, bf16[4,3,2,2,2,96,256]{6,5,4,3,2,1,0:T(8,128)(2,1)}, bf16[4,3,2,2,2,96,256]{6,5,4,3,2,1,0:T(8,128)(2,1)}) custom-call(s32[12]{0:T(128)} %compare_select_fusion.block.blocks.refs_0_, f32[384,768]{1,0:T(8,128)} %get-tuple-element.214.grad_out, ...), custom_call_target="tpu_custom_call" | custom-call | flops 7247757312 | bytes 31457280 | tf_op jit(solution)/shard_map/pallas_call | solution.py:359
  199.2 4.9 %shard_map.280 = (bf16[20,96,256]{2,1,0:T(8,128)(2,1)}, bf16[8,96,256]{2,1,0:T(8,128)(2,1)}, bf16[20,96,256]{2,1,0:T(8,128)(2,1)}) custom-call(s32[12]{0:T(128)} %compare_select_fusion.block.blocks.refs_0_, bf16[2,2,3,2,2,2,96,256]{7,6,5,4,3,2,1,0:T(8,128)(2,1)} %bitcast.58, ...), custom_call_target="tpu_custom_call" | custom-call | tf_op jit(solution)/shard_map/pallas_call | solution.py:795
  206.0 15.5 %shard_map.281 = (f32[384,768]{1,0:T(8,128)}, f32[8,768]{1,0:T(8,128)}, bf16[2,2,2,2,3,96,256]{6,5,4,3,2,1,0:T(8,128)(2,1)}, bf16[2,2,2,2,3,96,256]{6,5,4,3,2,1,0:T(8,128)(2,1)}) custom-call(s32[12]{0:T(128)} %compare_select_fusion.block.blocks.refs_0_, f32[384,768]{1,0:T(8,128)} %get-tuple-element.223.refs_1_, bf16[384,768]{1,0:T(8,128)(2,1)} %bitcast.71, ...), custom_call_target="tpu_custom_call" | custom-call | flops 3623878656 | bytes 25165824 | tf_op jit(solution)/shard_map/pallas_call | solution.py:482
  221.4 7.1 %collective-permute-done.28.refs_7_.refs_22_.refs_12_.refs_3_ = bf16[20,96,256]{2,1,0:T(8,128)(2,1)S(1)} collective-permute-done((bf16[20,96,256]{2,1,0:T(8,128)(2,1)}, bf16[20,96,256]{2,1,0:T(8,128)(2,1)S(1)}, u32[]{:S(2)}, u32[]{:S(2)}) %collective-permute-start.28) | collective-permute-done | bytes 983072 | tf_op jit(solution)/shard_map/ppermute | solution.py:562
  230.3 7.0 %shard_map.282 = (bf16[26,96,256]{2,1,0:T(8,128)(2,1)}, bf16[26,96,256]{2,1,0:T(8,128)(2,1)}, bf16[16,96,256]{2,1,0:T(8,128)(2,1)}, bf16[4,96,256]{2,1,0:T(8,128...) custom-call(s32[12]{0:T(128)} %compare_select_fusion.block.blocks.refs_0_, ...), custom_call_target="tpu_custom_call" | custom-call | tf_op jit(solution)/shard_map/pallas_call | solution.py:795
  243.4 17.6 %collective-permute-done.35.refs_13_.refs_27_.refs_4_ = bf16[4,96,256]{2,1,0:T(8,128)(2,1)S(1)} collective-permute-done((bf16[4,96,256]{2,1,0:T(8,128)(2,1)}, bf16[4,96,256]{2,1,0:T(8,128)(2,1)S(1)}, u32[]{:S(2)}, u32[]{:S(2)}) %collective-permute-start.35) | collective-permute-done | bytes 196640 | tf_op jit(solution)/shard_map/ppermute | solution.py:562
  262.9 5.2 %collective-permute-done.32.refs_4_.refs_25_.refs_5_.refs_6_.refs_12_ = bf16[26,96,256]{2,1,0:T(8,128)(2,1)S(1)} collective-permute-done((bf16[26,96,256]{2,1,0:T(8,128)(2,1)}, bf16[26,96,256]{2,1,0:T(8,128)(2,1)S(1)}, u32[]{:S(2)}, u32[]{:S(2)}) %collective-permute-start.32) | collective-permute-done | bytes 1277984 | tf_op jit(solution)/shard_map/ppermute | solution.py:562
  269.2 7.7 %shard_map.284 = (bf16[20,96,256]{2,1,0:T(8,128)(2,1)}, bf16[13,96,256]{2,1,0:T(8,128)(2,1)}, bf16[21,96,256]{2,1,0:T(8,128)(2,1)}, bf16[7,96,256]{2,1,0:T(8,128...) custom-call(s32[12]{0:T(128)} %compare_select_fusion.block.blocks.refs_0_, ...), custom_call_target="tpu_custom_call" | custom-call | tf_op jit(solution)/shard_map/pallas_call | solution.py:795
  283.4 21.6 %collective-permute-done.41.refs_18_.refs_13_ = bf16[3,96,256]{2,1,0:T(8,128)(2,1)} collective-permute-done((bf16[3,96,256]{2,1,0:T(8,128)(2,1)}, bf16[3,96,256]{2,1,0:T(8,128)(2,1)}, u32[]{:S(2)}, u32[]{:S(2)}) %collective-permute-start.41) | collective-permute-done | bytes 147488 | tf_op jit(solution)/shard_map/ppermute | solution.py:562
  328.2 5.3 %shard_map.288 = (bf16[5,96,256]{2,1,0:T(8,128)(2,1)}, bf16[7,96,256]{2,1,0:T(8,128)(2,1)}, bf16[3,96,256]{2,1,0:T(8,128)(2,1)}, bf16[1,96,256]{2,1,0:T(8,128)(2,1)}, f32[96,768]{1,0:T(8,128)}) custom-call(s32[12]{0:T(128)} %compare_select_fusion.block.blocks.refs_0_, bf16[2,2,3,2,2,2,96,256]{7,6,5,4,3,2,1,0:T(8,128)(2,1)} %bitcast.55, ...), custom_call_target="tpu_custom_call" | custom-call | tf_op jit(solution)/shard_map/pallas_call | solution.py:795
  343.1 9.7 %collective-permute-done.49.refs_13_ = bf16[3,96,256]{2,1,0:T(8,128)(2,1)S(1)} collective-permute-done((bf16[3,96,256]{2,1,0:T(8,128)(2,1)}, bf16[3,96,256]{2,1,0:T(8,128)(2,1)S(1)}, u32[]{:S(2)}, u32[]{:S(2)}) %collective-permute-start.49) | collective-permute-done | bytes 147488 | tf_op jit(solution)/shard_map/ppermute | solution.py:562
  355.6 4.6 %shard_map.290 = (f32[2,96,768]{2,1,0:T(8,128)}, f32[2,96,768]{2,1,0:T(8,128)}, f32[2,96,192]{2,1,0:T(8,128)}, f32[2,96,192]{2,1,0:T(8,128)}, f32[2,96,192]{2,1,...) custom-call(s32[12]{0:T(128)} %compare_select_fusion.block.blocks.re, ...), custom_call_target="tpu_custom_call", output_to_operand_aliasing={{0}: (21, {}), {1}: (22, {}), {2}: (23, {}), {3}: (24, {}),... | custom-call | tf_op jit(solution)/shard_map/pallas_call | solution.py:918
  (196 shorter events, 105.9 us)
Async XLA Ops:
  9.2 27.4 %collective-permute-start = (bf16[208,768]{1,0:T(8,128)(2,1)}, bf16[208,768]{1,0:T(8,128)(2,1)S(1)}, u32[]{:S(2)}, u32[]{:S(2)}) collective-permute-start(bf16[208,768]{1,0:T(8,128)(2,1)} %get-tuple-element.199.rest_0_.rest_14_.refs_9_), channel_id=1, source_target_pairs={{0,2},{1,3},{2,0},{3,1},{4,6},{5,7},{6,4},{7,5},{8,10},{9,11},{10,... | collective-permute-start | bytes 958472 | tf_op jit(solution)/shard_map/ppermute | solution.py:562
  49.7 19.6 %collective-permute-start.8 = (bf16[2,3,96,768]{3,2,1,0:T(8,128)(2,1)S(1)}, bf16[2,3,96,768]{3,2,1,0:T(8,128)(2,1)S(1)}, u32[]{:S(2)}, u32[]{:S(2)}) collective-permute-start(bf16[2,3,96,768]{3,2,1,0:T(8,128)(2,1)S(1)} %pad_maximum_fusion.rest_6_.rest_2_), channel_id=1, source_target_pairs={{0,16},{4,20},{8,24},{12,28},{16,0},{20,4},{24,8},{28,12},{1,17},{... | collective-permute-start | bytes 2654216 | tf_op jit(solution)/shard_map/ppermute | solution.py:562
  54.1 23.9 %collective-permute-start.3 = (bf16[208,768]{1,0:T(8,128)(2,1)S(1)}, bf16[208,768]{1,0:T(8,128)(2,1)S(1)}, u32[]{:S(2)}, u32[]{:S(2)}) collective-permute-start(bf16[208,768]{1,0:T(8,128)(2,1)S(1)} %copy-done.32), channel_id=1, source_target_pairs={{0,2},{1,3},{2,0},{3,1},{4,6},{5,7},{6,4},{7,5},{8,10},{9,11},{10,... | collective-permute-start | bytes 958472 | tf_op jit(solution)/shard_map/ppermute | solution.py:562
  101.1 21.9 %collective-permute-start.16 = (bf16[2,3,96,768]{3,2,1,0:T(8,128)(2,1)S(1)}, bf16[2,3,96,768]{3,2,1,0:T(8,128)(2,1)}, u32[]{:S(2)}, u32[]{:S(2)}) collective-permute-start(bf16[2,3,96,768]{3,2,1,0:T(8,128)(2,1)S(1)} %pad_maximum_fusion.2.rest_6_.rest_2_), channel_id=1, source_target_pairs={{0,16},{4,20},{8,24},{12,28},{16,0},{20,4},{24,8},{28,12},{1,17},{... | collective-permute-start | bytes 2654216 | tf_op jit(solution)/shard_map/ppermute | solution.py:562
  101.8 21.5 %collective-permute-start.17 = (bf16[2,3,96,768]{3,2,1,0:T(8,128)(2,1)S(1)}, bf16[2,3,96,768]{3,2,1,0:T(8,128)(2,1)}, u32[]{:S(2)}, u32[]{:S(2)}) collective-permute-start(bf16[2,3,96,768]{3,2,1,0:T(8,128)(2,1)S(1)} %pad_maximum_fusion.3.rest_8_.rest_4_), channel_id=1, source_target_pairs={{0,8},{4,12},{8,0},{12,4},{16,24},{20,28},{24,16},{28,20},{1,9},{5... | collective-permute-start | bytes 2654216 | tf_op jit(solution)/shard_map/ppermute | solution.py:562
  103.1 20.7 %collective-permute-start.18 = (bf16[2,3,96,768]{3,2,1,0:T(8,128)(2,1)S(1)}, bf16[2,3,96,768]{3,2,1,0:T(8,128)(2,1)}, u32[]{:S(2)}, u32[]{:S(2)}) collective-permute-start(bf16[2,3,96,768]{3,2,1,0:T(8,128)(2,1)S(1)} %pad_maximum_fusion.2.rest_6_.rest_2_), channel_id=1, source_target_pairs={{0,4},{4,0},{8,12},{12,8},{16,20},{20,16},{24,28},{28,24},{1,5},{5... | collective-permute-start | bytes 2654216 | tf_op jit(solution)/shard_map/ppermute | solution.py:562
  103.1 20.7 %collective-permute-start.20 = (bf16[2,3,96,768]{3,2,1,0:T(8,128)(2,1)S(1)}, bf16[2,3,96,768]{3,2,1,0:T(8,128)(2,1)}, u32[]{:S(2)}, u32[]{:S(2)}) collective-permute-start(bf16[2,3,96,768]{3,2,1,0:T(8,128)(2,1)S(1)} %pad_maximum_fusion.3.rest_8_.rest_4_), channel_id=1, source_target_pairs={{0,4},{4,0},{8,12},{12,8},{16,20},{20,16},{24,28},{28,24},{1,5},{5... | collective-permute-start | bytes 2654216 | tf_op jit(solution)/shard_map/ppermute | solution.py:562
  176.5 22.7 %collective-permute-start.26 = (bf16[2,2,2,2,3,96,256]{6,5,4,3,2,1,0:T(8,128)(2,1)}, bf16[2,2,2,2,3,96,256]{6,5,4,3,2,1,0:T(8,128)(2,1)}, u32[]{:S(2)}, u32[]{:S(2)}) collective-permute-start(bf16[2,2,2,2,3,96,256]{6,5,4,3,2,1,0:T(8,128)(2,1)} %get-tuple-element.235), channel_id=1, source_target_pairs={{0,4},{4,0},{8,12},{12,8},{16,20},{20,16},{24,28},{28,24},{1,5},{5... | collective-permute-start | bytes 7077896 | tf_op jit(solution)/shard_map/ppermute | solution.py:562
  176.9 19.8 %collective-permute-start.23 = (bf16[16,96,256]{2,1,0:T(8,128)(2,1)}, bf16[16,96,256]{2,1,0:T(8,128)(2,1)S(1)}, u32[]{:S(2)}, u32[]{:S(2)}) collective-permute-start(bf16[16,96,256]{2,1,0:T(8,128)(2,1)} %get-tuple-element.231.rest_10_), channel_id=1, source_target_pairs={{0,8},{4,12},{8,0},{12,4},{16,24},{20,28},{24,16},{28,20},{1,9},{5... | collective-permute-start | bytes 2359304 | tf_op jit(solution)/shard_map/ppermute | solution.py:562
  178.3 19.5 %collective-permute-start.24 = (bf16[16,96,256]{2,1,0:T(8,128)(2,1)}, bf16[16,96,256]{2,1,0:T(8,128)(2,1)S(1)}, u32[]{:S(2)}, u32[]{:S(2)}) collective-permute-start(bf16[16,96,256]{2,1,0:T(8,128)(2,1)} %get-tuple-element.232.rest_11_), channel_id=1, source_target_pairs={{0,16},{4,20},{8,24},{12,28},{16,0},{20,4},{24,8},{28,12},{1,17},{... | collective-permute-start | bytes 2359304 | tf_op jit(solution)/shard_map/ppermute | solution.py:562
  179.8 19.4 %collective-permute-start.25 = (bf16[16,96,256]{2,1,0:T(8,128)(2,1)}, bf16[16,96,256]{2,1,0:T(8,128)(2,1)}, u32[]{:S(2)}, u32[]{:S(2)}) collective-permute-start(bf16[16,96,256]{2,1,0:T(8,128)(2,1)} %get-tuple-element.233.rest_12_), channel_id=1, source_target_pairs={{0,1},{1,0},{2,3},{3,2},{4,5},{5,4},{6,7},{7,6},{8,9},{9,8},{10,11... | collective-permute-start | bytes 2359304 | tf_op jit(solution)/shard_map/ppermute | solution.py:562
  204.1 25.2 %collective-permute-start.27 = (bf16[4,3,2,2,2,96,256]{6,5,4,3,2,1,0:T(8,128)(2,1)}, bf16[4,3,2,2,2,96,256]{6,5,4,3,2,1,0:T(8,128)(2,1)}, u32[]{:S(2)}, u32[]{:S(2)}) collective-permute-start(bf16[4,3,2,2,2,96,256]{6,5,4,3,2,1,0:T(8,128)(2,1)} %get-tuple-element.243), channel_id=1, source_target_pairs={{0,4},{4,0},{8,12},{12,8},{16,20},{20,16},{24,28},{28,24},{1,5},{5... | collective-permute-start | bytes 14155784 | tf_op jit(solution)/shard_map/ppermute | solution.py:562
  204.2 24.4 %collective-permute-start.28 = (bf16[20,96,256]{2,1,0:T(8,128)(2,1)}, bf16[20,96,256]{2,1,0:T(8,128)(2,1)S(1)}, u32[]{:S(2)}, u32[]{:S(2)}) collective-permute-start(bf16[20,96,256]{2,1,0:T(8,128)(2,1)} %get-tuple-element.244.refs_16_), channel_id=1, source_target_pairs={{0,16},{4,20},{8,24},{12,28},{16,0},{20,4},{24,8},{28,12},{1,17},{... | collective-permute-start | bytes 2949128 | tf_op jit(solution)/shard_map/ppermute | solution.py:562
  205.3 24.0 %collective-permute-start.30 = (bf16[20,96,256]{2,1,0:T(8,128)(2,1)}, bf16[20,96,256]{2,1,0:T(8,128)(2,1)S(1)}, u32[]{:S(2)}, u32[]{:S(2)}) collective-permute-start(bf16[20,96,256]{2,1,0:T(8,128)(2,1)} %get-tuple-element.246.refs_18_), channel_id=1, source_target_pairs={{0,8},{4,12},{8,0},{12,4},{16,24},{20,28},{24,16},{28,20},{1,9},{5... | collective-permute-start | bytes 2949128 | tf_op jit(solution)/shard_map/ppermute | solution.py:562
  237.4 31.6 %collective-permute-start.34 = (bf16[2,2,2,2,3,96,256]{6,5,4,3,2,1,0:T(8,128)(2,1)}, bf16[2,2,2,2,3,96,256]{6,5,4,3,2,1,0:T(8,128)(2,1)}, u32[]{:S(2)}, u32[]{:S(2)}) collective-permute-start(bf16[2,2,2,2,3,96,256]{6,5,4,3,2,1,0:T(8,128)(2,1)} %get-tuple-element.261), channel_id=1, source_target_pairs={{0,4},{4,0},{8,12},{12,8},{16,20},{20,16},{24,28},{28,24},{1,5},{5... | collective-permute-start | bytes 7077896 | tf_op jit(solution)/shard_map/ppermute | solution.py:562
  237.5 30.7 %collective-permute-start.32 = (bf16[26,96,256]{2,1,0:T(8,128)(2,1)}, bf16[26,96,256]{2,1,0:T(8,128)(2,1)S(1)}, u32[]{:S(2)}, u32[]{:S(2)}) collective-permute-start(bf16[26,96,256]{2,1,0:T(8,128)(2,1)} %get-tuple-element.258), channel_id=1, source_target_pairs={{0,16},{4,20},{8,24},{12,28},{16,0},{20,4},{24,8},{28,12},{1,17},{... | collective-permute-start | bytes 3833864 | tf_op jit(solution)/shard_map/ppermute | solution.py:562
  238.5 30.5 %collective-permute-start.31 = (bf16[26,96,256]{2,1,0:T(8,128)(2,1)}, bf16[26,96,256]{2,1,0:T(8,128)(2,1)}, u32[]{:S(2)}, u32[]{:S(2)}) collective-permute-start(bf16[26,96,256]{2,1,0:T(8,128)(2,1)} %get-tuple-element.257.source), channel_id=1, source_target_pairs={{0,8},{4,12},{8,0},{12,4},{16,24},{20,28},{24,16},{28,20},{1,9},{5... | collective-permute-start | bytes 3833864 | tf_op jit(solution)/shard_map/ppermute | solution.py:562
  239.1 23.9 %collective-permute-start.33 = (bf16[16,96,256]{2,1,0:T(8,128)(2,1)}, bf16[16,96,256]{2,1,0:T(8,128)(2,1)}, u32[]{:S(2)}, u32[]{:S(2)}) collective-permute-start(bf16[16,96,256]{2,1,0:T(8,128)(2,1)} %get-tuple-element.259), channel_id=1, source_target_pairs={{0,1},{1,0},{2,3},{3,2},{4,5},{5,4},{6,7},{7,6},{8,9},{9,8},{10,11... | collective-permute-start | bytes 2359304 | tf_op jit(solution)/shard_map/ppermute | solution.py:562
  276.9 28.2 %collective-permute-start.39 = (bf16[21,96,256]{2,1,0:T(8,128)(2,1)}, bf16[21,96,256]{2,1,0:T(8,128)(2,1)S(1)}, u32[]{:S(2)}, u32[]{:S(2)}) collective-permute-start(bf16[21,96,256]{2,1,0:T(8,128)(2,1)} %get-tuple-element.272), channel_id=1, source_target_pairs={{0,8},{4,12},{8,0},{12,4},{16,24},{20,28},{24,16},{28,20},{1,9},{5... | collective-permute-start | bytes 3096584 | tf_op jit(solution)/shard_map/ppermute | solution.py:562
  277.5 27.6 %collective-permute-start.37 = (bf16[20,96,256]{2,1,0:T(8,128)(2,1)}, bf16[20,96,256]{2,1,0:T(8,128)(2,1)}, u32[]{:S(2)}, u32[]{:S(2)}) collective-permute-start(bf16[20,96,256]{2,1,0:T(8,128)(2,1)} %get-tuple-element.270.source), channel_id=1, source_target_pairs={{0,16},{4,20},{8,24},{12,28},{16,0},{20,4},{24,8},{28,12},{1,17},{... | collective-permute-start | bytes 2949128 | tf_op jit(solution)/shard_map/ppermute | solution.py:562
  278.5 26.6 %collective-permute-start.38 = (bf16[13,96,256]{2,1,0:T(8,128)(2,1)}, bf16[13,96,256]{2,1,0:T(8,128)(2,1)S(1)}, u32[]{:S(2)}, u32[]{:S(2)}) collective-permute-start(bf16[13,96,256]{2,1,0:T(8,128)(2,1)} %get-tuple-element.271), channel_id=1, source_target_pairs={{0,1},{1,0},{2,3},{3,2},{4,5},{5,4},{6,7},{7,6},{8,9},{9,8},{10,11... | collective-permute-start | bytes 1916936 | tf_op jit(solution)/shard_map/ppermute | solution.py:562
  279.0 26.0 %collective-permute-start.40 = (bf16[7,96,256]{2,1,0:T(8,128)(2,1)}, bf16[7,96,256]{2,1,0:T(8,128)(2,1)S(1)}, u32[]{:S(2)}, u32[]{:S(2)}) collective-permute-start(bf16[7,96,256]{2,1,0:T(8,128)(2,1)} %get-tuple-element.273), channel_id=1, source_target_pairs={{0,2},{1,3},{2,0},{3,1},{4,6},{5,7},{6,4},{7,5},{8,10},{9,11},{10,... | collective-permute-start | bytes 1032200 | tf_op jit(solution)/shard_map/ppermute | solution.py:562
  280.8 24.3 %collective-permute-start.41 = (bf16[3,96,256]{2,1,0:T(8,128)(2,1)}, bf16[3,96,256]{2,1,0:T(8,128)(2,1)}, u32[]{:S(2)}, u32[]{:S(2)}) collective-permute-start(bf16[3,96,256]{2,1,0:T(8,128)(2,1)} %get-tuple-element.274), channel_id=1, source_target_pairs={{0,3},{1,2},{2,1},{3,0},{4,7},{5,6},{6,5},{7,4},{8,11},{9,10},{10,... | collective-permute-start | bytes 442376 | tf_op jit(solution)/shard_map/ppermute | solution.py:562
  333.5 21.4 %collective-permute-start.48 = (bf16[7,96,256]{2,1,0:T(8,128)(2,1)}, bf16[7,96,256]{2,1,0:T(8,128)(2,1)S(1)}, u32[]{:S(2)}, u32[]{:S(2)}) collective-permute-start(bf16[7,96,256]{2,1,0:T(8,128)(2,1)} %get-tuple-element.285), channel_id=1, source_target_pairs={{0,2},{1,3},{2,0},{3,1},{4,6},{5,7},{6,4},{7,5},{8,10},{9,11},{10,... | collective-permute-start | bytes 1032200 | tf_op jit(solution)/shard_map/ppermute | solution.py:562
  (64 other events, 606.3 us)

commit v6 on v5

--- a/solution.py
+++ b/solution.py
@@ -1040,16 +1040,15 @@
         near_1 = [swap(ups, "dp", 2), swap(downs, "dp", 4)]
         core_0 = other_core(ups_0, side_0[0], downs_0, side_0[1])
         pieces_0 = far_pieces(0, w_up, w_down, [owns[0]] + far_0, [ups_0, side_0[0], downs_0, side_0[1]], core_0, blocks)
+        near_1 = chain.tie(*near_1)
+        ups_1, downs_1 = chain.tie(in_order(2, ups, near_1[0]), in_order(4, downs, near_1[1]))
+        side_1 = [swap(ups_1, "dp", 4), swap(downs_1, "dp", 2)]
         fed_0 = list(feed_layer(0, kept_0[5], pieces_0, chain.ties()))
         chain.need((fed_0, 0))
-        near_1 = chain.tie(*near_1)
+        ups_1, downs_1, *side_1 = chain.tie(ups_1, downs_1, *side_1)
         result_0, active_0, slope_0 = fed_0
-        ups_1, downs_1 = chain.tie(in_order(2, ups, near_1[0]), in_order(4, downs, near_1[1]))
-        side_1 = [swap(ups_1, "dp", 4), swap(downs_1, "dp", 2)]
-        kept_1 = list(attend_layer(1, result_0, chain.ties()))
-        chain.need((kept_1, 5))
-        side_1 = chain.tie(*side_1)
         core_1 = other_core(ups_1, side_1[0], downs_1, side_1[1])
+        kept_1 = list(attend_layer(1, result_0, side_1))
         pieces_1 = far_pieces(1, w_up, w_down, [owns[1]] + far_1, [ups_1, side_1[0], downs_1, side_1[1]], core_1, blocks)
     else:
         pieces_0 = gathered_pieces(0, w_up, w_down, b_up, blocks)

time: 366 us -> 362 us (0.989)
  transfers between devices with their start and end apart: 51 -> 51, of which waited for: 29 -> 27; matrix products, arithmetic and copies ran while one was open for 1% -> 1% of each run, Pallas kernels for 23% -> 23%
where the time goes in v6:
time: 362 us; the launch traced here: 356 us
  Pallas kernels  153 us (42%)
  waiting for transfers between devices  140 us (39%)
  starting transfers between devices  46.7 us (13%)
  local copies, waits for them, and re-layouts  9.33 us (3%)
  other arithmetic  4.81 us (1%)
    ppermute x51, waiting for transfers between devices, swap(): return lax.ppermute(value, axis, [(at, at ^ bit) for at in range(size)])  140 us
    ppermute x51, starting transfers between devices, swap(): return lax.ppermute(value, axis, [(at, at ^ bit) for at in range(size)])  46.7 us
    pallas_call x6, Pallas kernels, exchange(): pl.pallas_call(functools.partial(exchange_kernel, plan), out_shape=outs +...  33.8 us
    pallas_call x2, Pallas kernels, feed_back(): pl.pallas_call(functools.partial(feed_back_kernel, layer, pieces, joint,...  33.5 us
    pallas_call x2, Pallas kernels, attend_back(): pl.pallas_call(body, out_shape=[jax.ShapeDtypeStruct((rows, width), F32),...  30.6 us
    pallas_call x2, Pallas kernels, feed(): pl.pallas_call(functools.partial(feed_kernel, layer, pieces, len(ties)),...  25.8 us
    pallas_call x2, Pallas kernels, attend(): pl.pallas_call(body, out_shape=outs, in_specs=[vmem] * 5 + [pl.BlockSpec(...  16.7 us
    pallas_call x2, Pallas kernels, finish(): pl.pallas_call(functools.partial(finish_kernel, (wide_plan, feed_plan, fa...  8.36 us
  transfers between devices with their start and end apart: 51, of which 27 were waited for; matrix products, arithmetic and copies ran while one was open for 1% of the time, Pallas kernels for 23%

profile of v6, /device:TPU:0, one launch (start us, length us, event | category | flops | bytes accessed | tf_op | source)
XLA Modules:
  0.0 355.9 jit_solution(12212682631887044603)
XLA Ops:
  4.0 5.1 %collective-permute-start.2 = (bf16[208,768]{1,0:T(8,128)(2,1)}, bf16[208,768]{1,0:T(8,128)(2,1)S(1)}, u32[]{:S(2)}, u32[]{:S(2)}) collective-permute-start(bf16[208,768]{1,0:T(8,128)(2,1)} %get-tuple-element.194.rest_0_.rest_14_), channel_id=1, source_target_pairs={{0,3},{1,2},{2,1},{3,0},{4,7},{5,6},{6,5},{7,4},{8,11},{9,10},{10,... | collective-permute-start | bytes 958472 | tf_op jit(solution)/shard_map/ppermute | solution.py:562
  12.0 8.3 %shard_map.272 = (bf16[384,768]{1,0:T(8,128)(2,1)}, bf16[384,768]{1,0:T(8,128)(2,1)}, bf16[384,768]{1,0:T(8,128)(2,1)}, bf16[3,6,256,128]{3,2,1,0:T(8,128)(2,1)}...) custom-call(bf16[384,768]{1,0:T(8,128)(2,1)} %bitcast.70, ...), custom_call_target="tpu_custom_call" | custom-call | flops 1811939328 | bytes 14680064 | tf_op jit(solution)/shard_map/pallas_call | solution.py:167
  24.9 11.7 %collective-permute-done.rest_1_ = bf16[208,768]{1,0:T(8,128)(2,1)S(1)} collective-permute-done((bf16[208,768]{1,0:T(8,128)(2,1)}, bf16[208,768]{1,0:T(8,128)(2,1)S(1)}, u32[]{:S(2)}, u32[]{:S(2)}) %collective-permute-start) | collective-permute-done | bytes 319520 | tf_op jit(solution)/shard_map/ppermute | solution.py:562
  39.9 8.2 %collective-permute-done.6 = bf16[3,96,768]{2,1,0:T(8,128)(2,1)S(1)} collective-permute-done((bf16[3,96,768]{2,1,0:T(8,128)(2,1)S(1)}, bf16[3,96,768]{2,1,0:T(8,128)(2,1)S(1)}, u32[]{:S(2)}, u32[]{:S(2)}) %collective-permute-start.6) | collective-permute-done | bytes 442400 | tf_op jit(solution)/shard_map/ppermute | solution.py:562
  56.2 13.1 %collective-permute-done.8.rest_7_.rest_3_ = bf16[2,3,96,768]{3,2,1,0:T(8,128)(2,1)S(1)} collective-permute-done((bf16[2,3,96,768]{3,2,1,0:T(8,128)(2,1)S(1)}, bf16[2,3,96,768]{3,2,1,0:T(8,128)(2,1)S(1)}, u32[]{:S(2)}, u32[]{:S(2)}) %collective-permute-start.8) | collective-permute-done | bytes 884768 | tf_op jit(solution)/shard_map/ppermute | solution.py:562
  70.5 7.5 %collective-permute-done.3.rest_1_ = bf16[208,768]{1,0:T(8,128)(2,1)S(1)} collective-permute-done((bf16[208,768]{1,0:T(8,128)(2,1)S(1)}, bf16[208,768]{1,0:T(8,128)(2,1)S(1)}, u32[]{:S(2)}, u32[]{:S(2)}) %collective-permute-start.3) | collective-permute-done | bytes 319520 | tf_op jit(solution)/shard_map/ppermute | solution.py:562
  81.4 6.6 %collective-permute-done.10 = bf16[3,96,768]{2,1,0:T(8,128)(2,1)S(1)} collective-permute-done((bf16[3,96,768]{2,1,0:T(8,128)(2,1)S(1)}, bf16[3,96,768]{2,1,0:T(8,128)(2,1)S(1)}, u32[]{:S(2)}, u32[]{:S(2)}) %collective-permute-start.10) | collective-permute-done | bytes 442400 | tf_op jit(solution)/shard_map/ppermute | solution.py:562
  94.1 13.2 %shard_map.273 = (f32[384,768]{1,0:T(8,128)}, bf16[4,384,768]{2,1,0:T(8,128)(2,1)}, bf16[4,384,768]{2,1,0:T(8,128)(2,1)}) custom-call(s32[12]{0:T(128)} %compare_select_fusion.block.blocks.refs_0_, f32[384,768]{1,0:T(8,128)} %get-tuple-element.195.mixed, f32[2,768]{1,0:T(2,128)} %gain.7, f32[2,768]{1,0:T(2,128)} %shift.7, f32[2,768]{1,0:T(2,128)} %b_down.3, ...), custom_call_target="tpu_custom_call" | custom-call | flops 3623878656 | bytes 20971520 | tf_op jit(solution)/shard_map/pallas_call | solution.py:258
  107.2 5.2 %collective-permute-done.12.refs_9_.rest_7_.rest_3_ = bf16[2,3,96,768]{3,2,1,0:T(8,128)(2,1)S(1)} collective-permute-done((bf16[2,3,96,768]{3,2,1,0:T(8,128)(2,1)}, bf16[2,3,96,768]{3,2,1,0:T(8,128)(2,1)S(1)}, u32[]{:S(2)}, u32[]{:S(2)}) %collective-permute-start.12) | collective-permute-done | bytes 884768 | tf_op jit(solution)/shard_map/ppermute | solution.py:562
  114.6 8.4 %shard_map.274 = (bf16[384,768]{1,0:T(8,128)(2,1)}, bf16[384,768]{1,0:T(8,128)(2,1)}, bf16[384,768]{1,0:T(8,128)(2,1)}, bf16[3,6,256,128]{3,2,1,0:T(8,128)(2,1)}...) custom-call(f32[384,768]{1,0:T(8,128)} %get-tuple-element.201.refs_0_.refs_2_, f32[3,128,128]{2,1,0:T(8,128)} %broadcast_in_dim.32.refs_1_, ...), custom_call_target="tpu_custom_call" | custom-call | flops 1811939328 | bytes 14680064 | tf_op jit(solution)/shard_map/pallas_call | solution.py:167
  123.0 12.6 %shard_map.275 = (bf16[384,768]{1,0:T(8,128)(2,1)}, bf16[4,384,768]{2,1,0:T(8,128)(2,1)}, bf16[4,384,768]{2,1,0:T(8,128)(2,1)}) custom-call(s32[12]{0:T(128)} %compare_select_fusion.block.blocks.refs_0_, f32[384,768]{1,0:T(8,128)} %get-tuple-element.204.mixed, f32[2,768]{1,0:T(2,128)} %gain.7, f32[2,768]{1,0:T(2,128)} %shift.7, f32[2,768]{1,0:T(2,128)} %b_down.3, ...), custom_call_target="tpu_custom_call" | custom-call | flops 3623878656 | bytes 20971520 | tf_op jit(solution)/shard_map/pallas_call | solution.py:258
  135.7 16.8 %shard_map.276 = (f32[384,768]{1,0:T(8,128)}, f32[8,768]{1,0:T(8,128)}, f32[4,1,768]{2,1,0:T(1,128)}, bf16[4,3,2,2,2,96,256]{6,5,4,3,2,1,0:T(8,128)(2,1)}, bf16[4,3,2,2,2,96,256]{6,5,4,3,2,1,0:T(8,128)(2,1)}) custom-call(s32[12]{0:T(128)} %compare_select_fusion.block.blocks.refs_0_, bf16[384,768]{1,0:T(8,128)(2,1)} %bitcast.74, ...), custom_call_target="tpu_custom_call" | custom-call | flops 7247757312 | bytes 31457280 | tf_op jit(solution)/shard_map/pallas_call | solution.py:359
  152.6 15.1 %shard_map.277 = (f32[384,768]{1,0:T(8,128)}, f32[8,768]{1,0:T(8,128)}, bf16[2,2,2,2,3,96,256]{6,5,4,3,2,1,0:T(8,128)(2,1)}, bf16[2,2,2,2,3,96,256]{6,5,4,3,2,1,0:T(8,128)(2,1)}) custom-call(s32[12]{0:T(128)} %compare_select_fusion.block.blocks.refs_0_, f32[384,768]{1,0:T(8,128)} %get-tuple-element.210.refs_1_, ...), custom_call_target="tpu_custom_call" | custom-call | flops 3623878656 | bytes 25165824 | tf_op jit(solution)/shard_map/pallas_call | solution.py:482
  175.6 16.7 %shard_map.279 = (f32[384,768]{1,0:T(8,128)}, f32[8,768]{1,0:T(8,128)}, f32[4,1,768]{2,1,0:T(1,128)}, bf16[4,3,2,2,2,96,256]{6,5,4,3,2,1,0:T(8,128)(2,1)}, bf16[4,3,2,2,2,96,256]{6,5,4,3,2,1,0:T(8,128)(2,1)}) custom-call(s32[12]{0:T(128)} %compare_select_fusion.block.blocks.refs_0_, f32[384,768]{1,0:T(8,128)} %get-tuple-element.216.grad_out, ...), custom_call_target="tpu_custom_call" | custom-call | flops 7247757312 | bytes 31457280 | tf_op jit(solution)/shard_map/pallas_call | solution.py:359
  194.9 4.9 %shard_map.280 = (bf16[20,96,256]{2,1,0:T(8,128)(2,1)}, bf16[8,96,256]{2,1,0:T(8,128)(2,1)}, bf16[20,96,256]{2,1,0:T(8,128)(2,1)}) custom-call(s32[12]{0:T(128)} %compare_select_fusion.block.blocks.refs_0_, bf16[2,2,3,2,2,2,96,256]{7,6,5,4,3,2,1,0:T(8,128)(2,1)} %bitcast.58, ...), custom_call_target="tpu_custom_call" | custom-call | tf_op jit(solution)/shard_map/pallas_call | solution.py:795
  201.7 15.5 %shard_map.281 = (f32[384,768]{1,0:T(8,128)}, f32[8,768]{1,0:T(8,128)}, bf16[2,2,2,2,3,96,256]{6,5,4,3,2,1,0:T(8,128)(2,1)}, bf16[2,2,2,2,3,96,256]{6,5,4,3,2,1,0:T(8,128)(2,1)}) custom-call(s32[12]{0:T(128)} %compare_select_fusion.block.blocks.refs_0_, f32[384,768]{1,0:T(8,128)} %get-tuple-element.225.refs_1_, bf16[384,768]{1,0:T(8,128)(2,1)} %bitcast.71, ...), custom_call_target="tpu_custom_call" | custom-call | flops 3623878656 | bytes 25165824 | tf_op jit(solution)/shard_map/pallas_call | solution.py:482
  217.2 7.1 %collective-permute-done.28.refs_7_.refs_22_.refs_12_.refs_3_ = bf16[20,96,256]{2,1,0:T(8,128)(2,1)S(1)} collective-permute-done((bf16[20,96,256]{2,1,0:T(8,128)(2,1)}, bf16[20,96,256]{2,1,0:T(8,128)(2,1)S(1)}, u32[]{:S(2)}, u32[]{:S(2)}) %collective-permute-start.28) | collective-permute-done | bytes 983072 | tf_op jit(solution)/shard_map/ppermute | solution.py:562
  226.0 7.0 %shard_map.282 = (bf16[26,96,256]{2,1,0:T(8,128)(2,1)}, bf16[26,96,256]{2,1,0:T(8,128)(2,1)}, bf16[16,96,256]{2,1,0:T(8,128)(2,1)}, bf16[4,96,256]{2,1,0:T(8,128...) custom-call(s32[12]{0:T(128)} %compare_select_fusion.block.blocks.refs_0_, ...), custom_call_target="tpu_custom_call" | custom-call | tf_op jit(solution)/shard_map/pallas_call | solution.py:795
  238.8 17.9 %collective-permute-done.35.refs_13_.refs_27_.refs_4_ = bf16[4,96,256]{2,1,0:T(8,128)(2,1)S(1)} collective-permute-done((bf16[4,96,256]{2,1,0:T(8,128)(2,1)}, bf16[4,96,256]{2,1,0:T(8,128)(2,1)S(1)}, u32[]{:S(2)}, u32[]{:S(2)}) %collective-permute-start.35) | collective-permute-done | bytes 196640 | tf_op jit(solution)/shard_map/ppermute | solution.py:562
  258.6 5.2 %collective-permute-done.32.refs_4_.refs_25_.refs_5_.refs_6_.refs_12_ = bf16[26,96,256]{2,1,0:T(8,128)(2,1)S(1)} collective-permute-done((bf16[26,96,256]{2,1,0:T(8,128)(2,1)}, bf16[26,96,256]{2,1,0:T(8,128)(2,1)S(1)}, u32[]{:S(2)}, u32[]{:S(2)}) %collective-permute-start.32) | collective-permute-done | bytes 1277984 | tf_op jit(solution)/shard_map/ppermute | solution.py:562
  264.9 7.7 %shard_map.284 = (bf16[20,96,256]{2,1,0:T(8,128)(2,1)}, bf16[13,96,256]{2,1,0:T(8,128)(2,1)}, bf16[21,96,256]{2,1,0:T(8,128)(2,1)}, bf16[7,96,256]{2,1,0:T(8,128...) custom-call(s32[12]{0:T(128)} %compare_select_fusion.block.blocks.refs_0_, ...), custom_call_target="tpu_custom_call" | custom-call | tf_op jit(solution)/shard_map/pallas_call | solution.py:795
  279.2 21.4 %collective-permute-done.41.refs_18_.refs_13_ = bf16[3,96,256]{2,1,0:T(8,128)(2,1)} collective-permute-done((bf16[3,96,256]{2,1,0:T(8,128)(2,1)}, bf16[3,96,256]{2,1,0:T(8,128)(2,1)}, u32[]{:S(2)}, u32[]{:S(2)}) %collective-permute-start.41) | collective-permute-done | bytes 147488 | tf_op jit(solution)/shard_map/ppermute | solution.py:562
  323.9 5.3 %shard_map.288 = (bf16[5,96,256]{2,1,0:T(8,128)(2,1)}, bf16[7,96,256]{2,1,0:T(8,128)(2,1)}, bf16[3,96,256]{2,1,0:T(8,128)(2,1)}, bf16[1,96,256]{2,1,0:T(8,128)(2,1)}, f32[96,768]{1,0:T(8,128)}) custom-call(s32[12]{0:T(128)} %compare_select_fusion.block.blocks.refs_0_, bf16[2,2,3,2,2,2,96,256]{7,6,5,4,3,2,1,0:T(8,128)(2,1)} %bitcast.55, ...), custom_call_target="tpu_custom_call" | custom-call | tf_op jit(solution)/shard_map/pallas_call | solution.py:795
  338.8 9.4 %collective-permute-done.49.refs_13_ = bf16[3,96,256]{2,1,0:T(8,128)(2,1)S(1)} collective-permute-done((bf16[3,96,256]{2,1,0:T(8,128)(2,1)}, bf16[3,96,256]{2,1,0:T(8,128)(2,1)S(1)}, u32[]{:S(2)}, u32[]{:S(2)}) %collective-permute-start.49) | collective-permute-done | bytes 147488 | tf_op jit(solution)/shard_map/ppermute | solution.py:562
  (196 shorter events, 104.5 us)
Async XLA Ops:
  9.1 27.4 %collective-permute-start = (bf16[208,768]{1,0:T(8,128)(2,1)}, bf16[208,768]{1,0:T(8,128)(2,1)S(1)}, u32[]{:S(2)}, u32[]{:S(2)}) collective-permute-start(bf16[208,768]{1,0:T(8,128)(2,1)} %get-tuple-element.194.rest_0_.rest_14_), channel_id=1, source_target_pairs={{0,2},{1,3},{2,0},{3,1},{4,6},{5,7},{6,4},{7,5},{8,10},{9,11},{10,... | collective-permute-start | bytes 958472 | tf_op jit(solution)/shard_map/ppermute | solution.py:562
  49.7 19.6 %collective-permute-start.8 = (bf16[2,3,96,768]{3,2,1,0:T(8,128)(2,1)S(1)}, bf16[2,3,96,768]{3,2,1,0:T(8,128)(2,1)S(1)}, u32[]{:S(2)}, u32[]{:S(2)}) collective-permute-start(bf16[2,3,96,768]{3,2,1,0:T(8,128)(2,1)S(1)} %pad_maximum_fusion.rest_6_.rest_2_), channel_id=1, source_target_pairs={{0,16},{4,20},{8,24},{12,28},{16,0},{20,4},{24,8},{28,12},{1,17},{... | collective-permute-start | bytes 2654216 | tf_op jit(solution)/shard_map/ppermute | solution.py:562
  51.2 19.2 %collective-permute-start.9 = (bf16[2,3,96,768]{3,2,1,0:T(8,128)(2,1)S(1)}, bf16[2,3,96,768]{3,2,1,0:T(8,128)(2,1)S(1)}, u32[]{:S(2)}, u32[]{:S(2)}) collective-permute-start(bf16[2,3,96,768]{3,2,1,0:T(8,128)(2,1)S(1)} %pad_maximum_fusion.1.rest_8_.rest_4_), channel_id=1, source_target_pairs={{0,8},{4,12},{8,0},{12,4},{16,24},{20,28},{24,16},{28,20},{1,9},{5... | collective-permute-start | bytes 2654216 | tf_op jit(solution)/shard_map/ppermute | solution.py:562
  54.1 23.9 %collective-permute-start.3 = (bf16[208,768]{1,0:T(8,128)(2,1)S(1)}, bf16[208,768]{1,0:T(8,128)(2,1)S(1)}, u32[]{:S(2)}, u32[]{:S(2)}) collective-permute-start(bf16[208,768]{1,0:T(8,128)(2,1)S(1)} %copy-done.32), channel_id=1, source_target_pairs={{0,2},{1,3},{2,0},{3,1},{4,6},{5,7},{6,4},{7,5},{8,10},{9,11},{10,... | collective-permute-start | bytes 958472 | tf_op jit(solution)/shard_map/ppermute | solution.py:562
  91.3 21.1 %collective-permute-start.12 = (bf16[2,3,96,768]{3,2,1,0:T(8,128)(2,1)}, bf16[2,3,96,768]{3,2,1,0:T(8,128)(2,1)S(1)}, u32[]{:S(2)}, u32[]{:S(2)}) collective-permute-start(bf16[2,3,96,768]{3,2,1,0:T(8,128)(2,1)} %pad_maximum_fusion.2.rest_6_.rest_2_), channel_id=1, source_target_pairs={{0,16},{4,20},{8,24},{12,28},{16,0},{20,4},{24,8},{28,12},{1,17},{... | collective-permute-start | bytes 2654216 | tf_op jit(solution)/shard_map/ppermute | solution.py:562
  91.8 20.9 %collective-permute-start.13 = (bf16[2,3,96,768]{3,2,1,0:T(8,128)(2,1)}, bf16[2,3,96,768]{3,2,1,0:T(8,128)(2,1)S(1)}, u32[]{:S(2)}, u32[]{:S(2)}) collective-permute-start(bf16[2,3,96,768]{3,2,1,0:T(8,128)(2,1)} %pad_maximum_fusion.3.rest_8_.rest_4_), channel_id=1, source_target_pairs={{0,8},{4,12},{8,0},{12,4},{16,24},{20,28},{24,16},{28,20},{1,9},{5... | collective-permute-start | bytes 2654216 | tf_op jit(solution)/shard_map/ppermute | solution.py:562
  172.2 22.7 %collective-permute-start.26 = (bf16[2,2,2,2,3,96,256]{6,5,4,3,2,1,0:T(8,128)(2,1)}, bf16[2,2,2,2,3,96,256]{6,5,4,3,2,1,0:T(8,128)(2,1)}, u32[]{:S(2)}, u32[]{:S(2)}) collective-permute-start(bf16[2,2,2,2,3,96,256]{6,5,4,3,2,1,0:T(8,128)(2,1)} %get-tuple-element.237), channel_id=1, source_target_pairs={{0,4},{4,0},{8,12},{12,8},{16,20},{20,16},{24,28},{28,24},{1,5},{5... | collective-permute-start | bytes 7077896 | tf_op jit(solution)/shard_map/ppermute | solution.py:562
  172.7 19.7 %collective-permute-start.23 = (bf16[16,96,256]{2,1,0:T(8,128)(2,1)}, bf16[16,96,256]{2,1,0:T(8,128)(2,1)S(1)}, u32[]{:S(2)}, u32[]{:S(2)}) collective-permute-start(bf16[16,96,256]{2,1,0:T(8,128)(2,1)} %get-tuple-element.233.rest_10_), channel_id=1, source_target_pairs={{0,8},{4,12},{8,0},{12,4},{16,24},{20,28},{24,16},{28,20},{1,9},{5... | collective-permute-start | bytes 2359304 | tf_op jit(solution)/shard_map/ppermute | solution.py:562
  174.1 19.5 %collective-permute-start.24 = (bf16[16,96,256]{2,1,0:T(8,128)(2,1)}, bf16[16,96,256]{2,1,0:T(8,128)(2,1)S(1)}, u32[]{:S(2)}, u32[]{:S(2)}) collective-permute-start(bf16[16,96,256]{2,1,0:T(8,128)(2,1)} %get-tuple-element.234.rest_11_), channel_id=1, source_target_pairs={{0,16},{4,20},{8,24},{12,28},{16,0},{20,4},{24,8},{28,12},{1,17},{... | collective-permute-start | bytes 2359304 | tf_op jit(solution)/shard_map/ppermute | solution.py:562
  175.6 19.3 %collective-permute-start.25 = (bf16[16,96,256]{2,1,0:T(8,128)(2,1)}, bf16[16,96,256]{2,1,0:T(8,128)(2,1)}, u32[]{:S(2)}, u32[]{:S(2)}) collective-permute-start(bf16[16,96,256]{2,1,0:T(8,128)(2,1)} %get-tuple-element.235.rest_12_), channel_id=1, source_target_pairs={{0,1},{1,0},{2,3},{3,2},{4,5},{5,4},{6,7},{7,6},{8,9},{9,8},{10,11... | collective-permute-start | bytes 2359304 | tf_op jit(solution)/shard_map/ppermute | solution.py:562
  199.8 25.2 %collective-permute-start.27 = (bf16[4,3,2,2,2,96,256]{6,5,4,3,2,1,0:T(8,128)(2,1)}, bf16[4,3,2,2,2,96,256]{6,5,4,3,2,1,0:T(8,128)(2,1)}, u32[]{:S(2)}, u32[]{:S(2)}) collective-permute-start(bf16[4,3,2,2,2,96,256]{6,5,4,3,2,1,0:T(8,128)(2,1)} %get-tuple-element.245), channel_id=1, source_target_pairs={{0,4},{4,0},{8,12},{12,8},{16,20},{20,16},{24,28},{28,24},{1,5},{5... | collective-permute-start | bytes 14155784 | tf_op jit(solution)/shard_map/ppermute | solution.py:562
  199.9 24.4 %collective-permute-start.28 = (bf16[20,96,256]{2,1,0:T(8,128)(2,1)}, bf16[20,96,256]{2,1,0:T(8,128)(2,1)S(1)}, u32[]{:S(2)}, u32[]{:S(2)}) collective-permute-start(bf16[20,96,256]{2,1,0:T(8,128)(2,1)} %get-tuple-element.246.refs_16_), channel_id=1, source_target_pairs={{0,16},{4,20},{8,24},{12,28},{16,0},{20,4},{24,8},{28,12},{1,17},{... | collective-permute-start | bytes 2949128 | tf_op jit(solution)/shard_map/ppermute | solution.py:562
  201.0 24.0 %collective-permute-start.30 = (bf16[20,96,256]{2,1,0:T(8,128)(2,1)}, bf16[20,96,256]{2,1,0:T(8,128)(2,1)S(1)}, u32[]{:S(2)}, u32[]{:S(2)}) collective-permute-start(bf16[20,96,256]{2,1,0:T(8,128)(2,1)} %get-tuple-element.248.refs_18_), channel_id=1, source_target_pairs={{0,8},{4,12},{8,0},{12,4},{16,24},{20,28},{24,16},{28,20},{1,9},{5... | collective-permute-start | bytes 2949128 | tf_op jit(solution)/shard_map/ppermute | solution.py:562
  233.1 31.6 %collective-permute-start.34 = (bf16[2,2,2,2,3,96,256]{6,5,4,3,2,1,0:T(8,128)(2,1)}, bf16[2,2,2,2,3,96,256]{6,5,4,3,2,1,0:T(8,128)(2,1)}, u32[]{:S(2)}, u32[]{:S(2)}) collective-permute-start(bf16[2,2,2,2,3,96,256]{6,5,4,3,2,1,0:T(8,128)(2,1)} %get-tuple-element.263), channel_id=1, source_target_pairs={{0,4},{4,0},{8,12},{12,8},{16,20},{20,16},{24,28},{28,24},{1,5},{5... | collective-permute-start | bytes 7077896 | tf_op jit(solution)/shard_map/ppermute | solution.py:562
  233.2 30.7 %collective-permute-start.32 = (bf16[26,96,256]{2,1,0:T(8,128)(2,1)}, bf16[26,96,256]{2,1,0:T(8,128)(2,1)S(1)}, u32[]{:S(2)}, u32[]{:S(2)}) collective-permute-start(bf16[26,96,256]{2,1,0:T(8,128)(2,1)} %get-tuple-element.260), channel_id=1, source_target_pairs={{0,16},{4,20},{8,24},{12,28},{16,0},{20,4},{24,8},{28,12},{1,17},{... | collective-permute-start | bytes 3833864 | tf_op jit(solution)/shard_map/ppermute | solution.py:562
  234.2 30.5 %collective-permute-start.31 = (bf16[26,96,256]{2,1,0:T(8,128)(2,1)}, bf16[26,96,256]{2,1,0:T(8,128)(2,1)}, u32[]{:S(2)}, u32[]{:S(2)}) collective-permute-start(bf16[26,96,256]{2,1,0:T(8,128)(2,1)} %get-tuple-element.259.source), channel_id=1, source_target_pairs={{0,8},{4,12},{8,0},{12,4},{16,24},{20,28},{24,16},{28,20},{1,9},{5... | collective-permute-start | bytes 3833864 | tf_op jit(solution)/shard_map/ppermute | solution.py:562
  234.8 23.9 %collective-permute-start.33 = (bf16[16,96,256]{2,1,0:T(8,128)(2,1)}, bf16[16,96,256]{2,1,0:T(8,128)(2,1)}, u32[]{:S(2)}, u32[]{:S(2)}) collective-permute-start(bf16[16,96,256]{2,1,0:T(8,128)(2,1)} %get-tuple-element.261), channel_id=1, source_target_pairs={{0,1},{1,0},{2,3},{3,2},{4,5},{5,4},{6,7},{7,6},{8,9},{9,8},{10,11... | collective-permute-start | bytes 2359304 | tf_op jit(solution)/shard_map/ppermute | solution.py:562
  238.0 18.8 %collective-permute-start.35 = (bf16[4,96,256]{2,1,0:T(8,128)(2,1)}, bf16[4,96,256]{2,1,0:T(8,128)(2,1)S(1)}, u32[]{:S(2)}, u32[]{:S(2)}) collective-permute-start(bf16[4,96,256]{2,1,0:T(8,128)(2,1)} %get-tuple-element.264), channel_id=1, source_target_pairs={{0,2},{1,3},{2,0},{3,1},{4,6},{5,7},{6,4},{7,5},{8,10},{9,11},{10,... | collective-permute-start | bytes 589832 | tf_op jit(solution)/shard_map/ppermute | solution.py:562
  272.6 28.0 %collective-permute-start.39 = (bf16[21,96,256]{2,1,0:T(8,128)(2,1)}, bf16[21,96,256]{2,1,0:T(8,128)(2,1)S(1)}, u32[]{:S(2)}, u32[]{:S(2)}) collective-permute-start(bf16[21,96,256]{2,1,0:T(8,128)(2,1)} %get-tuple-element.274), channel_id=1, source_target_pairs={{0,8},{4,12},{8,0},{12,4},{16,24},{20,28},{24,16},{28,20},{1,9},{5... | collective-permute-start | bytes 3096584 | tf_op jit(solution)/shard_map/ppermute | solution.py:562
  273.2 27.4 %collective-permute-start.37 = (bf16[20,96,256]{2,1,0:T(8,128)(2,1)}, bf16[20,96,256]{2,1,0:T(8,128)(2,1)}, u32[]{:S(2)}, u32[]{:S(2)}) collective-permute-start(bf16[20,96,256]{2,1,0:T(8,128)(2,1)} %get-tuple-element.272.source), channel_id=1, source_target_pairs={{0,16},{4,20},{8,24},{12,28},{16,0},{20,4},{24,8},{28,12},{1,17},{... | collective-permute-start | bytes 2949128 | tf_op jit(solution)/shard_map/ppermute | solution.py:562
  274.2 26.4 %collective-permute-start.38 = (bf16[13,96,256]{2,1,0:T(8,128)(2,1)}, bf16[13,96,256]{2,1,0:T(8,128)(2,1)S(1)}, u32[]{:S(2)}, u32[]{:S(2)}) collective-permute-start(bf16[13,96,256]{2,1,0:T(8,128)(2,1)} %get-tuple-element.273), channel_id=1, source_target_pairs={{0,1},{1,0},{2,3},{3,2},{4,5},{5,4},{6,7},{7,6},{8,9},{9,8},{10,11... | collective-permute-start | bytes 1916936 | tf_op jit(solution)/shard_map/ppermute | solution.py:562
  274.8 25.8 %collective-permute-start.40 = (bf16[7,96,256]{2,1,0:T(8,128)(2,1)}, bf16[7,96,256]{2,1,0:T(8,128)(2,1)S(1)}, u32[]{:S(2)}, u32[]{:S(2)}) collective-permute-start(bf16[7,96,256]{2,1,0:T(8,128)(2,1)} %get-tuple-element.275), channel_id=1, source_target_pairs={{0,2},{1,3},{2,0},{3,1},{4,6},{5,7},{6,4},{7,5},{8,10},{9,11},{10,... | collective-permute-start | bytes 1032200 | tf_op jit(solution)/shard_map/ppermute | solution.py:562
  276.2 24.4 %collective-permute-start.41 = (bf16[3,96,256]{2,1,0:T(8,128)(2,1)}, bf16[3,96,256]{2,1,0:T(8,128)(2,1)}, u32[]{:S(2)}, u32[]{:S(2)}) collective-permute-start(bf16[3,96,256]{2,1,0:T(8,128)(2,1)} %get-tuple-element.276), channel_id=1, source_target_pairs={{0,3},{1,2},{2,1},{3,0},{4,7},{5,6},{6,5},{7,4},{8,11},{9,10},{10,... | collective-permute-start | bytes 442376 | tf_op jit(solution)/shard_map/ppermute | solution.py:562
  329.1 21.3 %collective-permute-start.48 = (bf16[7,96,256]{2,1,0:T(8,128)(2,1)}, bf16[7,96,256]{2,1,0:T(8,128)(2,1)S(1)}, u32[]{:S(2)}, u32[]{:S(2)}) collective-permute-start(bf16[7,96,256]{2,1,0:T(8,128)(2,1)} %get-tuple-element.287), channel_id=1, source_target_pairs={{0,2},{1,3},{2,0},{3,1},{4,6},{5,7},{6,4},{7,5},{8,10},{9,11},{10,... | collective-permute-start | bytes 1032200 | tf_op jit(solution)/shard_map/ppermute | solution.py:562
  (64 other events, 604.5 us)
